TPU v7x, 32 devices: a whole 2x2x4 slice. The times are simulated.
32 devices in a mesh: seq: 8 (over y, x, core), mlp: 4 (over z).
Axes of the slice: x: 2, y: 2, z: 4, core: 2. Of those that a mesh axis runs over, the one named last changes fastest.
Arguments:
- tokens: bfloat16 [8, 4, 256, 1024], P('seq'), may hold values from -6 to 6
- ln_gain: float32 [1024], replicated, may hold values from 0.5 to 1.5
- ln_bias: float32 [1024], replicated, may hold values from -3 to 3
- w_query: bfloat16 [1024, 1024], P(None, 'mlp'), may hold values from -0.1875 to 0.1875
- w_key: bfloat16 [1024, 1024], P(None, 'mlp'), may hold values from -0.1875 to 0.1875
- w_value: bfloat16 [1024, 1024], P(None, 'mlp'), may hold values from -0.1875 to 0.1875
- w_attn_out: bfloat16 [1024, 1024], P('mlp'), may hold values from -6 to 6
- w_in: bfloat16 [1024, 4096], P(None, 'mlp'), may hold values from -0.1875 to 0.1875
- b_in: float32 [4096], P('mlp'), may hold values from -3 to 3
- w_mlp_out: bfloat16 [4096, 1024], P('mlp'), may hold values from -0.09375 to 0.09375
- b_out: float32 [1024], replicated, may hold values from -3 to 3
- cotangent: bfloat16 [8, 4, 256, 1024], P('seq'), may hold values from -6 to 6
Outputs:
- mixed: bfloat16 [8, 4, 256, 1024], P('seq')
- d_tokens: bfloat16 [8, 4, 256, 1024], P('seq')
- d_ln_gain: float32 [1024], replicated
- d_ln_bias: float32 [1024], replicated
- d_w_query: float32 [1024, 1024], P(None, 'mlp')
- d_w_key: float32 [1024, 1024], P(None, 'mlp')
- d_w_value: float32 [1024, 1024], P(None, 'mlp')
- d_w_attn_out: float32 [1024, 1024], P('mlp')
- d_w_in: float32 [1024, 4096], P(None, 'mlp')
- d_b_in: float32 [4096], P('mlp')
- d_w_mlp_out: float32 [4096, 1024], P('mlp')
- d_b_out: float32 [1024], replicated
All inputs are finite; a program needn't handle non-finite values.
Results may differ from a plain program's by a relative error of at most 0.02.
Values may be sent and summed in bfloat16 or wider, within the bound.
No kernel may reach another device: no remote copies, remote signals or barrier semaphores. Data moves between devices by JAX's collectives and lax.ppermute only.
A program may use at most 192 MiB of HBM per device.

v0:
```python
from functools import partial

import jax
import jax.numpy as jnp
import numpy as np
from jax import lax
from jax.experimental import pallas as pl
from jax.experimental.pallas import tpu as pltpu
from jax.sharding import PartitionSpec as P

HEAD_DIM = 64
ROT = 32

epsilon = 1e-05
neg_big = -1e30
bf16 = jnp.bfloat16
f32 = jnp.float32


def passed_along(x, axis, by):
    peers = lax.axis_size(axis)
    pairs = [(i, i + by) for i in range(peers) if 0 <= i + by < peers]
    return lax.ppermute(x, axis, pairs)


def rotary_tables(positions, width):
    column = jnp.arange(width, dtype=jnp.int32) % HEAD_DIM
    pairs = (column // 2).astype(f32)
    freq = 10000.0 ** (-2.0 * pairs / ROT)
    angle = positions.astype(f32)[:, None] * freq[None, :]
    active = (column < ROT)[None, :]
    even = (column % 2 == 0)[None, :]
    cosine = jnp.where(active, jnp.cos(angle), 1.0)
    sine = jnp.where(active, jnp.sin(angle), 0.0)
    return cosine, jnp.where(even, -sine, 0.0), jnp.where(even, 0.0, sine)


def rotate(v, tables, sign):
    cosine, from_right, from_left = tables
    right = jnp.concatenate([v[..., 1:], v[..., :1]], -1)
    left = jnp.concatenate([v[..., -1:], v[..., :-1]], -1)
    return v * cosine + sign * (right * from_right + left * from_left)


def attention_kernel(x_ref, out_ref, xt, acc, sbuf, *, length, hd, tq, tk):
    xt[...] = x_ref[0].T
    scale = hd**-0.5
    nt = (((1,), (1,)), ((), ()))
    zero = jnp.zeros((hd, tq), bf16)

    def put(old, new, q0, join):
        if old is None:
            return new
        if q0 == 0:
            return join(old, new)
        return jnp.concatenate([old[:, :q0], join(old[:, q0:], new)], 1)

    add = lambda u, v: u + v
    for i in range(length // tq):
        first = i * tq
        qs = (xt[0:hd, first : first + tq].astype(f32) * scale).astype(bf16)
        at = xt[3 * hd : 4 * hd, first : first + tq].astype(f32)
        zq = jnp.concatenate([zero, qs], 0)
        qz = jnp.concatenate([qs, zero], 0)
        steps = [(k0, k0 + tk, 0) for k0 in range(0, first, tk)]
        steps += [(first + q0, first + q0 + tk // 2, q0) for q0 in range(0, tq, tk // 2)]
        top = None
        for k0, k1, q0 in steps:
            st = jnp.dot(x_ref[0, k0:k1, 0 : 2 * hd], zq[:, q0:], preferred_element_type=f32)
            if k0 >= first:
                kp = lax.broadcasted_iota(jnp.int32, st.shape, 0)
                qp = lax.broadcasted_iota(jnp.int32, st.shape, 1)
                st = jnp.where(kp <= qp, st, neg_big)
            sbuf[k0:k1, q0:] = st
            top = put(top, jnp.max(st, 0, keepdims=True), q0, jnp.maximum)
        tot = None
        ot = None
        for k0, k1, q0 in steps:
            e = jnp.exp(sbuf[k0:k1, q0:] - top[:, q0:])
            sbuf[k0:k1, q0:] = e
            tot = put(tot, jnp.sum(e, 0, keepdims=True), q0, add)
            ot = put(ot, jnp.dot(xt[2 * hd : 3 * hd, k0:k1], e.astype(bf16), preferred_element_type=f32), q0, add)
        r = 1.0 / tot
        ot = ot * r
        ar = (at * r).astype(bf16)
        spread = jnp.sum(ar.astype(f32) * ot, 0, keepdims=True)
        az = jnp.concatenate([ar, zero], 0)
        za = jnp.concatenate([zero, ar], 0)
        dqt = None
        for k0, k1, q0 in steps:
            dp = jnp.dot(x_ref[0, k0:k1, 2 * hd : 4 * hd], az[:, q0:], preferred_element_type=f32)
            e = sbuf[k0:k1, q0:]
            ds = (e * (dp - spread[:, q0:])).astype(bf16)
            dqt = put(dqt, jnp.dot(xt[hd : 2 * hd, k0:k1], ds, preferred_element_type=f32), q0, add)
            both = lax.dot_general(ds, qz[:, q0:], nt, preferred_element_type=f32) + lax.dot_general(
                e.astype(bf16), za[:, q0:], nt, preferred_element_type=f32
            )
            if k0 < first:
                both = acc[k0:k1, :] + both
            acc[k0:k1, :] = both
        both = jnp.concatenate([ot, dqt * scale], 0)
        out_ref[0, first : first + tq, 0 : 2 * hd] = both.T.astype(bf16)
    out_ref[0, :, 2 * hd : 4 * hd] = acc[...].astype(bf16)


def attention(x, after=()):
    n, length, width = x.shape
    hd = width // 4
    tq = 512 if length % 512 == 0 else 256
    spec = pl.BlockSpec((1, length, width), lambda i: (i, 0, 0))
    return call(
        partial(attention_kernel, length=length, hd=hd, tq=tq, tk=512),
        (n,),
        (x,),
        [spec],
        spec,
        shape_of(*x.shape),
        7,
        after,
        scratch=[pltpu.VMEM((width, length), bf16), pltpu.VMEM((length, 2 * hd), f32), pltpu.VMEM((length, tq), f32)],
        vmem=32,
        free_out=(0,),
    )


def ring_attention(q, k, v, a):
    seq_count, row_count, inner_width = q.shape
    score_scale = HEAD_DIM ** (-0.5)
    shard_total = lax.axis_size("seq")
    my_shard = lax.axis_index("seq")
    heads_of = lambda x: x.reshape(seq_count, row_count, inner_width // HEAD_DIM, HEAD_DIM)
    flat_of = lambda x: x.reshape(seq_count, row_count, inner_width)
    qh, gh = heads_of(q), heads_of(a)
    local = jnp.arange(row_count, dtype=jnp.int32)
    own_mask = local[:, None] >= local[None, :]
    ein = partial(jnp.einsum, preferred_element_type=f32)

    def attend_block(state, key_block, value_block, visible):
        running_max, exp_total, weighted = state
        raw = ein("sthd,suhd->shtu", qh, key_block) * score_scale
        raw = jnp.where(visible[None, None], raw, neg_big)
        new_max = jnp.maximum(running_max, jnp.max(raw, -1))
        weights = jnp.where(visible[None, None], jnp.exp(raw - new_max[..., None]), 0.0)
        shrink = jnp.exp(running_max - new_max)
        exp_total = exp_total * shrink + jnp.sum(weights, -1)
        weighted = weighted * jnp.transpose(shrink, (0, 2, 1))[..., None] + ein(
            "shtu,suhd->sthd", weights.astype(bf16), value_block
        )
        return (new_max, exp_total, weighted)

    head_count = inner_width // HEAD_DIM
    state = (
        jnp.full((seq_count, head_count, row_count), neg_big, f32),
        jnp.zeros((seq_count, head_count, row_count), f32),
        jnp.zeros(qh.shape, f32),
    )
    state = attend_block(state, heads_of(k), heads_of(v), own_mask)
    empty_stack = jnp.zeros((max(shard_total - 1, 1),) + q.shape, bf16)

    def forward_step(step, carry):
        state, near_keys, near_values, key_stack, value_stack = carry
        near_keys, near_values = passed_along((near_keys, near_values), "seq", 1)
        visible = jnp.broadcast_to(my_shard >= step, (row_count, row_count))
        state = attend_block(state, heads_of(near_keys), heads_of(near_values), visible)
        key_stack = lax.dynamic_update_index_in_dim(key_stack, near_keys, step - 1, 0)
        value_stack = lax.dynamic_update_index_in_dim(value_stack, near_values, step - 1, 0)
        return (state, near_keys, near_values, key_stack, value_stack)

    state, _, _, key_stack, value_stack = lax.fori_loop(
        1, shard_total, forward_step, (state, k, v, empty_stack, empty_stack)
    )
    running_max, exp_total, weighted = state
    log_total = running_max + jnp.log(exp_total)
    attended = weighted / jnp.transpose(exp_total, (0, 2, 1))[..., None]
    spread = jnp.transpose(jnp.sum(gh.astype(f32) * attended, -1), (0, 2, 1))

    def grads(key_block, value_block, visible):
        raw = ein("sthd,suhd->shtu", qh, key_block) * score_scale
        probs = jnp.where(visible[None, None], jnp.exp(raw - log_total[..., None]), 0.0)
        grad_probs = ein("sthd,suhd->shtu", gh, value_block)
        slopes = (probs * (grad_probs - spread[..., None])).astype(bf16)
        query_grad = ein("shtu,suhd->sthd", slopes, key_block) * score_scale
        key_grad = ein("shtu,sthd->suhd", slopes, qh) * score_scale
        value_grad = ein("shtu,sthd->suhd", probs.astype(bf16), gh)
        return query_grad, key_grad, value_grad

    d_query, d_keys, d_values = grads(heads_of(k), heads_of(v), own_mask)

    def return_step(index, carry):
        query_grad_total, travelling = carry
        step = shard_total - 1 - index
        near_keys = lax.dynamic_index_in_dim(key_stack, step - 1, 0, keepdims=False)
        near_values = lax.dynamic_index_in_dim(value_stack, step - 1, 0, keepdims=False)
        visible = jnp.broadcast_to(my_shard >= step, (row_count, row_count))
        query_grad, key_grad, value_grad = grads(heads_of(near_keys), heads_of(near_values), visible)
        joined = jnp.concatenate([flat_of(key_grad), flat_of(value_grad)], -1)
        travelling = passed_along((travelling + joined).astype(bf16), "seq", -1).astype(f32)
        return (query_grad_total + query_grad, travelling)

    start = jnp.zeros((seq_count, row_count, 2 * inner_width), f32)
    d_query, travelling = lax.fori_loop(0, shard_total - 1, return_step, (d_query, start))
    d_keys = flat_of(d_keys) + travelling[..., :inner_width]
    d_values = flat_of(d_values) + travelling[..., inner_width:]
    return tuple(x.astype(bf16) for x in (flat_of(attended), flat_of(d_query), d_keys, d_values))


def by_ring(
    tokens, ln_gain, ln_bias, w_query, w_key, w_value, w_attn_out, w_in, b_in, w_mlp_out, b_out, cotangent
):
    x_low = tokens[0]
    cot = cotangent[0]
    seqs, rows, width = x_low.shape
    inner = w_query.shape[1]
    my_shard = lax.axis_index("seq")
    ein = partial(jnp.einsum, preferred_element_type=f32)
    positions = my_shard * rows + jnp.arange(rows, dtype=jnp.int32)
    tables = rotary_tables(positions, inner)
    x = x_low.astype(f32)
    centred = x - jnp.mean(x, -1, keepdims=True)
    inv_std = lax.rsqrt(jnp.mean(centred * centred, -1, keepdims=True) + epsilon)
    unit = centred * inv_std
    normed = (unit * ln_gain + ln_bias).astype(bf16)
    query = rotate(ein("std,de->ste", normed, w_query), tables, 1.0).astype(bf16)
    keys = rotate(ein("std,de->ste", normed, w_key), tables, 1.0).astype(bf16)
    values = ein("std,de->ste", normed, w_value).astype(bf16)
    d_attended = ein("std,ed->ste", cot, w_attn_out).astype(bf16)

    attended, d_query, d_keys, d_values = ring_attention(query, keys, values, d_attended)

    gate_in = ein("std,df->stf", normed, w_in) + b_in
    hidden, gelu_pull = jax.vjp(partial(jax.nn.gelu, approximate=True), gate_in)
    hidden = hidden.astype(bf16)
    d_hidden = ein("std,fd->stf", cot, w_mlp_out)
    d_gate = gelu_pull(d_hidden)[0].astype(bf16)
    d_b_in = jnp.sum(d_gate, (0, 1), dtype=f32)
    d_b_out = jnp.sum(cot, (0, 1), dtype=f32)
    d_w_mlp_out = ein("stf,std->fd", hidden, cot)
    d_w_in = ein("std,stf->df", normed, d_gate)
    mlp_part = ein("stf,fd->std", hidden, w_mlp_out)
    d_normed_mlp = ein("stf,df->std", d_gate, w_in)

    attn_part = ein("ste,ed->std", attended, w_attn_out)
    branches = lax.psum((attn_part + mlp_part).astype(bf16), "mlp").astype(f32)
    mixed = (x + branches + b_out).astype(bf16)
    d_w_attn_out = ein("ste,std->ed", attended, cot)
    d_query_pre = rotate(d_query.astype(f32), tables, -1.0).astype(bf16)
    d_key_pre = rotate(d_keys.astype(f32), tables, -1.0).astype(bf16)
    d_w_query = ein("std,ste->de", normed, d_query_pre)
    d_w_key = ein("std,ste->de", normed, d_key_pre)
    d_w_value = ein("std,ste->de", normed, d_values)
    d_normed_part = d_normed_mlp + ein("ste,de->std", d_query_pre, w_query)
    d_normed_part = d_normed_part + ein("ste,de->std", d_key_pre, w_key)
    d_normed_part = d_normed_part + ein("ste,de->std", d_values, w_value)
    d_normed = lax.psum(d_normed_part.astype(bf16), "mlp").astype(f32)
    d_gain = jnp.sum(d_normed * unit, (0, 1))
    d_bias = jnp.sum(d_normed, (0, 1))
    d_unit = d_normed * ln_gain
    d_inputs = inv_std * (
        d_unit - jnp.mean(d_unit, -1, keepdims=True) - unit * jnp.mean(d_unit * unit, -1, keepdims=True)
    )
    d_tokens = (cot.astype(f32) + d_inputs).astype(bf16)

    def total(v):
        return lax.psum(v.astype(bf16), "seq").astype(f32)

    return (
        mixed[None],
        d_tokens[None],
        total(d_gain),
        total(d_bias),
        total(d_w_query),
        total(d_w_key),
        total(d_w_value),
        total(d_w_attn_out),
        total(d_w_in),
        total(d_b_in),
        total(d_w_mlp_out),
        total(d_b_out),
    )


anywhere = pl.BlockSpec(memory_space=pl.ANY)


class Placed(list):
    def add(self, *arrays):
        self.extend(arrays)

    def pin(self, x):
        return pltpu.with_memory_space_constraint(x, pltpu.HBM) if any(x is y for y in self) else x


in_hbm = Placed()


def call(
    kernel, grid, ins, in_specs, out_specs, out_shape, us, after=(), scalars=(), scratch=(), alias=None, vmem=24, free_out=()
):
    used = len(scalars) + len(ins)

    def body(*refs):
        kernel(*refs[:used], *refs[used + len(after) :])

    one = not isinstance(out_shape, list)
    shapes = [out_shape] if one else out_shape
    shapes = [s if i in free_out else pltpu.HBM(s.shape, s.dtype) for i, s in enumerate(shapes)]
    results = pl.pallas_call(
        body,
        name=getattr(kernel, "func", kernel).__name__.strip("<>"),
        grid_spec=pltpu.PrefetchScalarGridSpec(
            num_scalar_prefetch=len(scalars),
            grid=grid,
            in_specs=list(in_specs) + [anywhere] * len(after),
            out_specs=out_specs,
            scratch_shapes=list(scratch),
        ),
        out_shape=shapes[0] if one else shapes,
        input_output_aliases={len(scalars) + k: v for k, v in (alias or {}).items()},
        compiler_params=pltpu.CompilerParams(vmem_limit_bytes=vmem * 2**20),
        cost_estimate=pl.CostEstimate(flops=int(us * 1e11), bytes_accessed=0, transcendentals=0),
    )(*scalars, *map(in_hbm.pin, ins), *map(in_hbm.pin, after))
    in_hbm.add(*[r for i, r in enumerate([results] if one else results) if i not in free_out])
    return results


def fence(x, *after):
    known = any(x is y for y in in_hbm)
    return call(
        lambda *refs: None,
        (1,),
        (x,),
        [anywhere],
        anywhere,
        shape_of(*x.shape, dtype=x.dtype),
        1,
        after,
        alias={0: 0},
        vmem=1,
        free_out=() if known else (0,),
    )


def dot(a, b):
    return jnp.dot(a, b, preferred_element_type=f32)


def dot_nt(a, b):
    return lax.dot_general(a, b, (((1,), (1,)), ((), ())), preferred_element_type=f32)


def dot_tn(a, b):
    return lax.dot_general(a, b, (((0,), (0,)), ((), ())), preferred_element_type=f32)


def whole(x):
    return pl.BlockSpec(x.shape, lambda *_: (0,) * x.ndim, pipeline_mode=pl.Buffered(1))


def mine(rows):
    return pl.BlockSpec((rows, 2 * HEAD_DIM), lambda i, at: (at[0], 0), pipeline_mode=pl.Buffered(1))


def shape_of(*shape, dtype=bf16):
    return jax.ShapeDtypeStruct(shape, dtype)


def unit_rows(x):
    average = jnp.mean(x, -1, keepdims=True)
    centred = x - average
    inv_std = lax.rsqrt(jnp.mean(centred * centred, -1, keepdims=True) + epsilon)
    return centred * inv_std, inv_std


def half_swap(low, high, lane, keep_low):
    if keep_low:
        return jnp.where(lane < HEAD_DIM, low, pltpu.roll(high, HEAD_DIM, 1))
    return jnp.where(lane < HEAD_DIM, pltpu.roll(low, HEAD_DIM, 1), high)


def rope_tile(v, cosine, from_right, from_left):
    width = v.shape[1]
    return v * cosine + pltpu.roll(v, width - 1, 1) * from_right + pltpu.roll(v, 1, 1) * from_left


def position_tables(total):
    column = np.arange(2 * HEAD_DIM) % HEAD_DIM
    freq = np.float32(10000.0) ** (np.float32(-2.0 / ROT) * (column // 2).astype(np.float32))
    angle = np.arange(total, dtype=np.float32)[:, None] * freq.astype(np.float32)[None, :]
    active = (column < ROT)[None, :]
    cosine = np.where(active, np.cos(angle.astype(np.float64)), 1.0).astype(np.float32)
    sine = np.where(active, np.sin(angle.astype(np.float64)), 0.0).astype(np.float32)
    return cosine, sine


def signed(cosine, sine):
    even = lax.broadcasted_iota(jnp.int32, sine.shape, 1) % 2 == 0
    return cosine, jnp.where(even, -sine, 0.0), jnp.where(even, 0.0, sine)


def pre_kernel(shard_ref, x_ref, g_ref, gain, bias, wq, wk, wv, wo, cosine, sine, *rest):
    normed_ref, packed_ref = rest[-2:]
    unit, _ = unit_rows(x_ref[0].astype(f32))
    normed = (unit * gain[...] + bias[...]).astype(bf16)
    normed_ref[...] = normed
    q, k, v = dot(normed, wq[...]), dot(normed, wk[...]), dot(normed, wv[...])
    a = dot_nt(g_ref[0], wo[...])
    tables = signed(cosine[...], sine[...])
    lane = lax.broadcasted_iota(jnp.int32, tables[0].shape, 1)
    for tile in range(q.shape[1] // 128):
        cols = slice(tile * 128, (tile + 1) * 128)
        qt, kt = rope_tile(q[:, cols], *tables), rope_tile(k[:, cols], *tables)
        for side in (0, 1):
            head = tile * 2 + side
            packed_ref[head, :, 0:128] = half_swap(qt, kt, lane, side == 0).astype(bf16)
            packed_ref[head, :, 128:256] = half_swap(v[:, cols], a[:, cols], lane, side == 0).astype(bf16)


def pre(c, count, shard, x, g, consts, tables, before):
    seqs, rows, width = x.shape
    heads = consts[2].shape[1] // HEAD_DIM
    by_seq = pl.BlockSpec((1, rows, width), lambda i, _: (c * count + i, 0, 0))
    ins, specs = (x, g) + consts + tables, [by_seq, by_seq] + [whole(w) for w in consts] + [mine(rows)] * 2
    alias = {}
    if before is not None:
        alias = {len(ins): 0}
        ins, specs = ins + (before,), specs + [anywhere]
    return call(
        pre_kernel,
        (count,),
        ins,
        specs,
        [
            pl.BlockSpec((rows, width), lambda i, _: (c * count + i, 0)),
            pl.BlockSpec((heads, rows, 4 * HEAD_DIM), lambda i, _: (i, 0, 0)),
        ],
        [shape_of(seqs * rows, width), shape_of(count * heads, rows, 4 * HEAD_DIM)],
        3,
        scalars=(shard,),
        alias=alias,
        free_out=(1,),
    )


def mlp_kernel(n_ref, g_ref, w_in, b_in, w_out, *rest):
    hidden_ref, dgate_ref, part_ref, dn_ref, db_in, db_out = rest[-6:]
    c0, c1 = 0.7978845608028654, 0.044715
    g = g_ref[...]
    gate = dot(n_ref[...], w_in[...]) + b_in[...]
    square = gate * gate
    tanh = jnp.tanh(c0 * gate * (1.0 + c1 * square))
    left = 0.5 * (1.0 + tanh)
    hidden = (gate * left).astype(bf16)
    slope = left + 0.5 * gate * (1.0 - tanh * tanh) * (c0 * (1.0 + 3.0 * c1 * square))
    dgate = (dot_nt(g, w_out[...]) * slope).astype(bf16)
    hidden_ref[...] = hidden
    dgate_ref[...] = dgate
    part_ref[...] = dot(hidden, w_out[...]).astype(bf16)
    dn_ref[...] = dot_nt(dgate, w_in[...]).astype(bf16)

    @pl.when(pl.program_id(0) == 0)
    def _():
        db_in[...] = jnp.zeros_like(db_in)
        db_out[...] = jnp.zeros_like(db_out)

    db_in[...] += jnp.sum(dgate.astype(f32), 0, keepdims=True)
    db_out[...] += jnp.sum(g.astype(f32), 0, keepdims=True)


def mlp(c, count, rows, normed, g, w_in, b_in, w_out, before, after):
    total, width = g.shape
    ff = w_in.shape[1]
    there = lambda w: pl.BlockSpec((rows, w), lambda i: (c * count + i, 0))
    here = lambda w: pl.BlockSpec((rows, w), lambda i: (i, 0))
    one = lambda w: pl.BlockSpec((1, w), lambda i: (0, 0))
    ins = (normed, g, w_in, b_in, w_out)
    specs = [there(width), there(width), whole(w_in), whole(b_in), whole(w_out)]
    alias = {}
    if before is not None:
        alias = {len(ins): 0, len(ins) + 1: 1}
        ins, specs = ins + tuple(before), specs + [anywhere] * 2
    return call(
        mlp_kernel,
        (count,),
        ins,
        specs,
        [there(ff), there(ff), here(width), here(width), one(ff), one(width)],
        [
            shape_of(total, ff),
            shape_of(total, ff),
            shape_of(count * rows, width),
            shape_of(count * rows, width),
            shape_of(1, ff, dtype=f32),
            shape_of(1, width, dtype=f32),
        ],
        5,
        after,
        alias=alias,
        vmem=32,
    )


def dense_grads_kernel(core_ref, n_ref, dgate_ref, hidden_ref, g_ref, give_ref, keep_ref):
    step, half = pl.program_id(0), pl.num_programs(0) // 2
    both = dot_tn(n_ref[...], dgate_ref[...]).astype(bf16), dot_tn(hidden_ref[...], g_ref[...]).astype(bf16)

    @pl.when(step < half)
    def _():
        give_ref[0], give_ref[1] = both

    @pl.when(step >= half)
    def _():
        keep_ref[0], keep_ref[1] = both


def halves(steps, rows, wide, slots):
    half = steps // 2

    def place(i, core):
        return jnp.where(i < half, (1 - core[0]) * half + i, core[0] * half + i - half)

    cols = lambda total: pl.BlockSpec((total, rows), lambda i, core: (0, place(i, core)))
    give = pl.BlockSpec((slots, rows, wide), lambda i, core: (0, jnp.minimum(i, half - 1), 0))
    keep = pl.BlockSpec((slots, rows, wide), lambda i, core: (0, jnp.maximum(i - half, 0), 0))
    return cols, [give, keep]


def dense_grads(core, normed, dgate, hidden, g, loose, steps=4):
    total, width = g.shape
    cols, outs = halves(steps, width // steps, width, 2)
    return call(
        dense_grads_kernel,
        (steps,),
        (normed, dgate, hidden, g),
        [cols(total), whole(dgate), cols(total), whole(g)],
        outs,
        [shape_of(2, width // 2, width)] * 2,
        6,
        scalars=(core,),
        after=loose,
    )


def post_kernel(place_ref, back_ref, x_ref, part_ref, dn_ref, b_out, wq, wk, wv, wo, cosine, sine, *rest):
    give_ref, keep_ref, flat_ref, dgain, dbias = rest[-5:]
    tables = signed(cosine[...], sine[...])
    lane = lax.broadcasted_iota(jnp.int32, tables[0].shape, 1)
    inner = wo.shape[0]
    for tile in range(inner // 128):
        even, odd = back_ref[2 * tile].astype(f32), back_ref[2 * tile + 1].astype(f32)
        lows = half_swap(even[:, 0:128], odd[:, 0:128], lane, True)
        dq = half_swap(even[:, 0:128], odd[:, 0:128], lane, False)
        dk = half_swap(even[:, 128:256], odd[:, 128:256], lane, True)
        dv = half_swap(even[:, 128:256], odd[:, 128:256], lane, False)
        dq = rope_tile(dq, tables[0], -tables[1], -tables[2])
        dk = rope_tile(dk, tables[0], -tables[1], -tables[2])
        for which, value in enumerate((lows, dq, dk, dv)):
            at = which * inner + tile * 128
            flat_ref[:, at : at + 128] = value.astype(bf16)
    x = x_ref[0].astype(f32)
    z = place_ref[1]
    first = (z == 0).astype(f32)
    mixed = dot(flat_ref[:, 0:inner], wo[...]) + part_ref[...].astype(f32) + first * (x + b_out[...])
    dn = dn_ref[...].astype(f32)
    for which, w in enumerate((wq, wk, wv)):
        at = (which + 1) * inner
        dn = dn + dot_nt(flat_ref[:, at : at + inner], w[...])
    unit, _ = unit_rows(x)
    odd = z % 2 == 1
    half = dn.shape[0] // 2
    for which, share in enumerate((dn, mixed)):
        top, bottom = share[:half].astype(bf16), share[half:].astype(bf16)
        give_ref[0, which] = jnp.where(odd, top, bottom)
        keep_ref[0, which] = jnp.where(odd, bottom, top)

    @pl.when(pl.program_id(0) == 0)
    def _():
        dgain[...] = jnp.zeros_like(dgain)
        dbias[...] = jnp.zeros_like(dbias)

    dgain[...] += jnp.sum(dn * unit, 0, keepdims=True)
    dbias[...] += jnp.sum(dn, 0, keepdims=True)


def post(c, count, place, back, x, part, dn, consts, tables, before, after):
    seqs, rows, width = x.shape
    inner = consts[1].shape[1]
    heads = inner // HEAD_DIM
    here = pl.BlockSpec((rows, width), lambda i, _: (i, 0))
    one = pl.BlockSpec((1, width), lambda i, _: (0, 0))
    ins = (back, x, part, dn) + consts + tables
    specs = [
        pl.BlockSpec((heads, rows, 4 * HEAD_DIM), lambda i, _: (i, 0, 0)),
        pl.BlockSpec((1, rows, width), lambda i, _: (c * count + i, 0, 0)),
        here,
        here,
    ]
    specs += [whole(w) for w in consts] + [mine(rows)] * 2
    alias = {}
    if before is not None:
        alias = {len(ins): 2}
        ins, specs = ins + (before,), specs + [anywhere]
    share_spec = pl.BlockSpec((1, 2, rows // 2, width), lambda i, place: (i ^ (place[1] // 2), 0, 0, 0))
    return call(
        post_kernel,
        (count,),
        ins,
        specs,
        [share_spec] * 2 + [pl.BlockSpec((rows, 4 * inner), lambda i, _: (c * count + i, 0)), one, one],
        [shape_of(count, 2, rows // 2, width)] * 2
        + [shape_of(seqs * rows, 4 * inner)]
        + [shape_of(1, width, dtype=f32)] * 2,
        4,
        after,
        (place,),
        alias=alias,
    )


def head_grads_kernel(core_ref, n_ref, g_ref, flat_ref, small_ref, give_ref, keep_ref, *, inner):
    step, half = pl.program_id(0), pl.num_programs(0) // 2
    out = dot_tn(g_ref[...], flat_ref[:, 0:inner])
    rest = dot_tn(n_ref[...], flat_ref[:, inner:])

    @pl.when(step < half)
    def _():
        give_ref[0, :, 0:inner] = out.astype(bf16)
        give_ref[0, :, inner:] = rest.astype(bf16)

    @pl.when(step >= half)
    def _():
        give_ref[0, 0 : small_ref.shape[0]] = small_ref[...]
        keep_ref[0, :, 0:inner] = out.astype(bf16)
        keep_ref[0, :, inner:] = rest.astype(bf16)


def head_grads(core, normed, g, flat, small, after, steps=4):
    total, width = g.shape
    wide = flat.shape[1]
    rows, half = width // steps, steps // 2
    cols, (_, keep) = halves(steps, rows, wide, 1)
    give = pl.BlockSpec((1, rows, wide), lambda i, core: (0, jnp.minimum(i, half), 0))
    return call(
        partial(head_grads_kernel, inner=wide // 4),
        (steps,),
        (normed, g, flat, small),
        [cols(total), cols(total), whole(flat), whole(small)],
        [give, keep],
        [shape_of(1, (half + 1) * rows, wide), shape_of(1, half * rows, wide)],
        4,
        after,
        (core,),
    )


def split_kernel(keep_ref, got_ref, *rest, small):
    out_ref, token_ref = rest[-2:]
    token_ref[...] = jnp.zeros_like(token_ref)
    rows = keep_ref.shape[1]
    out_ref[0, :, 0:rows] = (keep_ref[...].astype(f32) + got_ref[...].astype(f32)).astype(bf16)
    if small:
        own, got = rest[0], rest[1]
        out_ref[0, 0, rows:] = (own[...].astype(f32) + got[0].astype(f32)).astype(bf16)


def split(keep, got, small, chips, after):
    slots, total, wide = keep.shape
    rows = total // chips
    block = pl.BlockSpec((slots, rows, wide), lambda k: (0, k, 0))
    ins, specs, extra = (keep, got), [block, block], 0
    if small is not None:
        extra = small.shape[0]
        ins += (small, got)
        specs += [whole(small), pl.BlockSpec((1, extra, wide), lambda k: (0, total // extra, 0))]
    return call(
        partial(split_kernel, small=extra > 0),
        (chips,),
        ins,
        specs,
        [pl.BlockSpec((1, slots, rows + extra, wide), lambda k: (k, 0, 0, 0)), pl.BlockSpec((8, 128), lambda k: (0, 0))],
        [shape_of(chips, slots, rows + extra, wide), shape_of(8, 128, dtype=f32)],
        2,
        after,
        vmem=16,
    )


def total_kernel(parts_ref, out_ref, token_ref):
    token_ref[...] = jnp.zeros_like(token_ref)
    total = parts_ref[0].astype(f32)
    for k in range(1, parts_ref.shape[0]):
        total = total + parts_ref[k].astype(f32)
    for k in range(out_ref.shape[0]):
        out_ref[k] = total.astype(bf16)


def total(parts, copies, loose):
    chips, slots, rows, wide = parts.shape
    steps = 2 * slots
    block = lambda n: pl.BlockSpec((n, 1, rows, wide // 2), lambda i: (0, i // 2, 0, i % 2))
    return call(
        total_kernel,
        (steps,),
        (parts,),
        [block(chips)],
        [block(copies), pl.BlockSpec((8, 128), lambda i: (0, 0))],
        [shape_of(copies, slots, rows, wide), shape_of(8, 128, dtype=f32)],
        2,
        vmem=16,
        after=loose,
    )


def widened(at_ref, own_ref, other_ref, stage, in_sems, take):
    chips = own_ref.shape[0]
    loads = [
        pltpu.make_async_copy((own_ref, other_ref)[i // chips].at[i % chips], stage.at[i], in_sems.at[i])
        for i in range(2 * chips)
    ]
    for load in loads:
        load.start()
    stores = []
    for i, load in enumerate(loads):
        load.wait()
        spot = (at_ref[0] ^ (i // chips)) * chips + (at_ref[1] ^ (i % chips))
        for store in take(i, spot):
            store.start()
            stores.append(store)
    for store in stores:
        store.wait()


def dense_outs_kernel(at_ref, own_ref, other_ref, out_in, out_out, stage, wide_stage, in_sems, out_sems):
    rows = stage.shape[2]

    def take(i, spot):
        for which, out in enumerate((out_in, out_out)):
            wide_stage[i, which] = stage[i, which].astype(f32)
            here = out.at[pl.ds(spot * rows, rows)]
            yield pltpu.make_async_copy(wide_stage.at[i, which], here, out_sems.at[i, which])

    widened(at_ref, own_ref, other_ref, stage, in_sems, take)


def head_outs_kernel(at_ref, own_ref, other_ref, out_t, out_q, out_k, out_v, stage, turned, wide_stage, in_sems, out_sems):
    rows, inner = wide_stage.shape[2:]

    def take(i, spot):
        here = pl.ds(spot * rows, rows)
        turned[i] = stage[i, 0, 0:rows, 0:inner].astype(f32).T
        yield pltpu.make_async_copy(turned.at[i], out_t.at[:, here], out_sems.at[i, 0])
        for which, out in enumerate((out_q, out_k, out_v)):
            cols = slice((which + 1) * inner, (which + 2) * inner)
            wide_stage[i, which] = stage[i, 0, 0:rows, cols].astype(f32)
            yield pltpu.make_async_copy(wide_stage.at[i, which], out.at[here], out_sems.at[i, which + 1])

    widened(at_ref, own_ref, other_ref, stage, in_sems, take)


def dense_outs(at, own, other, width, after):
    chips, slots, rows, wide = own.shape
    dma = pltpu.SemaphoreType.DMA
    return call(
        dense_outs_kernel,
        (1,),
        (own, other),
        [anywhere] * 2,
        [anywhere] * 2,
        [shape_of(width, wide, dtype=f32)] * 2,
        4,
        after,
        (at,),
        [
            pltpu.VMEM((2 * chips, slots, rows, wide), bf16),
            pltpu.VMEM((2 * chips, slots, rows, wide), f32),
            dma((2 * chips,)),
            dma((2 * chips, slots)),
        ],
        vmem=20,
    )


def head_outs(at, own, other, width, after):
    chips, slots, tall, wide = own.shape
    rows, inner = width // (2 * chips), wide // 4
    dma = pltpu.SemaphoreType.DMA
    return call(
        head_outs_kernel,
        (1,),
        (own, other),
        [anywhere] * 2,
        [anywhere] * 4,
        [shape_of(inner, width, dtype=f32)] + [shape_of(width, inner, dtype=f32)] * 3,
        3,
        after,
        (at,),
        [
            pltpu.VMEM((2 * chips, slots, tall, wide), bf16),
            pltpu.VMEM((2 * chips, inner, rows), f32),
            pltpu.VMEM((2 * chips, 3, rows, inner), f32),
            dma((2 * chips,)),
            dma((2 * chips, 4)),
        ],
        vmem=16,
    )


def input_grad(x, g, dn, gain):
    unit, inv_std = unit_rows(x.astype(f32))
    du = dn.astype(f32) * gain
    d = inv_std * (du - jnp.mean(du, -1, keepdims=True) - unit * jnp.mean(du * unit, -1, keepdims=True))
    return (g.astype(f32) + d).astype(bf16)


def pair_sum_kernel(keep_ref, got_ref, own_ref, other_ref):
    for at, ref in enumerate((own_ref, other_ref)):

        @pl.when(pl.program_id(0) == at)
        def _():
            ref[...] = (keep_ref[0].astype(f32) + got_ref[0].astype(f32)).astype(bf16)


def pair_sum(keep, got, after):
    _, _, rows, width = keep.shape
    block = pl.BlockSpec((1, 2, rows, width), lambda i: (i, 0, 0, 0))
    out = pl.BlockSpec((2, rows, width), lambda i: (0, 0, 0))
    return call(
        pair_sum_kernel, (2,), (keep, got), [block, block], [out, out], [shape_of(2, rows, width)] * 2, 1, after, vmem=12
    )


def own_quarter_kernel(place_ref, x_ref, g_ref, own_ref, got_ref, gain, out_ref, again_ref):
    total = own_ref[...].astype(f32) + got_ref[...].astype(f32)
    tokens = input_grad(x_ref[0], g_ref[0], total[0], gain[...])
    mixed = total[1].astype(bf16)
    for ref in (out_ref, again_ref):
        ref[0] = tokens
        ref[1] = mixed


def own_quarter(place, start, x, g, own, got, gain, loose):
    _, rows, width = own.shape
    per = x.shape[1] // rows
    block = pl.BlockSpec((1, rows, width), lambda i, place: (start + place[1] // per, place[1] % per, 0))
    return call(
        own_quarter_kernel,
        (1,),
        (x, g, own, got, gain),
        [block, block, whole(own), whole(got), whole(gain)],
        [pl.BlockSpec(own.shape, lambda i, _: (0, 0, 0))] * 2,
        [shape_of(*own.shape)] * 2,
        2,
        scalars=(place,),
        vmem=12,
        after=loose,
    )


def placed_kernel(place_ref, *refs, pieces, start):
    tokens_ref, mixed_ref, stage, in_sems, out_sems = refs[-5:]
    rows = stage.shape[2]
    per = tokens_ref.shape[1] // rows
    loads = [pltpu.make_async_copy(ref, stage.at[at], in_sems.at[at]) for at, ref in enumerate(refs[:pieces])]
    for load in loads:
        load.start()
    stores = []
    for at, load in enumerate(loads):
        load.wait()
        quarter = place_ref[1] ^ at
        spot = start + quarter // per, pl.ds((quarter % per) * rows, rows)
        for which, out in enumerate((tokens_ref, mixed_ref)):
            stores.append(pltpu.make_async_copy(stage.at[at, which], out.at[spot], out_sems.at[at, which]))
            stores[-1].start()
    for store in stores:
        store.wait()


def placed(place, shape, start, pieces, before, after):
    ins, alias, count = tuple(pieces), {}, len(pieces)
    if before is not None:
        alias = {count: 0, count + 1: 1}
        ins += tuple(before)
    dma = pltpu.SemaphoreType.DMA
    return call(
        partial(placed_kernel, pieces=count, start=start),
        (1,),
        ins,
        [anywhere] * len(ins),
        [anywhere, anywhere],
        [shape_of(*shape)] * 2,
        2,
        after,
        (place,),
        [pltpu.VMEM((count,) + pieces[0].shape, bf16), dma((count,)), dma((count, 2))],
        alias,
        vmem=6,
    )


def exchanged(x, bits):
    return lax.ppermute(x, "seq", [(i, i ^ bits) for i in range(lax.axis_size("seq"))])


def by_pairs(
    tokens, ln_gain, ln_bias, w_query, w_key, w_value, w_attn_out, w_in, b_in, w_mlp_out, b_out, cotangent
):
    x, cot = tokens[0], cotangent[0]
    seqs, rows, width = x.shape
    inner = w_query.shape[1]
    ff = w_in.shape[1]
    heads = inner // HEAD_DIM
    shards = lax.axis_size("seq")
    count = shards // heads
    in_hbm.clear()
    in_hbm.add(x, cot, w_query, w_key, w_value, w_attn_out, w_in, w_mlp_out)
    row = lambda v: v.reshape(1, -1)
    gain, b_in, b_out = row(ln_gain), row(b_in), row(b_out)
    flat_cot = cot.reshape(-1, width)
    in_hbm.add(flat_cot)
    shard = lax.axis_index("seq").astype(jnp.int32)
    core, chip, chips = (shard % 2).reshape(1), (shard // 2).reshape(1), shards // 2
    z = lax.axis_index("mlp").astype(jnp.int32)
    place = jnp.stack([shard, z])
    tables = tuple(map(jnp.asarray, position_tables(shards * rows)))
    in_hbm.add(*tables)
    weights = (w_query, w_key, w_value, w_attn_out)
    pre_consts = (gain, row(ln_bias)) + weights
    post_consts = (b_out,) + weights

    def attend(sent, after):
        done = attention(sent.reshape(1, shards * rows, 4 * HEAD_DIM), after)
        return done.reshape(shards, rows, 4 * HEAD_DIM)

    def traded(v):
        return lax.all_to_all(v, "seq", 0, 0, tiled=True)

    def over_line(v, bits):
        return lax.ppermute(v, "mlp", [(i, i ^ bits) for i in range(4)])

    dense_args = (flat_cot, w_in, b_in, w_mlp_out)
    normed, packed_a = pre(0, count, place, x, cot, pre_consts, tables, None)
    sent_a = traded(packed_a)
    normed, packed_b = pre(1, count, place, x, cot, pre_consts, tables, normed)
    hidden, dgate, part_a, dn_a, db_in_a, db_out_a = mlp(0, count, rows, normed, *dense_args, None, (packed_b,))
    done_a = attend(sent_a, (db_in_a,))
    back_a = traded(done_a)
    hidden, dgate, part_b, dn_b, db_in_b, db_out_b = mlp(1, count, rows, normed, *dense_args, (hidden, dgate), (done_a,))
    sent_b = traded(fence(packed_b, back_a, db_in_b))
    give_a, keep_a, flat, gain_a, bias_a = post(
        0, count, place, back_a, x, part_a, dn_a, post_consts, tables, None, (db_in_b,)
    )
    got_a = over_line(give_a, 1)
    done_b = attend(sent_b, (gain_a,))
    back_b = traded(done_b)
    own_a, other_a = pair_sum(keep_a, got_a, (done_b,))
    got_a = over_line(other_a, 2)
    give_e, keep_e = dense_grads(core, normed, dgate, hidden, flat_cot, (own_a,))
    got_e = exchanged(give_e, 1)
    give_b, keep_b, flat, gain_b, bias_b = post(
        1, count, place, back_b, x, part_b, dn_b, post_consts, tables, flat, (keep_e,)
    )

    def over_chips(v):
        same_core = [list(range(side, shards, 2)) for side in (0, 1)]
        return lax.all_to_all(v, "seq", 0, 0, axis_index_groups=same_core, tiled=True)

    dense, token = split(keep_e, got_e, None, chips, (gain_b,))
    dense = over_chips(dense)
    done_a, more_a = own_quarter(place, 0, x, cot, own_a, got_a, gain, (token,))
    small = jnp.concatenate([gain_a + gain_b, bias_a + bias_b, db_in_a + db_in_b, db_out_a + db_out_b], 0)
    small = jnp.concatenate([small, jnp.zeros((12, width), f32)], 0).astype(bf16)
    give_l, keep_l = head_grads(core, normed, flat_cot, flat, small, (more_a,))
    far_a = over_line(more_a, 2)
    got_b = over_line(give_b, 1)
    own_b, other_b = pair_sum(keep_b, got_b, (keep_l,))
    near_a = over_line(fence(done_a, own_b), 1)
    got_b = over_line(other_b, 2)
    got_l = exchanged(give_l, 1)
    head, token = split(keep_l, got_l, small, chips, (own_b,))
    dense, token = total(dense, 1, (token,))
    head = over_chips(fence(head, token))
    dense = [dense[0]] + [exchanged(dense[0], 2 * k) for k in range(1, chips)]
    far_a = fence(far_a, token)
    beside_a = over_line(far_a, 1)
    near_a = fence(near_a, far_a)
    done_b, more_b = own_quarter(place, count, x, cot, own_b, got_b, gain, (near_a,))
    near_b = over_line(done_b, 1)
    far_b = over_line(more_b, 2)
    dense = jnp.stack([dense[0]] + [fence(v, done_b) for v in dense[1:]])
    dense_other = exchanged(dense, 1)
    head, token = total(head, chips, (dense,))
    small = head[0, 0, -small.shape[0] :].astype(f32)
    vectors = small[:2]
    vectors_got = over_line(vectors, 1)
    head = over_chips(head)
    far_b = fence(far_b, token)
    beside_b = over_line(far_b, 1)
    dense_other = fence(dense_other, far_b)
    d_in, d_out = dense_outs(jnp.concatenate([core, chip]), dense, dense_other, width, (far_b,))
    beside_a = fence(beside_a, d_out)
    d_tokens, mixed = placed(place, x.shape, 0, (more_a, near_a, far_a, beside_a), None, (beside_a,))
    head = fence(head, d_tokens)
    head_other = exchanged(head, 1)
    near_b = fence(near_b, head)
    beside_b = fence(beside_b, near_b)
    d_tokens, mixed = placed(place, x.shape, count, (more_b, near_b, far_b, beside_b), (d_tokens, mixed), (beside_b,))
    vectors = vectors + fence(vectors_got, d_tokens)
    vectors_got = over_line(vectors, 2)
    head_other = fence(head_other, d_tokens)
    d_attn_out, d_query, d_key, d_value = head_outs(
        jnp.concatenate([core, jnp.zeros_like(core)]), head, head_other, width, (d_tokens,)
    )
    vectors = vectors + fence(vectors_got, d_value)
    return (
        mixed.reshape(tokens.shape),
        d_tokens[None],
        vectors[0],
        vectors[1],
        d_query,
        d_key,
        d_value,
        d_attn_out,
        d_in,
        small[2],
        d_out,
        small[3],
    )


def per_device(
    tokens, ln_gain, ln_bias, w_query, w_key, w_value, w_attn_out, w_in, b_in, w_mlp_out, b_out, cotangent
):
    _, seqs, rows, width = tokens.shape
    inner = w_query.shape[1]
    heads = inner // HEAD_DIM
    shards = lax.axis_size("seq")
    fits = shards == 8 and lax.axis_size("mlp") == 4 and seqs * heads == 2 * shards and shards % heads == 0
    fits = fits and inner % 128 == 0 and rows % 256 == 0 and width % 1024 == 0 and w_in.shape[1] == width
    fits = fits and 4 * inner == width
    plan = by_pairs if fits else by_ring
    return plan(
        tokens, ln_gain, ln_bias, w_query, w_key, w_value, w_attn_out, w_in, b_in, w_mlp_out, b_out, cotangent
    )


def solution(mesh):
    rows, whole = P("seq", None, None, None), P()
    cols, down = P(None, "mlp"), P("mlp", None)
    return jax.shard_map(
        per_device,
        mesh=mesh,
        in_specs=(rows, whole, whole, cols, cols, cols, down, cols, P("mlp"), down, whole, rows),
        out_specs=(rows, rows, whole, whole, cols, cols, cols, down, cols, P("mlp"), down, whole),
        check_vma=False,
    )
```

profile of v0, /device:TPU:0, one launch (start us, length us, event | category | flops | bytes accessed | tf_op | source)
XLA Modules:
  0.0 247.9 jit_solution(18216475309112088206)
XLA Ops:
  0.7 0.7 copy-done
  1.4 0.7 copy-done.5
  2.1 5.6 %pre_kernel.2 = (bf16[1024,1024]{1,0:T(8,128)(2,1)}, bf16[8,256,256]{2,1,0:T(8,128)(2,1)}) custom-call(s32[2]{0:T(128)S(1)} %pad_add_fusion.refs_0_, bf16[4,256,1024]{2,1,0:T(8,128)(2,1)} %bitcast.43, bf16[4,256,1024]{2,1,0:T(8,128)(2,1)} %bitcast.49, f32[1,1024]{1,0:T(1,128)S(1)} %bitcast.35, f32[1,1024]{1,0:T(1,128)S(1)} %bitcast.29, ...), custom_call_target="tpu_custom_call" | custom-call | flops 299999985664 | tf_op jit(solution)/shard_map/pre_kernel/pallas_call | solution.py:307
  7.7 5.3 %all-to-all-start = ((bf16[8,256,256]{2,1,0:T(8,128)(2,1)}), bf16[8,256,256]{2,1,0:T(8,128)(2,1)}, u32[]{:S(2)}, u32[]{:S(2)}) async-start(bf16[8,256,256]{2,1,0:T(8,128)(2,1)} %get-tuple-element.70), calls=%async_computation | async-start | bytes 2097152 | tf_op jit(solution)/shard_map/all_to_all | solution.py:934
  13.1 5.6 %pre_kernel.3 = (bf16[1024,1024]{1,0:T(8,128)(2,1)}, bf16[8,256,256]{2,1,0:T(8,128)(2,1)}) custom-call(s32[2]{0:T(128)S(1)} %pad_add_fusion.refs_0_, bf16[4,256,1024]{2,1,0:T(8,128)(2,1)} %bitcast.44, bf16[4,256,1024]{2,1,0:T(8,128)(2,1)} %bitcast.50, f32[1,1024]{1,0:T(1,128)S(1)} %bitcast.36, ...), custom_call_target="tpu_custom_call", output_to_operand_aliasing={{0}: (11, {})} | custom-call | flops 299999985664 | tf_op jit(solution)/shard_map/pre_kernel/pallas_call | solution.py:307
  18.7 9.2 %mlp_kernel.2 = (bf16[1024,1024]{1,0:T(8,128)(2,1)}, bf16[1024,1024]{1,0:T(8,128)(2,1)}, bf16[512,1024]{1,0:T(8,128)(2,1)}, bf16[512,1024]{1,0:T(8,128)(2,1)}, f32[1,1024]{1,0:T(1,128)}, /*index=5*/f32[1,1024]{1,0:T(1,128)}) custom-call(bf16[1024,1024]{1,0:T(8,128)(2,1)} %get-tuple-element.71.refs_0_.refs_1_, bf16[1024,1024]{1,0:T(8,128)(2,1)} %bitcast.51, ...), custom_call_target="tpu_custom_call" | custom-call | flops 499999997952 | tf_op jit(solution)/shard_map/mlp_kernel/pallas_call | solution.py:307
  28.1 0.5 all-to-all-done
  28.6 11.0 %attention_kernel.2 = bf16[1,2048,256]{2,1,0:T(8,128)(2,1)} custom-call(bf16[1,2048,256]{2,1,0:T(8,128)(2,1)} %bitcast.6.refs_0_, f32[1,1024]{1,0:T(1,128)} %get-tuple-element.72.refs_1_), custom_call_target="tpu_custom_call" | custom-call | flops 699999977472 | tf_op jit(solution)/shard_map/attention_kernel/pallas_call | solution.py:307
  39.6 4.6 %all-to-all-start.1 = ((bf16[8,256,256]{2,1,0:T(8,128)(2,1)}), bf16[8,256,256]{2,1,0:T(8,128)(2,1)}, u32[]{:S(2)}, u32[]{:S(2)}) async-start(bf16[8,256,256]{2,1,0:T(8,128)(2,1)} %bitcast.9.refs_7_), calls=%async_computation.1 | async-start | bytes 2097152 | tf_op jit(solution)/shard_map/all_to_all | solution.py:934
  44.2 9.3 %mlp_kernel.3 = (bf16[1024,1024]{1,0:T(8,128)(2,1)}, bf16[1024,1024]{1,0:T(8,128)(2,1)}, bf16[512,1024]{1,0:T(8,128)(2,1)}, bf16[512,1024]{1,0:T(8,128)(2,1)}, f32[1,1024]{1,0:T(1,128)}, /*index=5*/f32[1,1024]{1,0:T(1,128)}) custom-call(bf16[1024,1024]{1,0:T(8,128)(2,1)} %get-tuple-element.71.refs_0_.refs_1_, ...), custom_call_target="tpu_custom_call", output_to_operand_aliasing={{0}: (5, {}), {1}: (6, {})} | custom-call | flops 499999997952 | tf_op jit(solution)/shard_map/mlp_kernel/pallas_call | solution.py:307
  53.5 1.3 add_convert_fusion
  54.8 4.6 %all-to-all-done.1.refs_1_ = bf16[8,256,256]{2,1,0:T(8,128)(2,1)} async-done(((bf16[8,256,256]{2,1,0:T(8,128)(2,1)}), bf16[8,256,256]{2,1,0:T(8,128)(2,1)}, u32[]{:S(2)}, u32[]{:S(2)}) %all-to-all-start.1) | async-done | bytes 1048608 | tf_op jit(solution)/shard_map/all_to_all | solution.py:934
  59.4 4.4 %all-to-all-start.2 = ((bf16[8,256,256]{2,1,0:T(8,128)(2,1)}), bf16[8,256,256]{2,1,0:T(8,128)(2,1)}, u32[]{:S(2)}, u32[]{:S(2)}) async-start(bf16[8,256,256]{2,1,0:T(8,128)(2,1)} %lambda.17), calls=%async_computation.2 | async-start | bytes 2097152 | tf_op jit(solution)/shard_map/all_to_all | solution.py:934
  63.8 6.9 %post_kernel.2 = (bf16[2,2,128,1024]{3,2,1,0:T(8,128)(2,1)}, bf16[2,2,128,1024]{3,2,1,0:T(8,128)(2,1)}, bf16[1024,1024]{1,0:T(8,128)(2,1)}, f32[1,1024]{1,0:T(1,128)}, f32[1,1024]{1,0:T(1,128)}) custom-call(s32[2]{0:T(128)S(1)} %pad_add_fusion.refs_0_, bf16[8,256,256]{2,1,0:T(8,128)(2,1)} %all-to-all-done.1.refs_1_, bf16[4,256,1024]{2,1,0:T(8,128)(2,1)} %bitcast.45, ...), custom_call_target="tpu_custom_call" | custom-call | flops 399999991808 | tf_op jit(solution)/shard_map/post_kernel/pallas_call | solution.py:307
  70.7 2.0 collective-permute-start
  72.8 6.4 %all-to-all-done.2 = bf16[8,256,256]{2,1,0:T(8,128)(2,1)} async-done(((bf16[8,256,256]{2,1,0:T(8,128)(2,1)}), bf16[8,256,256]{2,1,0:T(8,128)(2,1)}, u32[]{:S(2)}, u32[]{:S(2)}) %all-to-all-start.2) | async-done | bytes 1048608 | tf_op jit(solution)/shard_map/all_to_all | solution.py:934
  79.2 11.0 %attention_kernel.3 = bf16[1,2048,256]{2,1,0:T(8,128)(2,1)} custom-call(bf16[1,2048,256]{2,1,0:T(8,128)(2,1)} %bitcast.10.refs_0_, f32[1,1024]{1,0:T(1,128)} %get-tuple-element.78.refs_1_), custom_call_target="tpu_custom_call" | custom-call | flops 699999977472 | tf_op jit(solution)/shard_map/attention_kernel/pallas_call | solution.py:307
  90.2 4.5 %all-to-all-start.3 = ((bf16[8,256,256]{2,1,0:T(8,128)(2,1)}), bf16[8,256,256]{2,1,0:T(8,128)(2,1)}, u32[]{:S(2)}, u32[]{:S(2)}) async-start(bf16[8,256,256]{2,1,0:T(8,128)(2,1)} %bitcast.12.refs_2_), calls=%async_computation.3 | async-start | bytes 2097152 | tf_op jit(solution)/shard_map/all_to_all | solution.py:934
  94.7 2.1 collective-permute-done.refs_1_
  96.7 2.6 %pair_sum_kernel.2 = (bf16[2,128,1024]{2,1,0:T(8,128)(2,1)}, bf16[2,128,1024]{2,1,0:T(8,128)(2,1)}) custom-call(bf16[2,2,128,1024]{3,2,1,0:T(8,128)(2,1)} %get-tuple-element.84.refs_0_, bf16[2,2,128,1024]{3,2,1,0:T(8,128)(2,1)} %collective-permute-done.refs_1_, bf16[8,256,256]{2,1,0:T(8,128)(2,1)} %bitcast.12.refs_2_), custom_call_target="tpu_custom_call" | custom-call | flops 99999997952 | tf_op jit(solution)/shard_map/pair_sum_kernel/pallas_call | solution.py:307
  99.4 2.8 %collective-permute-start.2 = (bf16[2,128,1024]{2,1,0:T(8,128)(2,1)}, bf16[2,128,1024]{2,1,0:T(8,128)(2,1)}, u32[]{:S(2)}, u32[]{:S(2)}) collective-permute-start(bf16[2,128,1024]{2,1,0:T(8,128)(2,1)} %get-tuple-element.96), channel_id=1, source_target_pairs={{0,2},{1,3},{2,0},{3,1},{4,6},{5,7},{6,4},{7,5},{8,10},{9,11},{10,... | collective-permute-start | bytes 1572872 | tf_op jit(solution)/shard_map/ppermute | solution.py:937
  102.1 9.7 %dense_grads_kernel.1 = (bf16[2,512,1024]{2,1,0:T(8,128)(2,1)}, bf16[2,512,1024]{2,1,0:T(8,128)(2,1)}) custom-call(s32[1]{0:T(128)} %bitcast.13.refs_0_, bf16[1024,1024]{1,0:T(8,128)(2,1)} %get-tuple-element.71.refs_0_.refs_1_, bf16[1024,1024]{1,0:T(8,128)(2,1)} %get-tuple-element.82.refs_2_, bf16[1024,1024]{1,0:T(8,128)(2,1)} %get-tuple-element.83.refs_3_, ...), custom_call_target="tpu_custom_call" | custom-call | flops 599999971328 | tf_op jit(solution)/shard_map/dense_grads_kernel/pallas_call | solution.py:307
  111.9 7.0 %post_kernel.3 = (bf16[2,2,128,1024]{3,2,1,0:T(8,128)(2,1)}, bf16[2,2,128,1024]{3,2,1,0:T(8,128)(2,1)}, bf16[1024,1024]{1,0:T(8,128)(2,1)}, f32[1,1024]{1,0:T(1,128)}, f32[1,1024]{1,0:T(1,128)}) custom-call(s32[2]{0:T(128)S(1)} %pad_add_fusion.refs_0_, bf16[8,256,256]{2,1,0:T(8,128)(2,1)} %all-to-all-done.3.refs_1_, ...), custom_call_target="tpu_custom_call", output_to_operand_aliasing={{2}: (12, {})} | custom-call | flops 399999991808 | tf_op jit(solution)/shard_map/post_kernel/pallas_call | solution.py:307
  118.8 1.6 collective-permute-start.1
  120.5 0.7 add_convert_fusion.2
  121.2 0.2 concatenate.10.refs_4_.refs_2_
  121.5 4.3 %split_kernel.2 = (bf16[4,2,128,1024]{3,2,1,0:T(8,128)(2,1)}, f32[8,128]{1,0:T(8,128)}) custom-call(bf16[2,512,1024]{2,1,0:T(8,128)(2,1)} %get-tuple-element.87.refs_13_.refs_0_, bf16[2,512,1024]{2,1,0:T(8,128)(2,1)} %collective-permute-done.3.refs_1_, f32[1,1024]{1,0:T(1,128)} %get-tuple-element.91.refs_2_), custom_call_target="tpu_custom_call" | custom-call | flops 199999995904 | tf_op jit(solution)/shard_map/split_kernel/pallas_call | solution.py:307
  125.8 4.6 %all-to-all-start.4 = ((bf16[4,2,128,1024]{3,2,1,0:T(8,128)(2,1)}), bf16[4,2,128,1024]{3,2,1,0:T(8,128)(2,1)}, u32[]{:S(2)}, u32[]{:S(2)}) async-start(bf16[4,2,128,1024]{3,2,1,0:T(8,128)(2,1)} %get-tuple-element.104), calls=%async_computation.4 | async-start | bytes 4194304 | tf_op jit(solution)/shard_map/all_to_all | solution.py:964
  130.4 3.4 %own_quarter_kernel.2 = (bf16[2,128,1024]{2,1,0:T(8,128)(2,1)}, bf16[2,128,1024]{2,1,0:T(8,128)(2,1)}) custom-call(s32[2]{0:T(128)S(1)} %copy-done.9, bf16[4,256,1024]{2,1,0:T(8,128)(2,1)} %bitcast.47, bf16[4,256,1024]{2,1,0:T(8,128)(2,1)} %bitcast.54, bf16[2,128,1024]{2,1,0:T(8,128)(2,1)} %get-tuple-element.86.refs_5_.refs_3_, ...), custom_call_target="tpu_custom_call" | custom-call | flops 199999995904 | tf_op jit(solution)/shard_map/own_quarter_kernel/pallas_call | solution.py:307
  133.9 1.2 collective-permute-start.6
  135.1 6.9 %head_grads_kernel.1 = (bf16[1,768,1024]{2,1,0:T(8,128)(2,1)}, bf16[1,512,1024]{2,1,0:T(8,128)(2,1)}) custom-call(s32[1]{0:T(128)} %bitcast.13.refs_0_, bf16[1024,1024]{1,0:T(8,128)(2,1)} %get-tuple-element.71.refs_0_.refs_1_, bf16[1024,1024]{1,0:T(8,128)(2,1)} %bitcast.55, bf16[1024,1024]{1,0:T(8,128)(2,1)} %get-tuple-element.90.refs_3_, ...), custom_call_target="tpu_custom_call" | custom-call | flops 399999991808 | tf_op jit(solution)/shard_map/head_grads_kernel/pallas_call | solution.py:307
  142.0 12.5 %collective-permute-done.1.refs_1_ = bf16[2,2,128,1024]{3,2,1,0:T(8,128)(2,1)} collective-permute-done((bf16[2,2,128,1024]{3,2,1,0:T(8,128)(2,1)}, bf16[2,2,128,1024]{3,2,1,0:T(8,128)(2,1)}, u32[]{:S(2)}, u32[]{:S(2)}) %collective-permute-start.1) | collective-permute-done | bytes 1048608 | tf_op jit(solution)/shard_map/ppermute | solution.py:937
  154.5 2.6 %pair_sum_kernel.3 = (bf16[2,128,1024]{2,1,0:T(8,128)(2,1)}, bf16[2,128,1024]{2,1,0:T(8,128)(2,1)}) custom-call(bf16[2,2,128,1024]{3,2,1,0:T(8,128)(2,1)} %get-tuple-element.88.refs_0_, bf16[2,2,128,1024]{3,2,1,0:T(8,128)(2,1)} %collective-permute-done.1.refs_1_, bf16[1,512,1024]{2,1,0:T(8,128)(2,1)} %get-tuple-element.100.refs_2_.refs_0_), custom_call_target="tpu_custom_call" | custom-call | flops 99999997952 | tf_op jit(solution)/shard_map/pair_sum_kernel/pallas_call | solution.py:307
  157.1 8.6 %collective-permute-start.4 = (bf16[2,128,1024]{2,1,0:T(8,128)(2,1)}, bf16[2,128,1024]{2,1,0:T(8,128)(2,1)}, u32[]{:S(2)}, u32[]{:S(2)}) collective-permute-start(bf16[2,128,1024]{2,1,0:T(8,128)(2,1)} %get-tuple-element.102), channel_id=1, source_target_pairs={{0,2},{1,3},{2,0},{3,1},{4,6},{5,7},{6,4},{7,5},{8,10},{9,11},{10,... | collective-permute-start | bytes 1572872 | tf_op jit(solution)/shard_map/ppermute | solution.py:937
  165.7 3.7 %split_kernel.3 = (bf16[4,1,144,1024]{3,2,1,0:T(8,128)(2,1)}, f32[8,128]{1,0:T(8,128)}) custom-call(bf16[1,512,1024]{2,1,0:T(8,128)(2,1)} %get-tuple-element.100.refs_2_.refs_0_, bf16[1,768,1024]{2,1,0:T(8,128)(2,1)} %collective-permute-done.7.refs_1_.refs_3_, bf16[16,1024]{1,0:T(8,128)(2,1)S(1)} %concatenate.10.refs_4_.refs_2_, ...), custom_call_target="tpu_custom_call" | custom-call | flops 199999995904 | tf_op jit(solution)/shard_map/split_kernel/pallas_call | solution.py:307
  169.4 3.6 %total_kernel.2 = (bf16[1,2,128,1024]{3,2,1,0:T(8,128)(2,1)}, f32[8,128]{1,0:T(8,128)}) custom-call(bf16[4,2,128,1024]{3,2,1,0:T(8,128)(2,1)} %all-to-all-done.4.refs_0_, f32[8,128]{1,0:T(8,128)} %get-tuple-element.106.refs_1_), custom_call_target="tpu_custom_call" | custom-call | flops 199999995904 | tf_op jit(solution)/shard_map/total_kernel/pallas_call | solution.py:307
  173.0 2.4 collective-permute-start.11
  175.3 0.6 collective-permute-start.10
  175.9 4.3 %all-to-all-start.5 = ((bf16[4,1,144,1024]{3,2,1,0:T(8,128)(2,1)}), bf16[4,1,144,1024]{3,2,1,0:T(8,128)(2,1)}, u32[]{:S(2)}, u32[]{:S(2)}) async-start(bf16[4,1,144,1024]{3,2,1,0:T(8,128)(2,1)} %lambda.21), calls=%async_computation.5 | async-start | bytes 2359296 | tf_op jit(solution)/shard_map/all_to_all | solution.py:964
  180.2 2.0 collective-permute-start.9
  182.2 0.5 collective-permute-done.5.refs_0_
  182.7 6.1 %collective-permute-done.4.refs_4_ = bf16[2,128,1024]{2,1,0:T(8,128)(2,1)} collective-permute-done((bf16[2,128,1024]{2,1,0:T(8,128)(2,1)}, bf16[2,128,1024]{2,1,0:T(8,128)(2,1)}, u32[]{:S(2)}, u32[]{:S(2)}) %collective-permute-start.4) | collective-permute-done | bytes 524320 | tf_op jit(solution)/shard_map/ppermute | solution.py:937
  188.8 3.4 %own_quarter_kernel.3 = (bf16[2,128,1024]{2,1,0:T(8,128)(2,1)}, bf16[2,128,1024]{2,1,0:T(8,128)(2,1)}) custom-call(s32[2]{0:T(128)S(1)} %copy-done.9, bf16[4,256,1024]{2,1,0:T(8,128)(2,1)} %bitcast.48, bf16[4,256,1024]{2,1,0:T(8,128)(2,1)} %bitcast.56, bf16[2,128,1024]{2,1,0:T(8,128)(2,1)} %get-tuple-element.101.refs_1_.refs_4_.refs_3_, ...), custom_call_target="tpu_custom_call" | custom-call | flops 199999995904 | tf_op jit(solution)/shard_map/own_quarter_kernel/pallas_call | solution.py:307
  192.2 3.4 %collective-permute-start.8 = (bf16[2,128,1024]{2,1,0:T(8,128)(2,1)}, bf16[2,128,1024]{2,1,0:T(8,128)(2,1)}, u32[]{:S(2)}, u32[]{:S(2)}) collective-permute-start(bf16[2,128,1024]{2,1,0:T(8,128)(2,1)} %get-tuple-element.109.refs_1_), channel_id=1, source_target_pairs={{0,1},{1,0},{2,3},{3,2},{4,5},{5,4},{6,7},{7,6},{8,9},{9,8},{10,11... | collective-permute-start | bytes 1572872 | tf_op jit(solution)/shard_map/ppermute | solution.py:937
  195.6 9.5 %collective-permute-done.10.refs_0_ = bf16[2,128,1024]{2,1,0:T(8,128)(2,1)} collective-permute-done((bf16[2,128,1024]{2,1,0:T(8,128)(2,1)}, bf16[2,128,1024]{2,1,0:T(8,128)(2,1)}, u32[]{:S(2)}, u32[]{:S(2)}) %collective-permute-start.10) | collective-permute-done | bytes 524320 | tf_op jit(solution)/shard_map/ppermute | solution.py:900
  205.1 6.3 %collective-permute-done.9.refs_0_ = bf16[2,128,1024]{2,1,0:T(8,128)(2,1)} collective-permute-done((bf16[2,128,1024]{2,1,0:T(8,128)(2,1)}, bf16[2,128,1024]{2,1,0:T(8,128)(2,1)}, u32[]{:S(2)}, u32[]{:S(2)}) %collective-permute-start.9) | collective-permute-done | bytes 524320 | tf_op jit(solution)/shard_map/ppermute | solution.py:900
  211.5 3.1 %pad_maximum_fusion.refs_1_ = bf16[4,2,128,1024]{3,2,1,0:T(8,128)(2,1)} fusion(bf16[1,2,128,1024]{3,2,1,0:T(8,128)(2,1)} %bitcast.17, bf16[1,2,128,1024]{3,2,1,0:T(8,128)(2,1)} %bitcast.16, bf16[1,2,128,1024]{3,2,1,0:T(8,128)(2,1)} %bitcast.15, bf16[1,2,128,1024]{3,2,1,0:T(8,128)(2,1)} %get-tuple-element.111), kind=kLoop, calls=%fused_computation | loop fusion | flops 3145728 | bytes 4194304 | tf_op jit(solution)/shard_map/stack | solution.py:988
  214.6 2.2 total_kernel.3
  216.8 4.3 %all-to-all-start.6 = ((bf16[4,1,144,1024]{3,2,1,0:T(8,128)(2,1)}), bf16[4,1,144,1024]{3,2,1,0:T(8,128)(2,1)}, u32[]{:S(2)}, u32[]{:S(2)}) async-start(bf16[4,1,144,1024]{3,2,1,0:T(8,128)(2,1)} %get-tuple-element.112), calls=%async_computation.6 | async-start | bytes 2359296 | tf_op jit(solution)/shard_map/all_to_all | solution.py:964
  221.1 0.8 slice_convert_fusion
  221.8 0.6 slice_bitcast_fusion
  222.5 0.3 collective-permute-start.16
  222.8 1.7 collective-permute-start.15
  224.5 0.6 fusion.1
  225.1 5.1 %dense_outs_kernel.1 = (f32[1024,1024]{1,0:T(8,128)}, f32[1024,1024]{1,0:T(8,128)}) custom-call(s32[2]{0:T(128)S(1)} %pad_add_fusion.1.refs_0_, bf16[4,2,128,1024]{3,2,1,0:T(8,128)(2,1)} %pad_maximum_fusion.refs_1_, bf16[4,2,128,1024]{3,2,1,0:T(8,128)(2,1)} %lambda.26.refs_2_, bf16[2,128,1024]{2,1,0:T(8,128)(2,1)} %lambda.25.refs_1_.refs_3_), custom_call_target="tpu_custom_call" | custom-call | flops 399999991808 | tf_op jit(solution)/shard_map/dense_outs_kernel/pallas_call | solution.py:307
  230.2 3.0 %placed_kernel.2 = (bf16[4,256,1024]{2,1,0:T(8,128)(2,1)}, bf16[4,256,1024]{2,1,0:T(8,128)(2,1)}) custom-call(s32[2]{0:T(128)S(1)} %copy-done.9, bf16[2,128,1024]{2,1,0:T(8,128)(2,1)} %get-tuple-element.99.refs_5_.refs_1_, bf16[2,128,1024]{2,1,0:T(8,128)(2,1)} %lambda.20.refs_6_.refs_2_, bf16[2,128,1024]{2,1,0:T(8,128)(2,1)} %lambda.19.refs_1_.refs_3_, ...), custom_call_target="tpu_custom_call" | custom-call | flops 199999995904 | tf_op jit(solution)/shard_map/placed_kernel/pallas_call | solution.py:307
  233.2 3.9 %all-to-all-done.6.refs_0_ = bf16[4,1,144,1024]{3,2,1,0:T(8,128)(2,1)} async-done(((bf16[4,1,144,1024]{3,2,1,0:T(8,128)(2,1)}), bf16[4,1,144,1024]{3,2,1,0:T(8,128)(2,1)}, u32[]{:S(2)}, u32[]{:S(2)}) %all-to-all-start.6) | async-done | bytes 1179680 | tf_op jit(solution)/shard_map/all_to_all | solution.py:964
  237.3 3.0 %placed_kernel.3 = (bf16[4,256,1024]{2,1,0:T(8,128)(2,1)}, bf16[4,256,1024]{2,1,0:T(8,128)(2,1)}) custom-call(s32[2]{0:T(128)S(1)} %copy-done.9, bf16[2,128,1024]{2,1,0:T(8,128)(2,1)} %get-tuple-element.108.refs_1_, bf16[2,128,1024]{2,1,0:T(8,128)(2,1)} %lambda.29.refs_1_.refs_2_, ...), custom_call_target="tpu_custom_call", output_to_operand_aliasing={{0}: (5, {}), {1}: (6, {})} | custom-call | flops 199999995904 | tf_op jit(solution)/shard_map/placed_kernel/pallas_call | solution.py:307
  240.3 1.4 fusion
  241.7 0.3 collective-permute-start.17
  242.0 3.9 %head_outs_kernel.1 = (f32[256,1024]{1,0:T(8,128)}, f32[1024,256]{1,0:T(8,128)}, f32[1024,256]{1,0:T(8,128)}, f32[1024,256]{1,0:T(8,128)}) custom-call(s32[2]{0:T(128)S(1)} %pad_add_fusion.2.refs_0_, bf16[4,1,144,1024]{3,2,1,0:T(8,128)(2,1)} %lambda.28.refs_1_, bf16[4,1,144,1024]{3,2,1,0:T(8,128)(2,1)} %lambda.32.refs_2_, ...), custom_call_target="tpu_custom_call" | custom-call | flops 299999985664 | tf_op jit(solution)/shard_map/head_outs_kernel/pallas_call | solution.py:307
  245.9 0.6 collective-permute-done.17.refs_0_
  246.6 0.7 add.29
  247.3 0.6 fusion.2
  (75 shorter events, 0.5 us)
Async XLA Ops:
  0.7 111.1 %copy-start.8 = (s32[2]{0:T(128)}, s32[2]{0:T(128)S(1)}, u32[]{:S(2)}) copy-start(s32[2]{0:T(128)S(1)} %pad_add_fusion.refs_0_) | copy-start | bytes 28
  0.7 0.7 copy-start
  1.4 0.7 copy-start.5
  7.7 5.3 %copy-start.1 = (f32[1024]{0:T(1024)S(1)}, f32[1024]{0:T(1024)}, u32[]{:S(2)}) copy-start(f32[1024]{0:T(1024)} %param.16) | copy-start | bytes 12292
  7.7 5.3 %copy-start.6 = (f32[1024]{0:T(1024)S(1)}, f32[1024]{0:T(1024)}, u32[]{:S(2)}) copy-start(f32[1024]{0:T(1024)} %param.15) | copy-start | bytes 12292
  7.7 20.8 %all-to-all-start = ((bf16[8,256,256]{2,1,0:T(8,128)(2,1)}), bf16[8,256,256]{2,1,0:T(8,128)(2,1)}, u32[]{:S(2)}, u32[]{:S(2)}) async-start(bf16[8,256,256]{2,1,0:T(8,128)(2,1)} %get-tuple-element.70), calls=%async_computation | async-start | bytes 2097152 | tf_op jit(solution)/shard_map/all_to_all | solution.py:934
  13.1 5.7 %copy-start.2 = (f32[1024]{0:T(1024)S(1)}, f32[1024]{0:T(1024)}, u32[]{:S(2)}) copy-start(f32[1024]{0:T(1024)} %param.22) | copy-start | bytes 12292
  39.6 4.6 %copy-start.3 = (f32[1024]{0:T(1024)S(1)}, f32[1024]{0:T(1024)}, u32[]{:S(2)}) copy-start(f32[1024]{0:T(1024)} %param.22) | copy-start | bytes 12292
  39.6 19.8 %all-to-all-start.1 = ((bf16[8,256,256]{2,1,0:T(8,128)(2,1)}), bf16[8,256,256]{2,1,0:T(8,128)(2,1)}, u32[]{:S(2)}, u32[]{:S(2)}) async-start(bf16[8,256,256]{2,1,0:T(8,128)(2,1)} %bitcast.9.refs_7_), calls=%async_computation.1 | async-start | bytes 2097152 | tf_op jit(solution)/shard_map/all_to_all | solution.py:934
  44.2 9.3 %copy-start.13 = (f32[1,1024]{1,0:T(1,128)S(1)}, f32[1,1024]{1,0:T(1,128)}, u32[]{:S(2)}) copy-start(f32[1,1024]{1,0:T(1,128)} %get-tuple-element.72.refs_1_) | copy-start | bytes 12292
  44.2 9.3 %copy-start.14 = (f32[1,1024]{1,0:T(1,128)S(1)}, f32[1,1024]{1,0:T(1,128)}, u32[]{:S(2)}) copy-start(f32[1,1024]{1,0:T(1,128)} %get-tuple-element.94) | copy-start | bytes 12292
  59.4 4.4 %copy-start.4 = (f32[1024]{0:T(1024)S(1)}, f32[1024]{0:T(1024)}, u32[]{:S(2)}) copy-start(f32[1024]{0:T(1024)} %param.24) | copy-start | bytes 12292
  59.4 19.8 %all-to-all-start.2 = ((bf16[8,256,256]{2,1,0:T(8,128)(2,1)}), bf16[8,256,256]{2,1,0:T(8,128)(2,1)}, u32[]{:S(2)}, u32[]{:S(2)}) async-start(bf16[8,256,256]{2,1,0:T(8,128)(2,1)} %lambda.17), calls=%async_computation.2 | async-start | bytes 2097152 | tf_op jit(solution)/shard_map/all_to_all | solution.py:934
  70.7 26.0 %collective-permute-start = (bf16[2,2,128,1024]{3,2,1,0:T(8,128)(2,1)}, bf16[2,2,128,1024]{3,2,1,0:T(8,128)(2,1)}, u32[]{:S(2)}, u32[]{:S(2)}) collective-permute-start(bf16[2,2,128,1024]{3,2,1,0:T(8,128)(2,1)} %get-tuple-element.85), channel_id=1, source_target_pairs={{0,1},{1,0},{2,3},{3,2},{4,5},{5,4},{6,7},{7,6},{8,9},{9,8},{10,11... | collective-permute-start | bytes 3145736 | tf_op jit(solution)/shard_map/ppermute | solution.py:937
  90.2 21.6 %all-to-all-start.3 = ((bf16[8,256,256]{2,1,0:T(8,128)(2,1)}), bf16[8,256,256]{2,1,0:T(8,128)(2,1)}, u32[]{:S(2)}, u32[]{:S(2)}) async-start(bf16[8,256,256]{2,1,0:T(8,128)(2,1)} %bitcast.12.refs_2_), calls=%async_computation.3 | async-start | bytes 2097152 | tf_op jit(solution)/shard_map/all_to_all | solution.py:934
  99.4 31.0 %collective-permute-start.2 = (bf16[2,128,1024]{2,1,0:T(8,128)(2,1)}, bf16[2,128,1024]{2,1,0:T(8,128)(2,1)}, u32[]{:S(2)}, u32[]{:S(2)}) collective-permute-start(bf16[2,128,1024]{2,1,0:T(8,128)(2,1)} %get-tuple-element.96), channel_id=1, source_target_pairs={{0,2},{1,3},{2,0},{3,1},{4,6},{5,7},{6,4},{7,5},{8,10},{9,11},{10,... | collective-permute-start | bytes 1572872 | tf_op jit(solution)/shard_map/ppermute | solution.py:937
  111.8 9.6 %collective-permute-start.3 = (bf16[2,512,1024]{2,1,0:T(8,128)(2,1)}, bf16[2,512,1024]{2,1,0:T(8,128)(2,1)}, u32[]{:S(2)}, u32[]{:S(2)}) collective-permute-start(bf16[2,512,1024]{2,1,0:T(8,128)(2,1)} %get-tuple-element.97), channel_id=1, source_target_pairs={{0,4},{4,0},{8,12},{12,8},{16,20},{20,16},{24,28},{28,24},{1,5},{5... | collective-permute-start | bytes 6291464 | tf_op jit(solution)/shard_map/ppermute | solution.py:900
  111.8 8.7 %copy-start.15 = (f32[1,1024]{1,0:T(1,128)S(1)}, f32[1,1024]{1,0:T(1,128)}, u32[]{:S(2)}) copy-start(f32[1,1024]{1,0:T(1,128)} %get-tuple-element.78.refs_1_) | copy-start | bytes 12292
  111.8 8.6 %copy-start.16 = (f32[1,1024]{1,0:T(1,128)S(1)}, f32[1,1024]{1,0:T(1,128)}, u32[]{:S(2)}) copy-start(f32[1,1024]{1,0:T(1,128)} %get-tuple-element.92) | copy-start | bytes 12292
  111.9 9.4 %copy-start.11 = (bf16[1,1024]{1,0:T(2,128)(2,1)S(1)}, bf16[1,1024]{1,0:T(2,128)(2,1)}, u32[]{:S(2)}) copy-start(bf16[1,1024]{1,0:T(2,128)(2,1)} %get-tuple-element.128) | copy-start | bytes 6148
  111.9 9.4 %copy-start.12 = (bf16[1,1024]{1,0:T(2,128)(2,1)S(1)}, bf16[1,1024]{1,0:T(2,128)(2,1)}, u32[]{:S(2)}) copy-start(bf16[1,1024]{1,0:T(2,128)(2,1)} %get-tuple-element.129) | copy-start | bytes 6148
  118.8 35.6 %collective-permute-start.1 = (bf16[2,2,128,1024]{3,2,1,0:T(8,128)(2,1)}, bf16[2,2,128,1024]{3,2,1,0:T(8,128)(2,1)}, u32[]{:S(2)}, u32[]{:S(2)}) collective-permute-start(bf16[2,2,128,1024]{3,2,1,0:T(8,128)(2,1)} %get-tuple-element.89), channel_id=1, source_target_pairs={{0,1},{1,0},{2,3},{3,2},{4,5},{5,4},{6,7},{7,6},{8,9},{9,8},{10,11... | collective-permute-start | bytes 3145736 | tf_op jit(solution)/shard_map/ppermute | solution.py:937
  125.8 4.6 %copy-start.7 = (f32[1024]{0:T(1024)S(1)}, f32[1024]{0:T(1024)}, u32[]{:S(2)}) copy-start(f32[1024]{0:T(1024)} %param.15) | copy-start | bytes 12292
  125.8 4.6 %copy-start.9 = (s32[2]{0:T(128)S(1)}, s32[2]{0:T(128)}, u32[]{:S(2)}) copy-start(s32[2]{0:T(128)} %copy-done.8) | copy-start | bytes 28
  125.8 43.6 %all-to-all-start.4 = ((bf16[4,2,128,1024]{3,2,1,0:T(8,128)(2,1)}), bf16[4,2,128,1024]{3,2,1,0:T(8,128)(2,1)}, u32[]{:S(2)}, u32[]{:S(2)}) async-start(bf16[4,2,128,1024]{3,2,1,0:T(8,128)(2,1)} %get-tuple-element.104), calls=%async_computation.4 | async-start | bytes 4194304 | tf_op jit(solution)/shard_map/all_to_all | solution.py:964
  133.9 46.3 %collective-permute-start.6 = (bf16[2,128,1024]{2,1,0:T(8,128)(2,1)}, bf16[2,128,1024]{2,1,0:T(8,128)(2,1)}, u32[]{:S(2)}, u32[]{:S(2)}) collective-permute-start(bf16[2,128,1024]{2,1,0:T(8,128)(2,1)} %get-tuple-element.99.refs_5_.refs_1_), channel_id=1, source_target_pairs={{0,2},{1,3},{2,0},{3,1},{4,6},{5,7},{6,4},{7,5},{8,10},{9,11},{10,... | collective-permute-start | bytes 1572872 | tf_op jit(solution)/shard_map/ppermute | solution.py:937
  142.0 23.7 %collective-permute-start.7 = (bf16[1,768,1024]{2,1,0:T(8,128)(2,1)}, bf16[1,768,1024]{2,1,0:T(8,128)(2,1)}, u32[]{:S(2)}, u32[]{:S(2)}) collective-permute-start(bf16[1,768,1024]{2,1,0:T(8,128)(2,1)} %get-tuple-element.105), channel_id=1, source_target_pairs={{0,4},{4,0},{8,12},{12,8},{16,20},{20,16},{24,28},{28,24},{1,5},{5... | collective-permute-start | bytes 4718600 | tf_op jit(solution)/shard_map/ppermute | solution.py:900
  157.1 25.6 %collective-permute-start.5 = (bf16[2,128,1024]{2,1,0:T(8,128)(2,1)}, bf16[2,128,1024]{2,1,0:T(8,128)(2,1)}, u32[]{:S(2)}, u32[]{:S(2)}) collective-permute-start(bf16[2,128,1024]{2,1,0:T(8,128)(2,1)} %lambda.18), channel_id=1, source_target_pairs={{0,1},{1,0},{2,3},{3,2},{4,5},{5,4},{6,7},{7,6},{8,9},{9,8},{10,11... | collective-permute-start | bytes 1572872 | tf_op jit(solution)/shard_map/ppermute | solution.py:937
  157.1 31.7 %collective-permute-start.4 = (bf16[2,128,1024]{2,1,0:T(8,128)(2,1)}, bf16[2,128,1024]{2,1,0:T(8,128)(2,1)}, u32[]{:S(2)}, u32[]{:S(2)}) collective-permute-start(bf16[2,128,1024]{2,1,0:T(8,128)(2,1)} %get-tuple-element.102), channel_id=1, source_target_pairs={{0,2},{1,3},{2,0},{3,1},{4,6},{5,7},{6,4},{7,5},{8,10},{9,11},{10,... | collective-permute-start | bytes 1572872 | tf_op jit(solution)/shard_map/ppermute | solution.py:937
  173.0 19.2 %collective-permute-start.11 = (bf16[2,128,1024]{2,1,0:T(8,128)(2,1)}, bf16[2,128,1024]{2,1,0:T(8,128)(2,1)}, u32[]{:S(2)}, u32[]{:S(2)}) collective-permute-start(bf16[2,128,1024]{2,1,0:T(8,128)(2,1)} %bitcast.14), channel_id=1, source_target_pairs={{0,24},{4,28},{8,16},{12,20},{16,8},{20,12},{24,0},{28,4},{1,25},{... | collective-permute-start | bytes 1572872 | tf_op jit(solution)/shard_map/ppermute | solution.py:900
  175.3 29.8 %collective-permute-start.10 = (bf16[2,128,1024]{2,1,0:T(8,128)(2,1)}, bf16[2,128,1024]{2,1,0:T(8,128)(2,1)}, u32[]{:S(2)}, u32[]{:S(2)}) collective-permute-start(bf16[2,128,1024]{2,1,0:T(8,128)(2,1)} %bitcast.14), channel_id=1, source_target_pairs={{0,16},{4,20},{8,24},{12,28},{16,0},{20,4},{24,8},{28,12},{1,17},{... | collective-permute-start | bytes 1572872 | tf_op jit(solution)/shard_map/ppermute | solution.py:900
  175.9 38.6 %all-to-all-start.5 = ((bf16[4,1,144,1024]{3,2,1,0:T(8,128)(2,1)}), bf16[4,1,144,1024]{3,2,1,0:T(8,128)(2,1)}, u32[]{:S(2)}, u32[]{:S(2)}) async-start(bf16[4,1,144,1024]{3,2,1,0:T(8,128)(2,1)} %lambda.21), calls=%async_computation.5 | async-start | bytes 2359296 | tf_op jit(solution)/shard_map/all_to_all | solution.py:964
  180.2 31.2 %collective-permute-start.9 = (bf16[2,128,1024]{2,1,0:T(8,128)(2,1)}, bf16[2,128,1024]{2,1,0:T(8,128)(2,1)}, u32[]{:S(2)}, u32[]{:S(2)}) collective-permute-start(bf16[2,128,1024]{2,1,0:T(8,128)(2,1)} %bitcast.14), channel_id=1, source_target_pairs={{0,8},{4,12},{8,0},{12,4},{16,24},{20,28},{24,16},{28,20},{1,9},{5... | collective-permute-start | bytes 1572872 | tf_op jit(solution)/shard_map/ppermute | solution.py:900
  182.7 47.6 %collective-permute-start.12 = (bf16[2,128,1024]{2,1,0:T(8,128)(2,1)}, bf16[2,128,1024]{2,1,0:T(8,128)(2,1)}, u32[]{:S(2)}, u32[]{:S(2)}) collective-permute-start(bf16[2,128,1024]{2,1,0:T(8,128)(2,1)} %lambda.19.refs_1_.refs_3_), channel_id=1, source_target_pairs={{0,1},{1,0},{2,3},{3,2},{4,5},{5,4},{6,7},{7,6},{8,9},{9,8},{10,11... | collective-permute-start | bytes 1572872 | tf_op jit(solution)/shard_map/ppermute | solution.py:937
  192.2 30.5 %collective-permute-start.14 = (bf16[2,128,1024]{2,1,0:T(8,128)(2,1)}, bf16[2,128,1024]{2,1,0:T(8,128)(2,1)}, u32[]{:S(2)}, u32[]{:S(2)}) collective-permute-start(bf16[2,128,1024]{2,1,0:T(8,128)(2,1)} %get-tuple-element.108.refs_1_), channel_id=1, source_target_pairs={{0,2},{1,3},{2,0},{3,1},{4,6},{5,7},{6,4},{7,5},{8,10},{9,11},{10,... | collective-permute-start | bytes 1572872 | tf_op jit(solution)/shard_map/ppermute | solution.py:937
  192.2 44.9 %collective-permute-start.8 = (bf16[2,128,1024]{2,1,0:T(8,128)(2,1)}, bf16[2,128,1024]{2,1,0:T(8,128)(2,1)}, u32[]{:S(2)}, u32[]{:S(2)}) collective-permute-start(bf16[2,128,1024]{2,1,0:T(8,128)(2,1)} %get-tuple-element.109.refs_1_), channel_id=1, source_target_pairs={{0,1},{1,0},{2,3},{3,2},{4,5},{5,4},{6,7},{7,6},{8,9},{9,8},{10,11... | collective-permute-start | bytes 1572872 | tf_op jit(solution)/shard_map/ppermute | solution.py:937
  214.6 10.6 %collective-permute-start.13 = (bf16[4,2,128,1024]{3,2,1,0:T(8,128)(2,1)}, bf16[4,2,128,1024]{3,2,1,0:T(8,128)(2,1)}, u32[]{:S(2)}, u32[]{:S(2)}) collective-permute-start(bf16[4,2,128,1024]{3,2,1,0:T(8,128)(2,1)} %pad_maximum_fusion.refs_1_), channel_id=1, source_target_pairs={{0,4},{4,0},{8,12},{12,8},{16,20},{20,16},{24,28},{28,24},{1,5},{5... | collective-permute-start | bytes 6291464 | tf_op jit(solution)/shard_map/ppermute | solution.py:900
  216.8 20.3 %all-to-all-start.6 = ((bf16[4,1,144,1024]{3,2,1,0:T(8,128)(2,1)}), bf16[4,1,144,1024]{3,2,1,0:T(8,128)(2,1)}, u32[]{:S(2)}, u32[]{:S(2)}) async-start(bf16[4,1,144,1024]{3,2,1,0:T(8,128)(2,1)} %get-tuple-element.112), calls=%async_computation.6 | async-start | bytes 2359296 | tf_op jit(solution)/shard_map/all_to_all | solution.py:964
  221.8 2.7 %copy-start.10 = (f32[1,1,16,1024]{3,2,1,0:T(8,128)}, f32[1,1,16,1024]{3,2,1,0:T(8,128)S(1)}, u32[]{:S(2)}) copy-start(f32[1,1,16,1024]{3,2,1,0:T(8,128)S(1)} %slice_convert_fusion) | copy-start | bytes 196612
  222.5 17.8 %collective-permute-start.16 = (f32[2,1024]{1,0:T(2,128)}, f32[2,1024]{1,0:T(2,128)}, u32[]{:S(2)}, u32[]{:S(2)}) collective-permute-start(f32[2,1024]{1,0:T(2,128)} %slice_bitcast_fusion), channel_id=1, source_target_pairs={{0,1},{1,0},{2,3},{3,2},{4,5},{5,4},{6,7},{7,6},{8,9},{9,8},{10,11... | collective-permute-start | bytes 24584 | tf_op jit(solution)/shard_map/ppermute | solution.py:937
  222.8 14.5 %collective-permute-start.15 = (bf16[2,128,1024]{2,1,0:T(8,128)(2,1)}, bf16[2,128,1024]{2,1,0:T(8,128)(2,1)}, u32[]{:S(2)}, u32[]{:S(2)}) collective-permute-start(bf16[2,128,1024]{2,1,0:T(8,128)(2,1)} %lambda.25.refs_1_.refs_3_), channel_id=1, source_target_pairs={{0,1},{1,0},{2,3},{3,2},{4,5},{5,4},{6,7},{7,6},{8,9},{9,8},{10,11... | collective-permute-start | bytes 1572872 | tf_op jit(solution)/shard_map/ppermute | solution.py:937
  237.1 4.9 %collective-permute-start.18 = (bf16[4,1,144,1024]{3,2,1,0:T(8,128)(2,1)}, bf16[4,1,144,1024]{3,2,1,0:T(8,128)(2,1)}, u32[]{:S(2)}, u32[]{:S(2)}) collective-permute-start(bf16[4,1,144,1024]{3,2,1,0:T(8,128)(2,1)} %lambda.28.refs_1_), channel_id=1, source_target_pairs={{0,4},{4,0},{8,12},{12,8},{16,20},{20,16},{24,28},{28,24},{1,5},{5... | collective-permute-start | bytes 3538952 | tf_op jit(solution)/shard_map/ppermute | solution.py:900
  241.7 4.9 %collective-permute-start.17 = (f32[2,1024]{1,0:T(2,128)}, f32[2,1024]{1,0:T(2,128)}, u32[]{:S(2)}, u32[]{:S(2)}) collective-permute-start(f32[2,1024]{1,0:T(2,128)} %fusion), channel_id=1, source_target_pairs={{0,2},{1,3},{2,0},{3,1},{4,6},{5,7},{6,4},{7,5},{8,10},{9,11},{10,... | collective-permute-start | bytes 24584 | tf_op jit(solution)/shard_map/ppermute | solution.py:937
where the time goes:
time: 250 us; the launch traced here: 248 us
  Pallas kernels  123 us (49%)
  starting transfers between devices  58.8 us (24%)
  waiting for transfers between devices  53.1 us (21%)
  other arithmetic  8.21 us (3%)
  local copies, waits for them, and re-layouts  3.46 us (1%)
    pallas_call x39, Pallas kernels, call(): pl.pallas_call(body, name=getattr(kernel, 'func', kernel).__name__.strip(...  123 us
    ppermute x12, starting transfers between devices, over_line(): return lax.ppermute(v, 'mlp', [(i, i ^ bits) for i in range(4)])  22 us
    ppermute x12, waiting for transfers between devices, over_line(): return lax.ppermute(v, 'mlp', [(i, i ^ bits) for i in range(4)])  21.9 us
    all_to_all x4, starting transfers between devices, traded(): return lax.all_to_all(v, 'seq', 0, 0, tiled=True)  18.7 us
    ppermute x7, waiting for transfers between devices, exchanged(): lax.ppermute(x, 'seq', [(i, i ^ bits) for i in range(lax.axis_size('seq'))])  15.9 us
    all_to_all x3, starting transfers between devices, over_chips(): lax.all_to_all(v, 'seq', 0, 0, axis_index_groups=same_core, tiled=True)  13.2 us
    all_to_all x4, waiting for transfers between devices, traded(): return lax.all_to_all(v, 'seq', 0, 0, tiled=True)  11.4 us
  transfers between devices with their start and end apart: 26, of which 12 were waited for; matrix products, arithmetic and copies ran while one was open for 4% of the time, Pallas kernels for 43%

commit v1 on v0

--- a/solution.py
+++ b/solution.py
@@ -684,6 +684,64 @@
     )
 
 
+def parted_kernel(chip_ref, keep_ref, got_ref, *outs):
+    outs[-1][...] = jnp.zeros_like(outs[-1])
+    total = (keep_ref[...].astype(f32) + got_ref[...].astype(f32)).astype(bf16)
+    for k, out in enumerate(outs[:-1]):
+
+        @pl.when(pl.program_id(0) == k)
+        def _():
+            out[...] = total
+
+
+def parted(chip, keep, got, chips, after):
+    slots, rows, wide = keep.shape
+    rows = rows // chips
+    block = pl.BlockSpec((slots, rows, wide), lambda k, chip: (0, chip[0] ^ k, 0))
+    one = pl.BlockSpec((slots, rows, wide), lambda k, chip: (0, 0, 0))
+    return call(
+        parted_kernel,
+        (chips,),
+        (keep, got),
+        [block, block],
+        [one] * chips + [pl.BlockSpec((8, 128), lambda k, chip: (0, 0))],
+        [shape_of(slots, rows, wide)] * chips + [shape_of(8, 128, dtype=f32)],
+        2,
+        after,
+        (chip,),
+        vmem=16,
+    )
+
+
+def joined_kernel(*refs):
+    parts, (out_ref, token_ref) = refs[:-2], refs[-2:]
+    token_ref[...] = jnp.zeros_like(token_ref)
+    total = parts[0][...].astype(f32)
+    for part in parts[1:]:
+        total = total + part[...].astype(f32)
+    for k in range(out_ref.shape[0]):
+        out_ref[k] = total.astype(bf16)
+
+
+def joined(parts, after):
+    slots, rows, wide = parts[0].shape
+    block = pl.BlockSpec((1, rows, wide // 2), lambda i: (i // 2, 0, i % 2))
+    return call(
+        joined_kernel,
+        (2 * slots,),
+        tuple(parts),
+        [block] * len(parts),
+        [
+            pl.BlockSpec((len(parts), 1, rows, wide // 2), lambda i: (0, i // 2, 0, i % 2)),
+            pl.BlockSpec((8, 128), lambda i: (0, 0)),
+        ],
+        [shape_of(len(parts), slots, rows, wide), shape_of(8, 128, dtype=f32)],
+        2,
+        after,
+        vmem=16,
+    )
+
+
 def total_kernel(parts_ref, out_ref, token_ref):
     token_ref[...] = jnp.zeros_like(token_ref)
     total = parts_ref[0].astype(f32)
@@ -828,16 +886,16 @@
     )
 
 
-def own_quarter_kernel(place_ref, x_ref, g_ref, own_ref, got_ref, gain, out_ref, again_ref):
+def own_quarter_kernel(place_ref, x_ref, g_ref, own_ref, got_ref, gain, *outs):
     total = own_ref[...].astype(f32) + got_ref[...].astype(f32)
     tokens = input_grad(x_ref[0], g_ref[0], total[0], gain[...])
     mixed = total[1].astype(bf16)
-    for ref in (out_ref, again_ref):
+    for ref in outs:
         ref[0] = tokens
         ref[1] = mixed
 
 
-def own_quarter(place, start, x, g, own, got, gain, loose):
+def own_quarter(place, start, x, g, own, got, gain, copies, loose):
     _, rows, width = own.shape
     per = x.shape[1] // rows
     block = pl.BlockSpec((1, rows, width), lambda i, place: (start + place[1] // per, place[1] % per, 0))
@@ -846,8 +904,8 @@
         (1,),
         (x, g, own, got, gain),
         [block, block, whole(own), whole(got), whole(gain)],
-        [pl.BlockSpec(own.shape, lambda i, _: (0, 0, 0))] * 2,
-        [shape_of(*own.shape)] * 2,
+        [pl.BlockSpec(own.shape, lambda i, _: (0, 0, 0))] * copies,
+        [shape_of(*own.shape)] * copies,
         2,
         scalars=(place,),
         vmem=12,
@@ -913,7 +971,8 @@
     in_hbm.clear()
     in_hbm.add(x, cot, w_query, w_key, w_value, w_attn_out, w_in, w_mlp_out)
     row = lambda v: v.reshape(1, -1)
-    gain, b_in, b_out = row(ln_gain), row(b_in), row(b_out)
+    gain, bias, b_in, b_out = row(ln_gain), row(ln_bias), row(b_in), row(b_out)
+    in_hbm.add(gain, bias, b_in, b_out)
     flat_cot = cot.reshape(-1, width)
     in_hbm.add(flat_cot)
     shard = lax.axis_index("seq").astype(jnp.int32)
@@ -923,7 +982,7 @@
     tables = tuple(map(jnp.asarray, position_tables(shards * rows)))
     in_hbm.add(*tables)
     weights = (w_query, w_key, w_value, w_attn_out)
-    pre_consts = (gain, row(ln_bias)) + weights
+    pre_consts = (gain, bias) + weights
     post_consts = (b_out,) + weights
 
     def attend(sent, after):
@@ -949,67 +1008,69 @@
         0, count, place, back_a, x, part_a, dn_a, post_consts, tables, None, (db_in_b,)
     )
     got_a = over_line(give_a, 1)
-    done_b = attend(sent_b, (gain_a,))
+    give_e, keep_e = dense_grads(core, normed, dgate, hidden, flat_cot, (gain_a,))
+    got_e = exchanged(give_e, 1)
+    done_b = attend(sent_b, (keep_e,))
     back_b = traded(done_b)
     own_a, other_a = pair_sum(keep_a, got_a, (done_b,))
+    *dense, token = parted(chip, keep_e, got_e, chips, (own_a,))
+    dense = [dense[0]] + [exchanged(dense[k], 2 * k) for k in range(1, chips)]
     got_a = over_line(other_a, 2)
-    give_e, keep_e = dense_grads(core, normed, dgate, hidden, flat_cot, (own_a,))
-    got_e = exchanged(give_e, 1)
     give_b, keep_b, flat, gain_b, bias_b = post(
-        1, count, place, back_b, x, part_b, dn_b, post_consts, tables, flat, (keep_e,)
+        1, count, place, back_b, x, part_b, dn_b, post_consts, tables, flat, (token,)
     )
 
     def over_chips(v):
         same_core = [list(range(side, shards, 2)) for side in (0, 1)]
         return lax.all_to_all(v, "seq", 0, 0, axis_index_groups=same_core, tiled=True)
 
-    dense, token = split(keep_e, got_e, None, chips, (gain_b,))
+    dense[1] = fence(dense[1], gain_b)
+    dense[2] = fence(dense[2], dense[1])
+    done_a, more_a, again_a = own_quarter(place, 0, x, cot, own_a, got_a, gain, 3, (dense[2],))
+    dense, token = joined(dense, (more_a,))
     dense = over_chips(dense)
-    done_a, more_a = own_quarter(place, 0, x, cot, own_a, got_a, gain, (token,))
     small = jnp.concatenate([gain_a + gain_b, bias_a + bias_b, db_in_a + db_in_b, db_out_a + db_out_b], 0)
     small = jnp.concatenate([small, jnp.zeros((12, width), f32)], 0).astype(bf16)
-    give_l, keep_l = head_grads(core, normed, flat_cot, flat, small, (more_a,))
-    far_a = over_line(more_a, 2)
+    give_l, keep_l = head_grads(core, normed, flat_cot, flat, small, (token,))
+    far_a = over_line(done_a, 2)
     got_b = over_line(give_b, 1)
     own_b, other_b = pair_sum(keep_b, got_b, (keep_l,))
-    near_a = over_line(fence(done_a, own_b), 1)
+    near_a = over_line(fence(again_a, own_b), 1)
     got_b = over_line(other_b, 2)
     got_l = exchanged(give_l, 1)
     head, token = split(keep_l, got_l, small, chips, (own_b,))
-    dense, token = total(dense, 1, (token,))
-    head = over_chips(fence(head, token))
-    dense = [dense[0]] + [exchanged(dense[0], 2 * k) for k in range(1, chips)]
-    far_a = fence(far_a, token)
+    dense = fence(dense, token)
+    head = over_chips(fence(head, dense))
+    dense_other = exchanged(dense, 1)
+    far_a = fence(far_a, dense)
     beside_a = over_line(far_a, 1)
-    near_a = fence(near_a, far_a)
-    done_b, more_b = own_quarter(place, count, x, cot, own_b, got_b, gain, (near_a,))
+    done_b, more_b = own_quarter(place, count, x, cot, own_b, got_b, gain, 2, (far_a,))
+    dense_other = fence(dense_other, done_b)
+    d_in, d_out = dense_outs(jnp.concatenate([core, jnp.zeros_like(core)]), dense, dense_other, width, (done_b,))
+    head, token = total(head, chips, (d_out,))
     near_b = over_line(done_b, 1)
     far_b = over_line(more_b, 2)
-    dense = jnp.stack([dense[0]] + [fence(v, done_b) for v in dense[1:]])
-    dense_other = exchanged(dense, 1)
-    head, token = total(head, chips, (dense,))
     small = head[0, 0, -small.shape[0] :].astype(f32)
     vectors = small[:2]
     vectors_got = over_line(vectors, 1)
     head = over_chips(head)
-    far_b = fence(far_b, token)
+    near_a = fence(near_a, token)
+    beside_a = fence(beside_a, near_a)
+    d_tokens, mixed = placed(place, x.shape, 0, (more_a, near_a, far_a, beside_a), None, (beside_a,))
+    far_b = fence(far_b, d_tokens)
     beside_b = over_line(far_b, 1)
-    dense_other = fence(dense_other, far_b)
-    d_in, d_out = dense_outs(jnp.concatenate([core, chip]), dense, dense_other, width, (far_b,))
-    beside_a = fence(beside_a, d_out)
-    d_tokens, mixed = placed(place, x.shape, 0, (more_a, near_a, far_a, beside_a), None, (beside_a,))
-    head = fence(head, d_tokens)
+    vectors = vectors + fence(vectors_got, far_b)
+    vectors_got = over_line(vectors, 2)
+    head = fence(head, far_b)
     head_other = exchanged(head, 1)
-    near_b = fence(near_b, head)
+    head_other = fence(head_other, far_b)
+    d_attn_out, d_query, d_key, d_value = head_outs(
+        jnp.concatenate([core, jnp.zeros_like(core)]), head, head_other, width, (far_b,)
+    )
+    vectors = vectors + fence(vectors_got, d_value)
+    near_b = fence(near_b, vectors)
     beside_b = fence(beside_b, near_b)
     d_tokens, mixed = placed(place, x.shape, count, (more_b, near_b, far_b, beside_b), (d_tokens, mixed), (beside_b,))
-    vectors = vectors + fence(vectors_got, d_tokens)
-    vectors_got = over_line(vectors, 2)
-    head_other = fence(head_other, d_tokens)
-    d_attn_out, d_query, d_key, d_value = head_outs(
-        jnp.concatenate([core, jnp.zeros_like(core)]), head, head_other, width, (d_tokens,)
-    )
-    vectors = vectors + fence(vectors_got, d_value)
     return (
         mixed.reshape(tokens.shape),
         d_tokens[None],

time: 250 us -> 238 us (0.952)
  starting transfers between devices: 58.8 us -> 50.6 us
  other arithmetic: 8.21 us -> 5.02 us
    ppermute x12, waiting for transfers between devices: 21.9 us -> 33.5 us  [over_line(): return lax.ppermute(v, 'mlp', [(i, i ^ bits) for i in range(4)])]
    ppermute x7, waiting for transfers between devices: 15.9 us -> 8.18 us  [exchanged(): lax.ppermute(x, 'seq', [(i, i ^ bits) for i in range(lax.axis_size('seq'))])]
    ppermute x12, starting transfers between devices: 22 us -> 14.7 us  [over_line(): return lax.ppermute(v, 'mlp', [(i, i ^ bits) for i in range(4)])]
    all_to_all x4, waiting for transfers between devices: 11.4 us -> 7.35 us  [traded(): return lax.all_to_all(v, 'seq', 0, 0, tiled=True)]
    another operation x3 -> x2, other arithmetic: 5.12 us -> 2.01 us  [the longest x1 3.09 us: by_pairs(): dense = jnp.stack([dense[0]] + [fence(v, done_b) for v in dense[1:]])]
  transfers between devices with their start and end apart: 26 -> 26, of which waited for: 12 -> 14; matrix products, arithmetic and copies ran while one was open for 4% -> 3% of each run, Pallas kernels for 43% -> 44%
where the time goes in v1:
time: 238 us; the launch traced here: 236 us
  Pallas kernels  124 us (52%)
  waiting for transfers between devices  51.3 us (22%)
  starting transfers between devices  50.6 us (21%)
  other arithmetic  5.02 us (2%)
  local copies, waits for them, and re-layouts  3.45 us (1%)
    pallas_call x39, Pallas kernels, call(): pl.pallas_call(body, name=getattr(kernel, 'func', kernel).__name__.strip(...  124 us
    ppermute x12, waiting for transfers between devices, over_line(): return lax.ppermute(v, 'mlp', [(i, i ^ bits) for i in range(4)])  33.5 us
    all_to_all x4, starting transfers between devices, traded(): return lax.all_to_all(v, 'seq', 0, 0, tiled=True)  18.3 us
    ppermute x12, starting transfers between devices, over_line(): return lax.ppermute(v, 'mlp', [(i, i ^ bits) for i in range(4)])  14.7 us
    all_to_all x3, starting transfers between devices, over_chips(): lax.all_to_all(v, 'seq', 0, 0, axis_index_groups=same_core, tiled=True)  13.9 us
    ppermute x7, waiting for transfers between devices, exchanged(): lax.ppermute(x, 'seq', [(i, i ^ bits) for i in range(lax.axis_size('seq'))])  8.18 us
    all_to_all x4, waiting for transfers between devices, traded(): return lax.all_to_all(v, 'seq', 0, 0, tiled=True)  7.35 us
  transfers between devices with their start and end apart: 26, of which 14 were waited for; matrix products, arithmetic and copies ran while one was open for 3% of the time, Pallas kernels for 44%

profile of v1, /device:TPU:0, one launch (start us, length us, event | category | flops | bytes accessed | tf_op | source)
XLA Modules:
  0.0 235.7 jit_solution(5648480131920425360)
XLA Ops:
  0.7 5.6 %pre_kernel.2 = (bf16[1024,1024]{1,0:T(8,128)(2,1)}, bf16[8,256,256]{2,1,0:T(8,128)(2,1)}) custom-call(s32[2]{0:T(128)S(1)} %pad_add_fusion.refs_0_, bf16[4,256,1024]{2,1,0:T(8,128)(2,1)} %bitcast.29, bf16[4,256,1024]{2,1,0:T(8,128)(2,1)} %bitcast.35, f32[1,1024]{1,0:T(1,128)} %bitcast.49, f32[1,1024]{1,0:T(1,128)} %bitcast.43, bf16[1024,256]{1,0:T(8,128)(2,1)} %refs_6_.7, ...), custom_call_target="tpu_custom_call" | custom-call | flops 299999985664 | tf_op jit(solution)/shard_map/pre_kernel/pallas_call | solution.py:307
  6.4 5.2 %all-to-all-start = ((bf16[8,256,256]{2,1,0:T(8,128)(2,1)}), bf16[8,256,256]{2,1,0:T(8,128)(2,1)}, u32[]{:S(2)}, u32[]{:S(2)}) async-start(bf16[8,256,256]{2,1,0:T(8,128)(2,1)} %get-tuple-element.74), calls=%async_computation | async-start | bytes 2097152 | tf_op jit(solution)/shard_map/all_to_all | solution.py:993
  11.5 5.7 %pre_kernel.3 = (bf16[1024,1024]{1,0:T(8,128)(2,1)}, bf16[8,256,256]{2,1,0:T(8,128)(2,1)}) custom-call(s32[2]{0:T(128)S(1)} %pad_add_fusion.refs_0_, bf16[4,256,1024]{2,1,0:T(8,128)(2,1)} %bitcast.30, bf16[4,256,1024]{2,1,0:T(8,128)(2,1)} %bitcast.36, f32[1,1024]{1,0:T(1,128)} %bitcast.50, f32[1,1024]{1,0:T(1,128)} %bitcast.44, ...), custom_call_target="tpu_custom_call", output_to_operand_aliasing={{0}: (11, {})} | custom-call | flops 299999985664 | tf_op jit(solution)/shard_map/pre_kernel/pallas_call | solution.py:307
  17.2 9.2 %mlp_kernel.2 = (bf16[1024,1024]{1,0:T(8,128)(2,1)}, bf16[1024,1024]{1,0:T(8,128)(2,1)}, bf16[512,1024]{1,0:T(8,128)(2,1)}, bf16[512,1024]{1,0:T(8,128)(2,1)}, f32[1,1024]{1,0:T(1,128)}, /*index=5*/f32[1,1024]{1,0:T(1,128)}) custom-call(bf16[1024,1024]{1,0:T(8,128)(2,1)} %get-tuple-element.75.refs_0_.refs_1_, bf16[1024,1024]{1,0:T(8,128)(2,1)} %bitcast.37, ...), custom_call_target="tpu_custom_call" | custom-call | flops 499999997952 | tf_op jit(solution)/shard_map/mlp_kernel/pallas_call | solution.py:307
  26.5 0.5 all-to-all-done
  27.0 11.0 %attention_kernel.2 = bf16[1,2048,256]{2,1,0:T(8,128)(2,1)} custom-call(bf16[1,2048,256]{2,1,0:T(8,128)(2,1)} %bitcast.6.refs_0_, f32[1,1024]{1,0:T(1,128)} %get-tuple-element.76.refs_1_), custom_call_target="tpu_custom_call" | custom-call | flops 699999977472 | tf_op jit(solution)/shard_map/attention_kernel/pallas_call | solution.py:307
  38.0 4.4 %all-to-all-start.1 = ((bf16[8,256,256]{2,1,0:T(8,128)(2,1)}), bf16[8,256,256]{2,1,0:T(8,128)(2,1)}, u32[]{:S(2)}, u32[]{:S(2)}) async-start(bf16[8,256,256]{2,1,0:T(8,128)(2,1)} %bitcast.9.refs_7_), calls=%async_computation.1 | async-start | bytes 2097152 | tf_op jit(solution)/shard_map/all_to_all | solution.py:993
  42.5 9.3 %mlp_kernel.3 = (bf16[1024,1024]{1,0:T(8,128)(2,1)}, bf16[1024,1024]{1,0:T(8,128)(2,1)}, bf16[512,1024]{1,0:T(8,128)(2,1)}, bf16[512,1024]{1,0:T(8,128)(2,1)}, f32[1,1024]{1,0:T(1,128)}, /*index=5*/f32[1,1024]{1,0:T(1,128)}) custom-call(bf16[1024,1024]{1,0:T(8,128)(2,1)} %get-tuple-element.75.refs_0_.refs_1_, ...), custom_call_target="tpu_custom_call", output_to_operand_aliasing={{0}: (5, {}), {1}: (6, {})} | custom-call | flops 499999997952 | tf_op jit(solution)/shard_map/mlp_kernel/pallas_call | solution.py:307
  51.9 1.3 add_convert_fusion
  53.2 4.5 %all-to-all-done.1.refs_1_ = bf16[8,256,256]{2,1,0:T(8,128)(2,1)} async-done(((bf16[8,256,256]{2,1,0:T(8,128)(2,1)}), bf16[8,256,256]{2,1,0:T(8,128)(2,1)}, u32[]{:S(2)}, u32[]{:S(2)}) %all-to-all-start.1) | async-done | bytes 1048608 | tf_op jit(solution)/shard_map/all_to_all | solution.py:993
  57.7 4.2 %all-to-all-start.2 = ((bf16[8,256,256]{2,1,0:T(8,128)(2,1)}), bf16[8,256,256]{2,1,0:T(8,128)(2,1)}, u32[]{:S(2)}, u32[]{:S(2)}) async-start(bf16[8,256,256]{2,1,0:T(8,128)(2,1)} %lambda.17), calls=%async_computation.2 | async-start | bytes 2097152 | tf_op jit(solution)/shard_map/all_to_all | solution.py:993
  62.0 7.1 %post_kernel.2 = (bf16[2,2,128,1024]{3,2,1,0:T(8,128)(2,1)}, bf16[2,2,128,1024]{3,2,1,0:T(8,128)(2,1)}, bf16[1024,1024]{1,0:T(8,128)(2,1)}, f32[1,1024]{1,0:T(1,128)}, f32[1,1024]{1,0:T(1,128)}) custom-call(s32[2]{0:T(128)S(1)} %pad_add_fusion.refs_0_, bf16[8,256,256]{2,1,0:T(8,128)(2,1)} %all-to-all-done.1.refs_1_, bf16[4,256,1024]{2,1,0:T(8,128)(2,1)} %bitcast.31, ...), custom_call_target="tpu_custom_call" | custom-call | flops 399999991808 | tf_op jit(solution)/shard_map/post_kernel/pallas_call | solution.py:307
  69.0 2.1 collective-permute-start.1
  71.1 9.7 %dense_grads_kernel.1 = (bf16[2,512,1024]{2,1,0:T(8,128)(2,1)}, bf16[2,512,1024]{2,1,0:T(8,128)(2,1)}) custom-call(s32[1]{0:T(128)} %bitcast.11.refs_0_, bf16[1024,1024]{1,0:T(8,128)(2,1)} %get-tuple-element.75.refs_0_.refs_1_, bf16[1024,1024]{1,0:T(8,128)(2,1)} %get-tuple-element.80.refs_2_, bf16[1024,1024]{1,0:T(8,128)(2,1)} %get-tuple-element.81.refs_3_, ...), custom_call_target="tpu_custom_call" | custom-call | flops 599999971328 | tf_op jit(solution)/shard_map/dense_grads_kernel/pallas_call | solution.py:307
  80.9 11.0 %attention_kernel.3 = bf16[1,2048,256]{2,1,0:T(8,128)(2,1)} custom-call(bf16[1,2048,256]{2,1,0:T(8,128)(2,1)} %bitcast.10.refs_0_, bf16[2,512,1024]{2,1,0:T(8,128)(2,1)} %get-tuple-element.85.refs_1_), custom_call_target="tpu_custom_call" | custom-call | flops 699999977472 | tf_op jit(solution)/shard_map/attention_kernel/pallas_call | solution.py:307
  91.9 4.5 %all-to-all-start.3 = ((bf16[8,256,256]{2,1,0:T(8,128)(2,1)}), bf16[8,256,256]{2,1,0:T(8,128)(2,1)}, u32[]{:S(2)}, u32[]{:S(2)}) async-start(bf16[8,256,256]{2,1,0:T(8,128)(2,1)} %bitcast.13.refs_2_), calls=%async_computation.3 | async-start | bytes 2097152 | tf_op jit(solution)/shard_map/all_to_all | solution.py:993
  96.4 2.6 %pair_sum_kernel.2 = (bf16[2,128,1024]{2,1,0:T(8,128)(2,1)}, bf16[2,128,1024]{2,1,0:T(8,128)(2,1)}) custom-call(bf16[2,2,128,1024]{3,2,1,0:T(8,128)(2,1)} %get-tuple-element.90.refs_0_, bf16[2,2,128,1024]{3,2,1,0:T(8,128)(2,1)} %collective-permute-done.1.refs_1_, bf16[8,256,256]{2,1,0:T(8,128)(2,1)} %bitcast.13.refs_2_), custom_call_target="tpu_custom_call" | custom-call | flops 99999997952 | tf_op jit(solution)/shard_map/pair_sum_kernel/pallas_call | solution.py:307
  99.0 2.6 %collective-permute-start.6 = (bf16[2,128,1024]{2,1,0:T(8,128)(2,1)}, bf16[2,128,1024]{2,1,0:T(8,128)(2,1)}, u32[]{:S(2)}, u32[]{:S(2)}) collective-permute-start(bf16[2,128,1024]{2,1,0:T(8,128)(2,1)} %get-tuple-element.106), channel_id=1, source_target_pairs={{0,2},{1,3},{2,0},{3,1},{4,6},{5,7},{6,4},{7,5},{8,10},{9,11},{10,... | collective-permute-start | bytes 1572872 | tf_op jit(solution)/shard_map/ppermute | solution.py:996
  101.6 4.7 %parted_kernel.1 = (bf16[2,128,1024]{2,1,0:T(8,128)(2,1)}, bf16[2,128,1024]{2,1,0:T(8,128)(2,1)}, bf16[2,128,1024]{2,1,0:T(8,128)(2,1)}, bf16[2,128,1024]{2,1,0:T(8,128)(2,1)}, f32[8,128]{1,0:T(8,128)}) custom-call(s32[1]{0:T(128)} %bitcast.14.refs_0_, bf16[2,512,1024]{2,1,0:T(8,128)(2,1)} %get-tuple-element.85.refs_1_, ...), custom_call_target="tpu_custom_call" | custom-call | flops 199999995904 | tf_op jit(solution)/shard_map/parted_kernel/pallas_call | solution.py:307
  106.3 1.7 collective-permute-start.3
  108.0 1.5 collective-permute-start.4
  109.6 0.3 collective-permute-start.5
  109.8 2.3 all-to-all-done.3.refs_1_
  112.1 6.9 %post_kernel.3 = (bf16[2,2,128,1024]{3,2,1,0:T(8,128)(2,1)}, bf16[2,2,128,1024]{3,2,1,0:T(8,128)(2,1)}, bf16[1024,1024]{1,0:T(8,128)(2,1)}, f32[1,1024]{1,0:T(1,128)}, f32[1,1024]{1,0:T(1,128)}) custom-call(s32[2]{0:T(128)S(1)} %pad_add_fusion.refs_0_, bf16[8,256,256]{2,1,0:T(8,128)(2,1)} %all-to-all-done.3.refs_1_, ...), custom_call_target="tpu_custom_call", output_to_operand_aliasing={{2}: (12, {})} | custom-call | flops 399999991808 | tf_op jit(solution)/shard_map/post_kernel/pallas_call | solution.py:307
  119.0 0.3 collective-permute-start.2
  119.4 0.7 add_convert_fusion.2
  120.1 0.2 concatenate.8.refs_4_.refs_2_
  120.3 2.1 collective-permute-done.3.refs_0_
  122.4 0.9 collective-permute-done.4.refs_0_
  123.3 2.3 collective-permute-done.6.refs_4_
  125.6 3.6 %own_quarter_kernel.2 = (bf16[2,128,1024]{2,1,0:T(8,128)(2,1)}, bf16[2,128,1024]{2,1,0:T(8,128)(2,1)}, bf16[2,128,1024]{2,1,0:T(8,128)(2,1)}) custom-call(s32[2]{0:T(128)S(1)} %copy-done.1, bf16[4,256,1024]{2,1,0:T(8,128)(2,1)} %bitcast.33, bf16[4,256,1024]{2,1,0:T(8,128)(2,1)} %bitcast.40, bf16[2,128,1024]{2,1,0:T(8,128)(2,1)} %get-tuple-element.92.refs_3_, ...), custom_call_target="tpu_custom_call" | custom-call | flops 199999995904 | tf_op jit(solution)/shard_map/own_quarter_kernel/pallas_call | solution.py:307
  129.3 5.2 %collective-permute-done.5.refs_3_ = bf16[2,128,1024]{2,1,0:T(8,128)(2,1)} collective-permute-done((bf16[2,128,1024]{2,1,0:T(8,128)(2,1)}, bf16[2,128,1024]{2,1,0:T(8,128)(2,1)}, u32[]{:S(2)}, u32[]{:S(2)}) %collective-permute-start.5) | collective-permute-done | bytes 524320 | tf_op jit(solution)/shard_map/ppermute | solution.py:958
  134.4 3.9 %joined_kernel.1 = (bf16[4,2,128,1024]{3,2,1,0:T(8,128)(2,1)}, f32[8,128]{1,0:T(8,128)}) custom-call(bf16[2,128,1024]{2,1,0:T(8,128)(2,1)} %get-tuple-element.102.refs_0_, bf16[2,128,1024]{2,1,0:T(8,128)(2,1)} %lambda.18.refs_1_, bf16[2,128,1024]{2,1,0:T(8,128)(2,1)} %lambda.19.refs_6_.refs_2_, bf16[2,128,1024]{2,1,0:T(8,128)(2,1)} %collective-permute-done.5.refs_3_, ...), custom_call_target="tpu_custom_call" | custom-call | flops 199999995904 | tf_op jit(solution)/shard_map/joined_kernel/pallas_call | solution.py:307
  138.3 5.4 %all-to-all-start.4 = ((bf16[4,2,128,1024]{3,2,1,0:T(8,128)(2,1)}), bf16[4,2,128,1024]{3,2,1,0:T(8,128)(2,1)}, u32[]{:S(2)}, u32[]{:S(2)}) async-start(bf16[4,2,128,1024]{3,2,1,0:T(8,128)(2,1)} %get-tuple-element.113), calls=%async_computation.4 | async-start | bytes 4194304 | tf_op jit(solution)/shard_map/all_to_all | solution.py:1025
  143.7 6.9 %head_grads_kernel.1 = (bf16[1,768,1024]{2,1,0:T(8,128)(2,1)}, bf16[1,512,1024]{2,1,0:T(8,128)(2,1)}) custom-call(s32[1]{0:T(128)} %bitcast.11.refs_0_, bf16[1024,1024]{1,0:T(8,128)(2,1)} %get-tuple-element.75.refs_0_.refs_1_, bf16[1024,1024]{1,0:T(8,128)(2,1)} %bitcast.41, bf16[1024,1024]{1,0:T(8,128)(2,1)} %get-tuple-element.96.refs_3_, ...), custom_call_target="tpu_custom_call" | custom-call | flops 399999991808 | tf_op jit(solution)/shard_map/head_grads_kernel/pallas_call | solution.py:307
  150.6 8.7 %collective-permute-done.2.refs_1_ = bf16[2,2,128,1024]{3,2,1,0:T(8,128)(2,1)} collective-permute-done((bf16[2,2,128,1024]{3,2,1,0:T(8,128)(2,1)}, bf16[2,2,128,1024]{3,2,1,0:T(8,128)(2,1)}, u32[]{:S(2)}, u32[]{:S(2)}) %collective-permute-start.2) | collective-permute-done | bytes 1048608 | tf_op jit(solution)/shard_map/ppermute | solution.py:996
  159.2 2.6 %pair_sum_kernel.3 = (bf16[2,128,1024]{2,1,0:T(8,128)(2,1)}, bf16[2,128,1024]{2,1,0:T(8,128)(2,1)}) custom-call(bf16[2,2,128,1024]{3,2,1,0:T(8,128)(2,1)} %get-tuple-element.94.refs_0_, bf16[2,2,128,1024]{3,2,1,0:T(8,128)(2,1)} %collective-permute-done.2.refs_1_, bf16[1,512,1024]{2,1,0:T(8,128)(2,1)} %get-tuple-element.109.refs_2_.refs_0_), custom_call_target="tpu_custom_call" | custom-call | flops 99999997952 | tf_op jit(solution)/shard_map/pair_sum_kernel/pallas_call | solution.py:307
  161.8 3.2 %collective-permute-start.7 = (bf16[2,128,1024]{2,1,0:T(8,128)(2,1)}, bf16[2,128,1024]{2,1,0:T(8,128)(2,1)}, u32[]{:S(2)}, u32[]{:S(2)}) collective-permute-start(bf16[2,128,1024]{2,1,0:T(8,128)(2,1)} %get-tuple-element.111), channel_id=1, source_target_pairs={{0,2},{1,3},{2,0},{3,1},{4,6},{5,7},{6,4},{7,5},{8,10},{9,11},{10,... | collective-permute-start | bytes 1572872 | tf_op jit(solution)/shard_map/ppermute | solution.py:996
  165.1 3.7 %split_kernel.1 = (bf16[4,1,144,1024]{3,2,1,0:T(8,128)(2,1)}, f32[8,128]{1,0:T(8,128)}) custom-call(bf16[1,512,1024]{2,1,0:T(8,128)(2,1)} %get-tuple-element.109.refs_2_.refs_0_, bf16[1,768,1024]{2,1,0:T(8,128)(2,1)} %collective-permute-done.9.refs_1_.refs_3_, bf16[16,1024]{1,0:T(8,128)(2,1)S(1)} %concatenate.8.refs_4_.refs_2_, ...), custom_call_target="tpu_custom_call" | custom-call | flops 199999995904 | tf_op jit(solution)/shard_map/split_kernel/pallas_call | solution.py:307
  168.8 4.3 %all-to-all-start.5 = ((bf16[4,1,144,1024]{3,2,1,0:T(8,128)(2,1)}), bf16[4,1,144,1024]{3,2,1,0:T(8,128)(2,1)}, u32[]{:S(2)}, u32[]{:S(2)}) async-start(bf16[4,1,144,1024]{3,2,1,0:T(8,128)(2,1)} %lambda.22), calls=%async_computation.5 | async-start | bytes 2359296 | tf_op jit(solution)/shard_map/all_to_all | solution.py:1025
  173.2 14.9 %collective-permute-done.7.refs_4_ = bf16[2,128,1024]{2,1,0:T(8,128)(2,1)} collective-permute-done((bf16[2,128,1024]{2,1,0:T(8,128)(2,1)}, bf16[2,128,1024]{2,1,0:T(8,128)(2,1)}, u32[]{:S(2)}, u32[]{:S(2)}) %collective-permute-start.7) | collective-permute-done | bytes 524320 | tf_op jit(solution)/shard_map/ppermute | solution.py:996
  188.1 3.4 %own_quarter_kernel.3 = (bf16[2,128,1024]{2,1,0:T(8,128)(2,1)}, bf16[2,128,1024]{2,1,0:T(8,128)(2,1)}) custom-call(s32[2]{0:T(128)S(1)} %copy-done.2, bf16[4,256,1024]{2,1,0:T(8,128)(2,1)} %bitcast.34, bf16[4,256,1024]{2,1,0:T(8,128)(2,1)} %bitcast.42, bf16[2,128,1024]{2,1,0:T(8,128)(2,1)} %get-tuple-element.110.refs_4_.refs_3_.refs_1_, ...), custom_call_target="tpu_custom_call" | custom-call | flops 199999995904 | tf_op jit(solution)/shard_map/own_quarter_kernel/pallas_call | solution.py:307
  191.6 0.9 collective-permute-start.13
  192.5 2.4 %collective-permute-start.10 = (bf16[2,128,1024]{2,1,0:T(8,128)(2,1)}, bf16[2,128,1024]{2,1,0:T(8,128)(2,1)}, u32[]{:S(2)}, u32[]{:S(2)}) collective-permute-start(bf16[2,128,1024]{2,1,0:T(8,128)(2,1)} %get-tuple-element.117.refs_1_.refs_3_), channel_id=1, source_target_pairs={{0,1},{1,0},{2,3},{3,2},{4,5},{5,4},{6,7},{7,6},{8,9},{9,8},{10,11... | collective-permute-start | bytes 1572872 | tf_op jit(solution)/shard_map/ppermute | solution.py:996
  195.0 5.1 %dense_outs_kernel.1 = (f32[1024,1024]{1,0:T(8,128)}, f32[1024,1024]{1,0:T(8,128)}) custom-call(s32[2]{0:T(128)S(1)} %pad_add_fusion.1.refs_0_, bf16[4,2,128,1024]{3,2,1,0:T(8,128)(2,1)} %lambda.20.refs_1_, bf16[4,2,128,1024]{3,2,1,0:T(8,128)(2,1)} %lambda.23.refs_2_, bf16[2,128,1024]{2,1,0:T(8,128)(2,1)} %get-tuple-element.117.refs_1_.refs_3_), custom_call_target="tpu_custom_call" | custom-call | flops 399999991808 | tf_op jit(solution)/shard_map/dense_outs_kernel/pallas_call | solution.py:307
  200.1 2.2 total_kernel.1
  202.3 4.3 %all-to-all-start.6 = ((bf16[4,1,144,1024]{3,2,1,0:T(8,128)(2,1)}), bf16[4,1,144,1024]{3,2,1,0:T(8,128)(2,1)}, u32[]{:S(2)}, u32[]{:S(2)}) async-start(bf16[4,1,144,1024]{3,2,1,0:T(8,128)(2,1)} %get-tuple-element.120), calls=%async_computation.6 | async-start | bytes 2359296 | tf_op jit(solution)/shard_map/all_to_all | solution.py:1025
  206.6 0.8 slice_convert_fusion
  207.4 0.6 slice_bitcast_fusion
  208.0 0.5 copy-done.3
  208.6 3.0 %placed_kernel.2 = (bf16[4,256,1024]{2,1,0:T(8,128)(2,1)}, bf16[4,256,1024]{2,1,0:T(8,128)(2,1)}) custom-call(s32[2]{0:T(128)S(1)} %copy-done.3, bf16[2,128,1024]{2,1,0:T(8,128)(2,1)} %get-tuple-element.107.refs_4_.refs_1_, bf16[2,128,1024]{2,1,0:T(8,128)(2,1)} %lambda.25.refs_1_.refs_2_, bf16[2,128,1024]{2,1,0:T(8,128)(2,1)} %lambda.21.refs_6_.refs_3_, ...), custom_call_target="tpu_custom_call" | custom-call | flops 199999995904 | tf_op jit(solution)/shard_map/placed_kernel/pallas_call | solution.py:307
  211.6 3.6 %collective-permute-done.13.refs_0_ = bf16[2,128,1024]{2,1,0:T(8,128)(2,1)} collective-permute-done((bf16[2,128,1024]{2,1,0:T(8,128)(2,1)}, bf16[2,128,1024]{2,1,0:T(8,128)(2,1)}, u32[]{:S(2)}, u32[]{:S(2)}) %collective-permute-start.13) | collective-permute-done | bytes 524320 | tf_op jit(solution)/shard_map/ppermute | solution.py:996
  215.2 1.7 collective-permute-start.18
  216.9 1.4 fusion.1
  218.4 2.3 all-to-all-done.6.refs_0_
  220.6 1.4 collective-permute-done.12.refs_0_
  222.1 1.4 fusion
  223.4 1.3 collective-permute-start.16
  224.7 3.9 %head_outs_kernel.1 = (f32[256,1024]{1,0:T(8,128)}, f32[1024,256]{1,0:T(8,128)}, f32[1024,256]{1,0:T(8,128)}, f32[1024,256]{1,0:T(8,128)}) custom-call(s32[2]{0:T(128)S(1)} %pad_add_fusion.1.refs_0_, bf16[4,1,144,1024]{3,2,1,0:T(8,128)(2,1)} %lambda.29.refs_1_, bf16[4,1,144,1024]{3,2,1,0:T(8,128)(2,1)S(1)} %lambda.30.refs_2_, ...), custom_call_target="tpu_custom_call" | custom-call | flops 299999985664 | tf_op jit(solution)/shard_map/head_outs_kernel/pallas_call | solution.py:307
  228.6 1.7 collective-permute-done.16.refs_0_
  230.3 0.7 add.29.refs_1_
  231.1 0.6 fusion.2
  231.7 0.8 collective-permute-done.18.refs_0_
  232.5 3.0 %placed_kernel.3 = (bf16[4,256,1024]{2,1,0:T(8,128)(2,1)}, bf16[4,256,1024]{2,1,0:T(8,128)(2,1)}) custom-call(s32[2]{0:T(128)S(1)} %copy-done.4, bf16[2,128,1024]{2,1,0:T(8,128)(2,1)} %get-tuple-element.116.refs_1_, bf16[2,128,1024]{2,1,0:T(8,128)(2,1)} %lambda.32.refs_1_.refs_2_, ...), custom_call_target="tpu_custom_call", output_to_operand_aliasing={{0}: (5, {}), {1}: (6, {})} | custom-call | flops 199999995904 | tf_op jit(solution)/shard_map/placed_kernel/pallas_call | solution.py:307
  (63 shorter events, 0.5 us)
Async XLA Ops:
  0.7 111.4 %copy-start = (s32[2]{0:T(128)}, s32[2]{0:T(128)S(1)}, u32[]{:S(2)}) copy-start(s32[2]{0:T(128)S(1)} %pad_add_fusion.refs_0_) | copy-start | bytes 28
  6.4 20.7 %all-to-all-start = ((bf16[8,256,256]{2,1,0:T(8,128)(2,1)}), bf16[8,256,256]{2,1,0:T(8,128)(2,1)}, u32[]{:S(2)}, u32[]{:S(2)}) async-start(bf16[8,256,256]{2,1,0:T(8,128)(2,1)} %get-tuple-element.74), calls=%async_computation | async-start | bytes 2097152 | tf_op jit(solution)/shard_map/all_to_all | solution.py:993
  38.0 19.7 %all-to-all-start.1 = ((bf16[8,256,256]{2,1,0:T(8,128)(2,1)}), bf16[8,256,256]{2,1,0:T(8,128)(2,1)}, u32[]{:S(2)}, u32[]{:S(2)}) async-start(bf16[8,256,256]{2,1,0:T(8,128)(2,1)} %bitcast.9.refs_7_), calls=%async_computation.1 | async-start | bytes 2097152 | tf_op jit(solution)/shard_map/all_to_all | solution.py:993
  42.5 9.4 %copy-start.10 = (f32[1,1024]{1,0:T(1,128)S(1)}, f32[1,1024]{1,0:T(1,128)}, u32[]{:S(2)}) copy-start(f32[1,1024]{1,0:T(1,128)} %get-tuple-element.76.refs_1_) | copy-start | bytes 12292
  42.5 9.4 %copy-start.11 = (f32[1,1024]{1,0:T(1,128)S(1)}, f32[1,1024]{1,0:T(1,128)}, u32[]{:S(2)}) copy-start(f32[1,1024]{1,0:T(1,128)} %get-tuple-element.100) | copy-start | bytes 12292
  57.7 23.2 %all-to-all-start.2 = ((bf16[8,256,256]{2,1,0:T(8,128)(2,1)}), bf16[8,256,256]{2,1,0:T(8,128)(2,1)}, u32[]{:S(2)}, u32[]{:S(2)}) async-start(bf16[8,256,256]{2,1,0:T(8,128)(2,1)} %lambda.17), calls=%async_computation.2 | async-start | bytes 2097152 | tf_op jit(solution)/shard_map/all_to_all | solution.py:993
  69.0 27.3 %collective-permute-start.1 = (bf16[2,2,128,1024]{3,2,1,0:T(8,128)(2,1)}, bf16[2,2,128,1024]{3,2,1,0:T(8,128)(2,1)}, u32[]{:S(2)}, u32[]{:S(2)}) collective-permute-start(bf16[2,2,128,1024]{3,2,1,0:T(8,128)(2,1)} %get-tuple-element.91), channel_id=1, source_target_pairs={{0,1},{1,0},{2,3},{3,2},{4,5},{5,4},{6,7},{7,6},{8,9},{9,8},{10,11... | collective-permute-start | bytes 3145736 | tf_op jit(solution)/shard_map/ppermute | solution.py:996
  80.8 20.8 %collective-permute-start = (bf16[2,512,1024]{2,1,0:T(8,128)(2,1)}, bf16[2,512,1024]{2,1,0:T(8,128)(2,1)}, u32[]{:S(2)}, u32[]{:S(2)}) collective-permute-start(bf16[2,512,1024]{2,1,0:T(8,128)(2,1)} %get-tuple-element.89), channel_id=1, source_target_pairs={{0,4},{4,0},{8,12},{12,8},{16,20},{20,16},{24,28},{28,24},{1,5},{5... | collective-permute-start | bytes 6291464 | tf_op jit(solution)/shard_map/ppermute | solution.py:958
  91.9 20.2 %all-to-all-start.3 = ((bf16[8,256,256]{2,1,0:T(8,128)(2,1)}), bf16[8,256,256]{2,1,0:T(8,128)(2,1)}, u32[]{:S(2)}, u32[]{:S(2)}) async-start(bf16[8,256,256]{2,1,0:T(8,128)(2,1)} %bitcast.13.refs_2_), calls=%async_computation.3 | async-start | bytes 2097152 | tf_op jit(solution)/shard_map/all_to_all | solution.py:993
  99.0 26.6 %collective-permute-start.6 = (bf16[2,128,1024]{2,1,0:T(8,128)(2,1)}, bf16[2,128,1024]{2,1,0:T(8,128)(2,1)}, u32[]{:S(2)}, u32[]{:S(2)}) collective-permute-start(bf16[2,128,1024]{2,1,0:T(8,128)(2,1)} %get-tuple-element.106), channel_id=1, source_target_pairs={{0,2},{1,3},{2,0},{3,1},{4,6},{5,7},{6,4},{7,5},{8,10},{9,11},{10,... | collective-permute-start | bytes 1572872 | tf_op jit(solution)/shard_map/ppermute | solution.py:996
  106.3 16.1 %collective-permute-start.3 = (bf16[2,128,1024]{2,1,0:T(8,128)(2,1)}, bf16[2,128,1024]{2,1,0:T(8,128)(2,1)}, u32[]{:S(2)}, u32[]{:S(2)}) collective-permute-start(bf16[2,128,1024]{2,1,0:T(8,128)(2,1)} %get-tuple-element.103), channel_id=1, source_target_pairs={{0,8},{4,12},{8,0},{12,4},{16,24},{20,28},{24,16},{28,20},{1,9},{5... | collective-permute-start | bytes 1572872 | tf_op jit(solution)/shard_map/ppermute | solution.py:958
  108.0 15.3 %collective-permute-start.4 = (bf16[2,128,1024]{2,1,0:T(8,128)(2,1)}, bf16[2,128,1024]{2,1,0:T(8,128)(2,1)}, u32[]{:S(2)}, u32[]{:S(2)}) collective-permute-start(bf16[2,128,1024]{2,1,0:T(8,128)(2,1)} %get-tuple-element.104), channel_id=1, source_target_pairs={{0,16},{4,20},{8,24},{12,28},{16,0},{20,4},{24,8},{28,12},{1,17},{... | collective-permute-start | bytes 1572872 | tf_op jit(solution)/shard_map/ppermute | solution.py:958
  109.6 24.9 %collective-permute-start.5 = (bf16[2,128,1024]{2,1,0:T(8,128)(2,1)}, bf16[2,128,1024]{2,1,0:T(8,128)(2,1)}, u32[]{:S(2)}, u32[]{:S(2)}) collective-permute-start(bf16[2,128,1024]{2,1,0:T(8,128)(2,1)} %get-tuple-element.105), channel_id=1, source_target_pairs={{0,24},{4,28},{8,16},{12,20},{16,8},{20,12},{24,0},{28,4},{1,25},{... | collective-permute-start | bytes 1572872 | tf_op jit(solution)/shard_map/ppermute | solution.py:958
  112.1 7.3 %copy-start.8 = (f32[1,1024]{1,0:T(1,128)S(1)}, f32[1,1024]{1,0:T(1,128)}, u32[]{:S(2)}) copy-start(f32[1,1024]{1,0:T(1,128)} %get-tuple-element.84.refs_5_) | copy-start | bytes 12292
  112.1 7.3 %copy-start.9 = (f32[1,1024]{1,0:T(1,128)S(1)}, f32[1,1024]{1,0:T(1,128)}, u32[]{:S(2)}) copy-start(f32[1,1024]{1,0:T(1,128)} %get-tuple-element.98) | copy-start | bytes 12292
  112.1 8.0 %copy-start.6 = (bf16[1,1024]{1,0:T(2,128)(2,1)S(1)}, bf16[1,1024]{1,0:T(2,128)(2,1)}, u32[]{:S(2)}) copy-start(bf16[1,1024]{1,0:T(2,128)(2,1)} %get-tuple-element.136) | copy-start | bytes 6148
  112.1 8.0 %copy-start.7 = (bf16[1,1024]{1,0:T(2,128)(2,1)S(1)}, bf16[1,1024]{1,0:T(2,128)(2,1)}, u32[]{:S(2)}) copy-start(bf16[1,1024]{1,0:T(2,128)(2,1)} %get-tuple-element.137) | copy-start | bytes 6148
  119.0 40.2 %collective-permute-start.2 = (bf16[2,2,128,1024]{3,2,1,0:T(8,128)(2,1)}, bf16[2,2,128,1024]{3,2,1,0:T(8,128)(2,1)}, u32[]{:S(2)}, u32[]{:S(2)}) collective-permute-start(bf16[2,2,128,1024]{3,2,1,0:T(8,128)(2,1)} %get-tuple-element.95), channel_id=1, source_target_pairs={{0,1},{1,0},{2,3},{3,2},{4,5},{5,4},{6,7},{7,6},{8,9},{9,8},{10,11... | collective-permute-start | bytes 3145736 | tf_op jit(solution)/shard_map/ppermute | solution.py:996
  122.4 3.2 %copy-start.1 = (s32[2]{0:T(128)S(1)}, s32[2]{0:T(128)}, u32[]{:S(2)}) copy-start(s32[2]{0:T(128)} %copy-done) | copy-start | bytes 28
  129.2 43.9 %collective-permute-start.8 = (bf16[2,128,1024]{2,1,0:T(8,128)(2,1)}, bf16[2,128,1024]{2,1,0:T(8,128)(2,1)}, u32[]{:S(2)}, u32[]{:S(2)}) collective-permute-start(bf16[2,128,1024]{2,1,0:T(8,128)(2,1)} %get-tuple-element.112), channel_id=1, source_target_pairs={{0,2},{1,3},{2,0},{3,1},{4,6},{5,7},{6,4},{7,5},{8,10},{9,11},{10,... | collective-permute-start | bytes 1572872 | tf_op jit(solution)/shard_map/ppermute | solution.py:996
  138.3 30.4 %all-to-all-start.4 = ((bf16[4,2,128,1024]{3,2,1,0:T(8,128)(2,1)}), bf16[4,2,128,1024]{3,2,1,0:T(8,128)(2,1)}, u32[]{:S(2)}, u32[]{:S(2)}) async-start(bf16[4,2,128,1024]{3,2,1,0:T(8,128)(2,1)} %get-tuple-element.113), calls=%async_computation.4 | async-start | bytes 4194304 | tf_op jit(solution)/shard_map/all_to_all | solution.py:1025
  150.6 14.5 %collective-permute-start.9 = (bf16[1,768,1024]{2,1,0:T(8,128)(2,1)}, bf16[1,768,1024]{2,1,0:T(8,128)(2,1)}, u32[]{:S(2)}, u32[]{:S(2)}) collective-permute-start(bf16[1,768,1024]{2,1,0:T(8,128)(2,1)} %get-tuple-element.114), channel_id=1, source_target_pairs={{0,4},{4,0},{8,12},{12,8},{16,20},{20,16},{24,28},{28,24},{1,5},{5... | collective-permute-start | bytes 4718600 | tf_op jit(solution)/shard_map/ppermute | solution.py:958
  161.8 46.1 %collective-permute-start.14 = (bf16[2,128,1024]{2,1,0:T(8,128)(2,1)}, bf16[2,128,1024]{2,1,0:T(8,128)(2,1)}, u32[]{:S(2)}, u32[]{:S(2)}) collective-permute-start(bf16[2,128,1024]{2,1,0:T(8,128)(2,1)} %lambda.24), channel_id=1, source_target_pairs={{0,1},{1,0},{2,3},{3,2},{4,5},{5,4},{6,7},{7,6},{8,9},{9,8},{10,11... | collective-permute-start | bytes 1572872 | tf_op jit(solution)/shard_map/ppermute | solution.py:996
  161.8 26.3 %collective-permute-start.7 = (bf16[2,128,1024]{2,1,0:T(8,128)(2,1)}, bf16[2,128,1024]{2,1,0:T(8,128)(2,1)}, u32[]{:S(2)}, u32[]{:S(2)}) collective-permute-start(bf16[2,128,1024]{2,1,0:T(8,128)(2,1)} %get-tuple-element.111), channel_id=1, source_target_pairs={{0,2},{1,3},{2,0},{3,1},{4,6},{5,7},{6,4},{7,5},{8,10},{9,11},{10,... | collective-permute-start | bytes 1572872 | tf_op jit(solution)/shard_map/ppermute | solution.py:996
  168.7 26.2 %collective-permute-start.11 = (bf16[4,2,128,1024]{3,2,1,0:T(8,128)(2,1)}, bf16[4,2,128,1024]{3,2,1,0:T(8,128)(2,1)}, u32[]{:S(2)}, u32[]{:S(2)}) collective-permute-start(bf16[4,2,128,1024]{3,2,1,0:T(8,128)(2,1)} %lambda.20.refs_1_), channel_id=1, source_target_pairs={{0,4},{4,0},{8,12},{12,8},{16,20},{20,16},{24,28},{28,24},{1,5},{5... | collective-permute-start | bytes 6291464 | tf_op jit(solution)/shard_map/ppermute | solution.py:958
  168.8 31.2 %all-to-all-start.5 = ((bf16[4,1,144,1024]{3,2,1,0:T(8,128)(2,1)}), bf16[4,1,144,1024]{3,2,1,0:T(8,128)(2,1)}, u32[]{:S(2)}, u32[]{:S(2)}) async-start(bf16[4,1,144,1024]{3,2,1,0:T(8,128)(2,1)} %lambda.22), calls=%async_computation.5 | async-start | bytes 2359296 | tf_op jit(solution)/shard_map/all_to_all | solution.py:1025
  173.1 15.0 %copy-start.2 = (s32[2]{0:T(128)S(1)}, s32[2]{0:T(128)}, u32[]{:S(2)}) copy-start(s32[2]{0:T(128)} %copy-done) | copy-start | bytes 28
  173.2 34.8 %collective-permute-start.15 = (bf16[2,128,1024]{2,1,0:T(8,128)(2,1)}, bf16[2,128,1024]{2,1,0:T(8,128)(2,1)}, u32[]{:S(2)}, u32[]{:S(2)}) collective-permute-start(bf16[2,128,1024]{2,1,0:T(8,128)(2,1)} %lambda.21.refs_6_.refs_3_), channel_id=1, source_target_pairs={{0,1},{1,0},{2,3},{3,2},{4,5},{5,4},{6,7},{7,6},{8,9},{9,8},{10,11... | collective-permute-start | bytes 1572872 | tf_op jit(solution)/shard_map/ppermute | solution.py:996
  191.6 23.6 %collective-permute-start.13 = (bf16[2,128,1024]{2,1,0:T(8,128)(2,1)}, bf16[2,128,1024]{2,1,0:T(8,128)(2,1)}, u32[]{:S(2)}, u32[]{:S(2)}) collective-permute-start(bf16[2,128,1024]{2,1,0:T(8,128)(2,1)} %get-tuple-element.116.refs_1_), channel_id=1, source_target_pairs={{0,2},{1,3},{2,0},{3,1},{4,6},{5,7},{6,4},{7,5},{8,10},{9,11},{10,... | collective-permute-start | bytes 1572872 | tf_op jit(solution)/shard_map/ppermute | solution.py:996
  192.5 38.5 %collective-permute-start.10 = (bf16[2,128,1024]{2,1,0:T(8,128)(2,1)}, bf16[2,128,1024]{2,1,0:T(8,128)(2,1)}, u32[]{:S(2)}, u32[]{:S(2)}) collective-permute-start(bf16[2,128,1024]{2,1,0:T(8,128)(2,1)} %get-tuple-element.117.refs_1_.refs_3_), channel_id=1, source_target_pairs={{0,1},{1,0},{2,3},{3,2},{4,5},{5,4},{6,7},{7,6},{8,9},{9,8},{10,11... | collective-permute-start | bytes 1572872 | tf_op jit(solution)/shard_map/ppermute | solution.py:996
  202.3 18.3 %all-to-all-start.6 = ((bf16[4,1,144,1024]{3,2,1,0:T(8,128)(2,1)}), bf16[4,1,144,1024]{3,2,1,0:T(8,128)(2,1)}, u32[]{:S(2)}, u32[]{:S(2)}) async-start(bf16[4,1,144,1024]{3,2,1,0:T(8,128)(2,1)} %get-tuple-element.120), calls=%async_computation.6 | async-start | bytes 2359296 | tf_op jit(solution)/shard_map/all_to_all | solution.py:1025
  207.3 0.6 copy-start.5
  208.0 14.1 %collective-permute-start.12 = (f32[2,1024]{1,0:T(2,128)}, f32[2,1024]{1,0:T(2,128)}, u32[]{:S(2)}, u32[]{:S(2)}) collective-permute-start(f32[2,1024]{1,0:T(2,128)} %slice_bitcast_fusion), channel_id=1, source_target_pairs={{0,1},{1,0},{2,3},{3,2},{4,5},{5,4},{6,7},{7,6},{8,9},{9,8},{10,11... | collective-permute-start | bytes 24584 | tf_op jit(solution)/shard_map/ppermute | solution.py:996
  208.0 0.6 copy-start.3
  215.2 17.3 %collective-permute-start.18 = (bf16[2,128,1024]{2,1,0:T(8,128)(2,1)}, bf16[2,128,1024]{2,1,0:T(8,128)(2,1)}, u32[]{:S(2)}, u32[]{:S(2)}) collective-permute-start(bf16[2,128,1024]{2,1,0:T(8,128)(2,1)} %lambda.27.refs_1_.refs_3_), channel_id=1, source_target_pairs={{0,1},{1,0},{2,3},{3,2},{4,5},{5,4},{6,7},{7,6},{8,9},{9,8},{10,11... | collective-permute-start | bytes 1572872 | tf_op jit(solution)/shard_map/ppermute | solution.py:996
  220.6 4.1 %collective-permute-start.17 = (bf16[4,1,144,1024]{3,2,1,0:T(8,128)(2,1)}, bf16[4,1,144,1024]{3,2,1,0:T(8,128)(2,1)S(1)}, u32[]{:S(2)}, u32[]{:S(2)}) collective-permute-start(bf16[4,1,144,1024]{3,2,1,0:T(8,128)(2,1)} %lambda.29.refs_1_), channel_id=1, source_target_pairs={{0,4},{4,0},{8,12},{12,8},{16,20},{20,16},{24,28},{28,24},{1,5},{5... | collective-permute-start | bytes 3538952 | tf_op jit(solution)/shard_map/ppermute | solution.py:958
  223.4 6.9 %collective-permute-start.16 = (f32[2,1024]{1,0:T(2,128)}, f32[2,1024]{1,0:T(2,128)}, u32[]{:S(2)}, u32[]{:S(2)}) collective-permute-start(f32[2,1024]{1,0:T(2,128)} %fusion), channel_id=1, source_target_pairs={{0,2},{1,3},{2,0},{3,1},{4,6},{5,7},{6,4},{7,5},{8,10},{9,11},{10,... | collective-permute-start | bytes 24584 | tf_op jit(solution)/shard_map/ppermute | solution.py:996
  231.7 0.9 copy-start.4

commit v2 on v1

--- a/solution.py
+++ b/solution.py
@@ -123,6 +123,40 @@
     )
 
 
+def gathered_kernel(shard_ref, *refs, parts, **sizes):
+    x_ref = refs[parts + 1]
+    rows = refs[0].shape[1]
+    for k in range(parts):
+        x_ref[0, pl.ds((shard_ref[0] ^ k) * rows, rows)] = refs[k][0]
+    attention_kernel(x_ref, refs[parts], *refs[parts + 2 :], **sizes)
+
+
+def attention_of(shard, same, other, after=()):
+    _, rows, width = same[0].shape
+    length, hd = 2 * rows * len(same), width // 4
+    tq = 512 if length % 512 == 0 else 256
+    specs = [pl.BlockSpec((1, rows, width), lambda i, _, side=side: (side, 0, 0)) for side in (0, 1)]
+    return call(
+        partial(gathered_kernel, parts=2 * len(same), length=length, hd=hd, tq=tq, tk=512),
+        (1,),
+        tuple(v for pair in zip(same, other) for v in pair),
+        specs * len(same),
+        pl.BlockSpec((1, length, width), lambda i, _: (0, 0, 0)),
+        shape_of(1, length, width),
+        7,
+        after,
+        (shard,),
+        [
+            pltpu.VMEM((1, length, width), bf16),
+            pltpu.VMEM((width, length), bf16),
+            pltpu.VMEM((length, 2 * hd), f32),
+            pltpu.VMEM((length, tq), f32),
+        ],
+        vmem=32,
+        free_out=(0,),
+    )
+
+
 def ring_attention(q, k, v, a):
     seq_count, row_count, inner_width = q.shape
     score_scale = HEAD_DIM ** (-0.5)
@@ -397,8 +431,12 @@
     return cosine, jnp.where(even, -sine, 0.0), jnp.where(even, 0.0, sine)
 
 
-def pre_kernel(shard_ref, x_ref, g_ref, gain, bias, wq, wk, wv, wo, cosine, sine, *rest):
-    normed_ref, packed_ref = rest[-2:]
+def pre_kernel(shard_ref, x_ref, g_ref, gain, bias, wq, wk, wv, wo, cosine, sine, *rest, partners):
+    if partners:
+        normed_ref, packed_ref = rest[-2 - partners], rest[-1]
+        outs = rest[-1 - partners : -1]
+    else:
+        normed_ref, packed_ref = rest[-2:]
     unit, _ = unit_rows(x_ref[0].astype(f32))
     normed = (unit * gain[...] + bias[...]).astype(bf16)
     normed_ref[...] = normed
@@ -413,9 +451,17 @@
             head = tile * 2 + side
             packed_ref[head, :, 0:128] = half_swap(qt, kt, lane, side == 0).astype(bf16)
             packed_ref[head, :, 128:256] = half_swap(v[:, cols], a[:, cols], lane, side == 0).astype(bf16)
-
-
-def pre(c, count, shard, x, g, consts, tables, before):
+    for k in range(partners):
+        for side in range(2):
+            pair = shard_ref[0] ^ (2 * k + side)
+            heads = packed_ref.shape[0]
+
+            @pl.when(pair // heads == pl.program_id(0))
+            def _():
+                outs[k][side] = packed_ref[pair % heads]
+
+
+def pre(c, count, shard, x, g, consts, tables, before, partners=0):
     seqs, rows, width = x.shape
     heads = consts[2].shape[1] // HEAD_DIM
     by_seq = pl.BlockSpec((1, rows, width), lambda i, _: (c * count + i, 0, 0))
@@ -424,20 +470,28 @@
     if before is not None:
         alias = {len(ins): 0}
         ins, specs = ins + (before,), specs + [anywhere]
-    return call(
-        pre_kernel,
+    blocks = pl.BlockSpec((heads, rows, 4 * HEAD_DIM), lambda i, _: (i, 0, 0))
+    shapes = [shape_of(count * heads, rows, 4 * HEAD_DIM)]
+    scratch = []
+    if partners:
+        shapes = [shape_of(2, rows, 4 * HEAD_DIM)] * partners
+        scratch = [pltpu.VMEM((heads, rows, 4 * HEAD_DIM), bf16)]
+        blocks = pl.BlockSpec((2, rows, 4 * HEAD_DIM), lambda i, _: (0, 0, 0))
+    return call(
+        partial(pre_kernel, partners=partners),
         (count,),
         ins,
         specs,
         [
             pl.BlockSpec((rows, width), lambda i, _: (c * count + i, 0)),
-            pl.BlockSpec((heads, rows, 4 * HEAD_DIM), lambda i, _: (i, 0, 0)),
-        ],
-        [shape_of(seqs * rows, width), shape_of(count * heads, rows, 4 * HEAD_DIM)],
+        ]
+        + [blocks] * len(shapes),
+        [shape_of(seqs * rows, width)] + shapes,
         3,
         scalars=(shard,),
         alias=alias,
-        free_out=(1,),
+        scratch=scratch,
+        free_out=range(1, 1 + len(shapes)),
     )
 
 
@@ -998,74 +1052,80 @@
     dense_args = (flat_cot, w_in, b_in, w_mlp_out)
     normed, packed_a = pre(0, count, place, x, cot, pre_consts, tables, None)
     sent_a = traded(packed_a)
-    normed, packed_b = pre(1, count, place, x, cot, pre_consts, tables, normed)
-    hidden, dgate, part_a, dn_a, db_in_a, db_out_a = mlp(0, count, rows, normed, *dense_args, None, (packed_b,))
+    normed, *packed_b = pre(1, count, place, x, cot, pre_consts, tables, normed, chips)
+    hidden, dgate, part_a, dn_a, db_in_a, db_out_a = mlp(0, count, rows, normed, *dense_args, None, (normed,))
     done_a = attend(sent_a, (db_in_a,))
     back_a = traded(done_a)
     hidden, dgate, part_b, dn_b, db_in_b, db_out_b = mlp(1, count, rows, normed, *dense_args, (hidden, dgate), (done_a,))
-    sent_b = traded(fence(packed_b, back_a, db_in_b))
+    packed_b = [fence(v, db_in_b) for v in packed_b]
+    same = [packed_b[0]] + [exchanged(packed_b[k], 2 * k) for k in (1, 2, 3)]
+    beside = exchanged(packed_b[0], 1)
     give_a, keep_a, flat, gain_a, bias_a = post(
         0, count, place, back_a, x, part_a, dn_a, post_consts, tables, None, (db_in_b,)
     )
+    same = [same[0]] + [fence(v, gain_a) for v in same[1:]]
     got_a = over_line(give_a, 1)
-    give_e, keep_e = dense_grads(core, normed, dgate, hidden, flat_cot, (gain_a,))
+    other = [beside] + [exchanged(v, 1) for v in same[1:]]
+    done_b = attention_of(shard.reshape(1), same, other, (gain_a,))
+    done_b = done_b.reshape(shards, rows, 4 * HEAD_DIM)
+    back_b = traded(done_b)
+    give_e, keep_e = dense_grads(core, normed, dgate, hidden, flat_cot, (done_b,))
     got_e = exchanged(give_e, 1)
-    done_b = attend(sent_b, (keep_e,))
-    back_b = traded(done_b)
-    own_a, other_a = pair_sum(keep_a, got_a, (done_b,))
-    *dense, token = parted(chip, keep_e, got_e, chips, (own_a,))
-    dense = [dense[0]] + [exchanged(dense[k], 2 * k) for k in range(1, chips)]
+    own_a, other_a = pair_sum(keep_a, got_a, (keep_e,))
     got_a = over_line(other_a, 2)
     give_b, keep_b, flat, gain_b, bias_b = post(
-        1, count, place, back_b, x, part_b, dn_b, post_consts, tables, flat, (token,)
+        1, count, place, back_b, x, part_b, dn_b, post_consts, tables, flat, (own_a,)
     )
 
     def over_chips(v):
         same_core = [list(range(side, shards, 2)) for side in (0, 1)]
         return lax.all_to_all(v, "seq", 0, 0, axis_index_groups=same_core, tiled=True)
 
-    dense[1] = fence(dense[1], gain_b)
-    dense[2] = fence(dense[2], dense[1])
-    done_a, more_a, again_a = own_quarter(place, 0, x, cot, own_a, got_a, gain, 3, (dense[2],))
-    dense, token = joined(dense, (more_a,))
-    dense = over_chips(dense)
+    *dense, token = parted(chip, keep_e, got_e, chips, (gain_b,))
+    dense = [dense[0]] + [exchanged(dense[k], 2 * k) for k in range(1, chips)]
     small = jnp.concatenate([gain_a + gain_b, bias_a + bias_b, db_in_a + db_in_b, db_out_a + db_out_b], 0)
     small = jnp.concatenate([small, jnp.zeros((12, width), f32)], 0).astype(bf16)
     give_l, keep_l = head_grads(core, normed, flat_cot, flat, small, (token,))
+    got_l = exchanged(give_l, 1)
+    done_a, more_a, again_a = own_quarter(place, 0, x, cot, own_a, got_a, gain, 3, (keep_l,))
+    got_l = fence(got_l, more_a)
+    head, token = split(keep_l, got_l, small, chips, (more_a,))
+    head = over_chips(head)
     far_a = over_line(done_a, 2)
     got_b = over_line(give_b, 1)
-    own_b, other_b = pair_sum(keep_b, got_b, (keep_l,))
+    own_b, other_b = pair_sum(keep_b, got_b, (token,))
     near_a = over_line(fence(again_a, own_b), 1)
     got_b = over_line(other_b, 2)
-    got_l = exchanged(give_l, 1)
-    head, token = split(keep_l, got_l, small, chips, (own_b,))
-    dense = fence(dense, token)
-    head = over_chips(fence(head, dense))
-    dense_other = exchanged(dense, 1)
-    far_a = fence(far_a, dense)
+    dense[1] = fence(dense[1], own_b)
+    dense[2] = fence(dense[2], dense[1])
+    dense, token = joined(dense, (dense[2],))
+    head, token = total(head, chips, (token,))
+    dense = over_chips(fence(dense, token))
+    far_a = fence(far_a, token)
     beside_a = over_line(far_a, 1)
     done_b, more_b = own_quarter(place, count, x, cot, own_b, got_b, gain, 2, (far_a,))
-    dense_other = fence(dense_other, done_b)
-    d_in, d_out = dense_outs(jnp.concatenate([core, jnp.zeros_like(core)]), dense, dense_other, width, (done_b,))
-    head, token = total(head, chips, (d_out,))
     near_b = over_line(done_b, 1)
     far_b = over_line(more_b, 2)
     small = head[0, 0, -small.shape[0] :].astype(f32)
-    vectors = small[:2]
+    dense = fence(dense, done_b)
+    vectors = fence(small[:2], dense)
+    head = over_chips(fence(head, dense))
+    dense_other = exchanged(dense, 1)
+    near_a = fence(near_a, dense)
     vectors_got = over_line(vectors, 1)
-    head = over_chips(head)
-    near_a = fence(near_a, token)
     beside_a = fence(beside_a, near_a)
     d_tokens, mixed = placed(place, x.shape, 0, (more_a, near_a, far_a, beside_a), None, (beside_a,))
     far_b = fence(far_b, d_tokens)
     beside_b = over_line(far_b, 1)
-    vectors = vectors + fence(vectors_got, far_b)
+    dense_other = fence(dense_other, far_b)
+    d_in, d_out = dense_outs(jnp.concatenate([core, jnp.zeros_like(core)]), dense, dense_other, width, (far_b,))
+    vectors = vectors + fence(vectors_got, d_out)
     vectors_got = over_line(vectors, 2)
-    head = fence(head, far_b)
+    head = fence(head, d_out)
     head_other = exchanged(head, 1)
-    head_other = fence(head_other, far_b)
+    head_other = fence(head_other, d_out)
     d_attn_out, d_query, d_key, d_value = head_outs(
-        jnp.concatenate([core, jnp.zeros_like(core)]), head, head_other, width, (far_b,)
+        jnp.concatenate([core, jnp.zeros_like(core)]), head, head_other, width, (d_out,)
     )
     vectors = vectors + fence(vectors_got, d_value)
     near_b = fence(near_b, vectors)

time: 238 us -> 234 us (0.983)
  waiting for transfers between devices: 51.3 us -> 47.4 us
    all_to_all x3, waiting for transfers between devices: 2.28 us -> 16.6 us  [over_chips(): lax.all_to_all(v, 'seq', 0, 0, axis_index_groups=same_core, tiled=True)]
    ppermute x12, waiting for transfers between devices: 33.5 us -> 24.4 us  [over_line(): return lax.ppermute(v, 'mlp', [(i, i ^ bits) for i in range(4)])]
    ppermute x7 -> x14, waiting for transfers between devices: 8.18 us -> 3.43 us  [exchanged(): lax.ppermute(x, 'seq', [(i, i ^ bits) for i in range(lax.axis_size('seq'))])]
    all_to_all x4 -> x3, waiting for transfers between devices: 7.35 us -> 3.01 us  [traded(): return lax.all_to_all(v, 'seq', 0, 0, tiled=True)]
    all_to_all x4 -> x3, starting transfers between devices: 18.3 us -> 14 us  [traded(): return lax.all_to_all(v, 'seq', 0, 0, tiled=True)]
    ppermute x7 -> x14, starting transfers between devices: 3.63 us -> 7.86 us  [exchanged(): lax.ppermute(x, 'seq', [(i, i ^ bits) for i in range(lax.axis_size('seq'))])]
    pallas_call x39 -> x48, Pallas kernels: 124 us -> 125 us  [call(): pl.pallas_call(body, name=getattr(kernel, 'func', kernel).__name__.strip(...]
  transfers between devices with their start and end apart: 26 -> 32, of which waited for: 14 -> 10; matrix products, arithmetic and copies ran while one was open for 3% -> 3% of each run, Pallas kernels for 44% -> 45%
where the time goes in v2:
time: 234 us; the launch traced here: 233 us
  Pallas kernels  125 us (53%)
  starting transfers between devices  51.6 us (22%)
  waiting for transfers between devices  47.4 us (20%)
  other arithmetic  4.28 us (2%)
  local copies, waits for them, and re-layouts  3.27 us (1%)
    pallas_call x48, Pallas kernels, call(): pl.pallas_call(body, name=getattr(kernel, 'func', kernel).__name__.strip(...  125 us
    ppermute x12, waiting for transfers between devices, over_line(): return lax.ppermute(v, 'mlp', [(i, i ^ bits) for i in range(4)])  24.4 us
    ppermute x12, starting transfers between devices, over_line(): return lax.ppermute(v, 'mlp', [(i, i ^ bits) for i in range(4)])  16.7 us
    all_to_all x3, waiting for transfers between devices, over_chips(): lax.all_to_all(v, 'seq', 0, 0, axis_index_groups=same_core, tiled=True)  16.6 us
    all_to_all x3, starting transfers between devices, traded(): return lax.all_to_all(v, 'seq', 0, 0, tiled=True)  14 us
    all_to_all x3, starting transfers between devices, over_chips(): lax.all_to_all(v, 'seq', 0, 0, axis_index_groups=same_core, tiled=True)  13 us
    ppermute x14, starting transfers between devices, exchanged(): lax.ppermute(x, 'seq', [(i, i ^ bits) for i in range(lax.axis_size('seq'))])  7.86 us
  transfers between devices with their start and end apart: 32, of which 10 were waited for; matrix products, arithmetic and copies ran while one was open for 3% of the time, Pallas kernels for 45%

profile of v2, /device:TPU:0, one launch (start us, length us, event | category | flops | bytes accessed | tf_op | source)
XLA Modules:
  0.0 232.9 jit_solution(15913201094887222330)
XLA Ops:
  0.7 5.6 %pre_kernel.2 = (bf16[1024,1024]{1,0:T(8,128)(2,1)}, bf16[8,256,256]{2,1,0:T(8,128)(2,1)}) custom-call(s32[2]{0:T(128)S(1)} %pad_add_fusion.refs_0_, bf16[4,256,1024]{2,1,0:T(8,128)(2,1)} %bitcast.26, bf16[4,256,1024]{2,1,0:T(8,128)(2,1)} %bitcast.32, f32[1,1024]{1,0:T(1,128)} %bitcast.46, f32[1,1024]{1,0:T(1,128)} %bitcast.40, bf16[1024,256]{1,0:T(8,128)(2,1)} %refs_6_.7, ...), custom_call_target="tpu_custom_call" | custom-call | flops 299999985664 | tf_op jit(solution)/shard_map/pre_kernel/pallas_call | solution.py:341
  6.4 5.2 %all-to-all-start = ((bf16[8,256,256]{2,1,0:T(8,128)(2,1)}), bf16[8,256,256]{2,1,0:T(8,128)(2,1)}, u32[]{:S(2)}, u32[]{:S(2)}) async-start(bf16[8,256,256]{2,1,0:T(8,128)(2,1)} %get-tuple-element.80), calls=%async_computation | async-start | bytes 2097152 | tf_op jit(solution)/shard_map/all_to_all | solution.py:1047
  11.5 6.3 %pre_kernel.3 = (bf16[1024,1024]{1,0:T(8,128)(2,1)}, bf16[2,256,256]{2,1,0:T(8,128)(2,1)}, bf16[2,256,256]{2,1,0:T(8,128)(2,1)}, bf16[2,256,256]{2,1,0:T(8,128)(2,1)}, bf16[2,256,256]{2,1,0:T(8,128)(2,1)}) custom-call(s32[2]{0:T(128)S(1)} %pad_add_fusion.refs_0_, bf16[4,256,1024]{2,1,0:T(8,128)(2,1)} %bitcast.27, ...), custom_call_target="tpu_custom_call", output_to_operand_aliasing={{0}: (11, {})} | custom-call | flops 299999985664 | tf_op jit(solution)/shard_map/pre_kernel/pallas_call | solution.py:341
  17.8 9.3 %mlp_kernel.2 = (bf16[1024,1024]{1,0:T(8,128)(2,1)}, bf16[1024,1024]{1,0:T(8,128)(2,1)}, bf16[512,1024]{1,0:T(8,128)(2,1)}, bf16[512,1024]{1,0:T(8,128)(2,1)}, f32[1,1024]{1,0:T(1,128)}, /*index=5*/f32[1,1024]{1,0:T(1,128)}) custom-call(bf16[1024,1024]{1,0:T(8,128)(2,1)} %get-tuple-element.77.refs_0_.refs_5_.refs_1_, bf16[1024,1024]{1,0:T(8,128)(2,1)} %bitcast.34, ...), custom_call_target="tpu_custom_call" | custom-call | flops 499999997952 | tf_op jit(solution)/shard_map/mlp_kernel/pallas_call | solution.py:341
  27.1 11.0 %attention_kernel.1 = bf16[1,2048,256]{2,1,0:T(8,128)(2,1)} custom-call(bf16[1,2048,256]{2,1,0:T(8,128)(2,1)} %bitcast.8.refs_0_, f32[1,1024]{1,0:T(1,128)} %get-tuple-element.81.refs_1_), custom_call_target="tpu_custom_call" | custom-call | flops 699999977472 | tf_op jit(solution)/shard_map/attention_kernel/pallas_call | solution.py:341
  38.1 4.4 %all-to-all-start.1 = ((bf16[8,256,256]{2,1,0:T(8,128)(2,1)}), bf16[8,256,256]{2,1,0:T(8,128)(2,1)}, u32[]{:S(2)}, u32[]{:S(2)}) async-start(bf16[8,256,256]{2,1,0:T(8,128)(2,1)} %bitcast.9.refs_7_), calls=%async_computation.1 | async-start | bytes 2097152 | tf_op jit(solution)/shard_map/all_to_all | solution.py:1047
  42.5 9.3 %mlp_kernel.3 = (bf16[1024,1024]{1,0:T(8,128)(2,1)}, bf16[1024,1024]{1,0:T(8,128)(2,1)}, bf16[512,1024]{1,0:T(8,128)(2,1)}, bf16[512,1024]{1,0:T(8,128)(2,1)}, f32[1,1024]{1,0:T(1,128)}, /*index=5*/f32[1,1024]{1,0:T(1,128)}) custom-call(bf16[1024,1024]{1,0:T(8,128)(2,1)} %get-tuple-element.77.refs_0_.refs_5_.refs_1_, ...), custom_call_target="tpu_custom_call", output_to_operand_aliasing={{0}: (5, {}), {1}: (6, {})} | custom-call | flops 499999997952 | tf_op jit(solution)/shard_map/mlp_kernel/pallas_call | solution.py:341
  51.9 2.1 collective-permute-start.1
  54.0 1.5 collective-permute-start.3
  55.5 2.9 %all-to-all-done.1.refs_1_ = bf16[8,256,256]{2,1,0:T(8,128)(2,1)} async-done(((bf16[8,256,256]{2,1,0:T(8,128)(2,1)}), bf16[8,256,256]{2,1,0:T(8,128)(2,1)}, u32[]{:S(2)}, u32[]{:S(2)}) %all-to-all-start.1) | async-done | bytes 1048608 | tf_op jit(solution)/shard_map/all_to_all | solution.py:1047
  58.4 7.0 %post_kernel.2 = (bf16[2,2,128,1024]{3,2,1,0:T(8,128)(2,1)}, bf16[2,2,128,1024]{3,2,1,0:T(8,128)(2,1)}, bf16[1024,1024]{1,0:T(8,128)(2,1)}, f32[1,1024]{1,0:T(1,128)}, f32[1,1024]{1,0:T(1,128)}) custom-call(s32[2]{0:T(128)S(1)} %pad_add_fusion.refs_0_, bf16[8,256,256]{2,1,0:T(8,128)(2,1)} %all-to-all-done.1.refs_1_, bf16[4,256,1024]{2,1,0:T(8,128)(2,1)} %bitcast.28, ...), custom_call_target="tpu_custom_call" | custom-call | flops 399999991808 | tf_op jit(solution)/shard_map/post_kernel/pallas_call | solution.py:341
  65.6 0.5 collective-permute-start.4
  66.2 3.0 %collective-permute-done.5.refs_0_ = bf16[2,256,256]{2,1,0:T(8,128)(2,1)} collective-permute-done((bf16[2,256,256]{2,1,0:T(8,128)(2,1)}, bf16[2,256,256]{2,1,0:T(8,128)(2,1)}, u32[]{:S(2)}, u32[]{:S(2)}) %collective-permute-start.5) | collective-permute-done | bytes 262176 | tf_op jit(solution)/shard_map/ppermute | solution.py:1012
  69.3 0.6 add_convert_fusion
  69.9 2.0 collective-permute-start.7
  71.9 11.1 %gathered_kernel.1 = bf16[1,2048,256]{2,1,0:T(8,128)(2,1)} custom-call(s32[1]{0:T(128)} %bitcast.refs_0_, bf16[2,256,256]{2,1,0:T(8,128)(2,1)} %lambda.26.refs_1_, bf16[2,256,256]{2,1,0:T(8,128)(2,1)} %collective-permute-done.refs_2_, bf16[2,256,256]{2,1,0:T(8,128)(2,1)} %lambda.28.refs_3_, bf16[2,256,256]{2,1,0:T(8,128)(2,1)} %collective-permute-done.2.refs_4_, ...), custom_call_target="tpu_custom_call" | custom-call | flops 699999977472 | tf_op jit(solution)/shard_map/gathered_kernel/pallas_call | solution.py:341
  83.0 4.5 %all-to-all-start.2 = ((bf16[8,256,256]{2,1,0:T(8,128)(2,1)}), bf16[8,256,256]{2,1,0:T(8,128)(2,1)}, u32[]{:S(2)}, u32[]{:S(2)}) async-start(bf16[8,256,256]{2,1,0:T(8,128)(2,1)} %bitcast.11.refs_5_), calls=%async_computation.2 | async-start | bytes 2097152 | tf_op jit(solution)/shard_map/all_to_all | solution.py:1047
  87.5 9.7 %dense_grads_kernel.1 = (bf16[2,512,1024]{2,1,0:T(8,128)(2,1)}, bf16[2,512,1024]{2,1,0:T(8,128)(2,1)}) custom-call(s32[1]{0:T(128)} %bitcast.12.refs_0_, bf16[1024,1024]{1,0:T(8,128)(2,1)} %get-tuple-element.77.refs_0_.refs_5_.refs_1_, bf16[1024,1024]{1,0:T(8,128)(2,1)} %get-tuple-element.94.refs_2_, bf16[1024,1024]{1,0:T(8,128)(2,1)} %get-tuple-element.95.refs_3_, ...), custom_call_target="tpu_custom_call" | custom-call | flops 599999971328 | tf_op jit(solution)/shard_map/dense_grads_kernel/pallas_call | solution.py:341
  97.2 0.2 collective-permute-start.9
  97.4 2.6 %pair_sum_kernel.2 = (bf16[2,128,1024]{2,1,0:T(8,128)(2,1)}, bf16[2,128,1024]{2,1,0:T(8,128)(2,1)}) custom-call(bf16[2,2,128,1024]{3,2,1,0:T(8,128)(2,1)} %get-tuple-element.92.refs_0_, bf16[2,2,128,1024]{3,2,1,0:T(8,128)(2,1)} %collective-permute-done.7.refs_1_, bf16[2,512,1024]{2,1,0:T(8,128)(2,1)} %get-tuple-element.96.refs_2_.refs_1_), custom_call_target="tpu_custom_call" | custom-call | flops 99999997952 | tf_op jit(solution)/shard_map/pair_sum_kernel/pallas_call | solution.py:341
  100.0 2.6 %collective-permute-start.11 = (bf16[2,128,1024]{2,1,0:T(8,128)(2,1)}, bf16[2,128,1024]{2,1,0:T(8,128)(2,1)}, u32[]{:S(2)}, u32[]{:S(2)}) collective-permute-start(bf16[2,128,1024]{2,1,0:T(8,128)(2,1)} %get-tuple-element.110), channel_id=1, source_target_pairs={{0,2},{1,3},{2,0},{3,1},{4,6},{5,7},{6,4},{7,5},{8,10},{9,11},{10,... | collective-permute-start | bytes 1572872 | tf_op jit(solution)/shard_map/ppermute | solution.py:1050
  102.7 6.9 %post_kernel.3 = (bf16[2,2,128,1024]{3,2,1,0:T(8,128)(2,1)}, bf16[2,2,128,1024]{3,2,1,0:T(8,128)(2,1)}, bf16[1024,1024]{1,0:T(8,128)(2,1)}, f32[1,1024]{1,0:T(1,128)}, f32[1,1024]{1,0:T(1,128)}) custom-call(s32[2]{0:T(128)S(1)} %copy-done.1, bf16[8,256,256]{2,1,0:T(8,128)(2,1)} %all-to-all-done.2.refs_1_, ...), custom_call_target="tpu_custom_call", output_to_operand_aliasing={{2}: (12, {})} | custom-call | flops 399999991808 | tf_op jit(solution)/shard_map/post_kernel/pallas_call | solution.py:341
  109.6 1.1 collective-permute-start.8
  110.7 0.7 add_convert_fusion.2
  111.4 0.2 concatenate.8.refs_4_.refs_2_
  111.6 4.7 %parted_kernel.1 = (bf16[2,128,1024]{2,1,0:T(8,128)(2,1)}, bf16[2,128,1024]{2,1,0:T(8,128)(2,1)}, bf16[2,128,1024]{2,1,0:T(8,128)(2,1)}, bf16[2,128,1024]{2,1,0:T(8,128)(2,1)}, f32[8,128]{1,0:T(8,128)}) custom-call(s32[1]{0:T(128)} %bitcast.13.refs_0_, bf16[2,512,1024]{2,1,0:T(8,128)(2,1)} %get-tuple-element.96.refs_2_.refs_1_, ...), custom_call_target="tpu_custom_call" | custom-call | flops 199999995904 | tf_op jit(solution)/shard_map/parted_kernel/pallas_call | solution.py:341
  116.4 6.9 %head_grads_kernel.1 = (bf16[1,768,1024]{2,1,0:T(8,128)(2,1)}, bf16[1,512,1024]{2,1,0:T(8,128)(2,1)}) custom-call(s32[1]{0:T(128)} %bitcast.12.refs_0_, bf16[1024,1024]{1,0:T(8,128)(2,1)} %get-tuple-element.77.refs_0_.refs_5_.refs_1_, bf16[1024,1024]{1,0:T(8,128)(2,1)} %bitcast.37, bf16[1024,1024]{1,0:T(8,128)(2,1)} %get-tuple-element.100.refs_3_, ...), custom_call_target="tpu_custom_call" | custom-call | flops 399999991808 | tf_op jit(solution)/shard_map/head_grads_kernel/pallas_call | solution.py:341
  123.3 3.4 %collective-permute-done.11.refs_4_ = bf16[2,128,1024]{2,1,0:T(8,128)(2,1)} collective-permute-done((bf16[2,128,1024]{2,1,0:T(8,128)(2,1)}, bf16[2,128,1024]{2,1,0:T(8,128)(2,1)}, u32[]{:S(2)}, u32[]{:S(2)}) %collective-permute-start.11) | collective-permute-done | bytes 524320 | tf_op jit(solution)/shard_map/ppermute | solution.py:1050
  126.7 3.6 %own_quarter_kernel.2 = (bf16[2,128,1024]{2,1,0:T(8,128)(2,1)}, bf16[2,128,1024]{2,1,0:T(8,128)(2,1)}, bf16[2,128,1024]{2,1,0:T(8,128)(2,1)}) custom-call(s32[2]{0:T(128)S(1)} %copy-done.2, bf16[4,256,1024]{2,1,0:T(8,128)(2,1)} %bitcast.30, bf16[4,256,1024]{2,1,0:T(8,128)(2,1)} %bitcast.38, bf16[2,128,1024]{2,1,0:T(8,128)(2,1)} %get-tuple-element.97.refs_13_.refs_3_, ...), custom_call_target="tpu_custom_call" | custom-call | flops 199999995904 | tf_op jit(solution)/shard_map/own_quarter_kernel/pallas_call | solution.py:341
  130.3 1.7 collective-permute-start.14
  132.0 1.5 collective-permute-start.15
  133.5 0.3 collective-permute-start.16
  133.8 3.7 %split_kernel.1 = (bf16[4,1,144,1024]{3,2,1,0:T(8,128)(2,1)}, f32[8,128]{1,0:T(8,128)}) custom-call(bf16[1,512,1024]{2,1,0:T(8,128)(2,1)} %get-tuple-element.108.refs_6_.refs_0_, bf16[1,768,1024]{2,1,0:T(8,128)(2,1)} %lambda.33.refs_1_.refs_3_, bf16[16,1024]{1,0:T(8,128)(2,1)S(1)} %concatenate.8.refs_4_.refs_2_, ...), custom_call_target="tpu_custom_call" | custom-call | flops 199999995904 | tf_op jit(solution)/shard_map/split_kernel/pallas_call | solution.py:341
  137.5 4.3 %all-to-all-start.3 = ((bf16[4,1,144,1024]{3,2,1,0:T(8,128)(2,1)}), bf16[4,1,144,1024]{3,2,1,0:T(8,128)(2,1)}, u32[]{:S(2)}, u32[]{:S(2)}) async-start(bf16[4,1,144,1024]{3,2,1,0:T(8,128)(2,1)} %get-tuple-element.116), calls=%async_computation.3 | async-start | bytes 2359296 | tf_op jit(solution)/shard_map/all_to_all | solution.py:1082
  141.8 19.8 %collective-permute-done.8.refs_1_ = bf16[2,2,128,1024]{3,2,1,0:T(8,128)(2,1)} collective-permute-done((bf16[2,2,128,1024]{3,2,1,0:T(8,128)(2,1)}, bf16[2,2,128,1024]{3,2,1,0:T(8,128)(2,1)}, u32[]{:S(2)}, u32[]{:S(2)}) %collective-permute-start.8) | collective-permute-done | bytes 1048608 | tf_op jit(solution)/shard_map/ppermute | solution.py:1050
  161.6 2.6 %pair_sum_kernel.3 = (bf16[2,128,1024]{2,1,0:T(8,128)(2,1)}, bf16[2,128,1024]{2,1,0:T(8,128)(2,1)}) custom-call(bf16[2,2,128,1024]{3,2,1,0:T(8,128)(2,1)} %get-tuple-element.98.refs_0_, bf16[2,2,128,1024]{3,2,1,0:T(8,128)(2,1)} %collective-permute-done.8.refs_1_, f32[8,128]{1,0:T(8,128)} %get-tuple-element.112.refs_2_), custom_call_target="tpu_custom_call" | custom-call | flops 99999997952 | tf_op jit(solution)/shard_map/pair_sum_kernel/pallas_call | solution.py:341
  164.4 0.4 collective-permute-done.15.refs_0_
  164.8 3.9 %joined_kernel.1 = (bf16[4,2,128,1024]{3,2,1,0:T(8,128)(2,1)}, f32[8,128]{1,0:T(8,128)}) custom-call(bf16[2,128,1024]{2,1,0:T(8,128)(2,1)} %get-tuple-element.117.refs_0_, bf16[2,128,1024]{2,1,0:T(8,128)(2,1)} %lambda.34.refs_1_, bf16[2,128,1024]{2,1,0:T(8,128)(2,1)} %lambda.35.refs_2_.refs_4_, bf16[2,128,1024]{2,1,0:T(8,128)(2,1)} %collective-permute-done.16.refs_3_, ...), custom_call_target="tpu_custom_call" | custom-call | flops 199999995904 | tf_op jit(solution)/shard_map/joined_kernel/pallas_call | solution.py:341
  168.7 0.7 all-to-all-done.3.refs_0_
  169.3 2.2 total_kernel.1
  171.5 4.5 %all-to-all-start.4 = ((bf16[4,2,128,1024]{3,2,1,0:T(8,128)(2,1)}), bf16[4,2,128,1024]{3,2,1,0:T(8,128)(2,1)}, u32[]{:S(2)}, u32[]{:S(2)}) async-start(bf16[4,2,128,1024]{3,2,1,0:T(8,128)(2,1)} %lambda.37), calls=%async_computation.4 | async-start | bytes 4194304 | tf_op jit(solution)/shard_map/all_to_all | solution.py:1082
  176.0 3.4 %collective-permute-start.22 = (bf16[2,128,1024]{2,1,0:T(8,128)(2,1)}, bf16[2,128,1024]{2,1,0:T(8,128)(2,1)}, u32[]{:S(2)}, u32[]{:S(2)}) collective-permute-start(bf16[2,128,1024]{2,1,0:T(8,128)(2,1)} %lambda.36.refs_6_.refs_3_), channel_id=1, source_target_pairs={{0,1},{1,0},{2,3},{3,2},{4,5},{5,4},{6,7},{7,6},{8,9},{9,8},{10,11... | collective-permute-start | bytes 1572872 | tf_op jit(solution)/shard_map/ppermute | solution.py:1050
  179.4 1.1 collective-permute-done.12.refs_4_
  180.5 3.5 %own_quarter_kernel.3 = (bf16[2,128,1024]{2,1,0:T(8,128)(2,1)}, bf16[2,128,1024]{2,1,0:T(8,128)(2,1)}) custom-call(s32[2]{0:T(128)S(1)} %copy-done.3, bf16[4,256,1024]{2,1,0:T(8,128)(2,1)} %bitcast.31, bf16[4,256,1024]{2,1,0:T(8,128)(2,1)} %bitcast.39, bf16[2,128,1024]{2,1,0:T(8,128)(2,1)} %get-tuple-element.113.refs_1_.refs_3_, ...), custom_call_target="tpu_custom_call" | custom-call | flops 199999995904 | tf_op jit(solution)/shard_map/own_quarter_kernel/pallas_call | solution.py:341
  183.9 0.3 collective-permute-start.20
  184.3 1.7 collective-permute-start.17
  186.0 0.8 slice_convert_fusion
  186.7 0.6 slice_bitcast_fusion.refs_0_
  187.3 0.6 fusion
  187.9 11.8 %all-to-all-done.4.refs_0_ = bf16[4,2,128,1024]{3,2,1,0:T(8,128)(2,1)} async-done(((bf16[4,2,128,1024]{3,2,1,0:T(8,128)(2,1)}), bf16[4,2,128,1024]{3,2,1,0:T(8,128)(2,1)}, u32[]{:S(2)}, u32[]{:S(2)}) %all-to-all-start.4) | async-done | bytes 2097184 | tf_op jit(solution)/shard_map/all_to_all | solution.py:1082
  199.7 4.3 %all-to-all-start.5 = ((bf16[4,1,144,1024]{3,2,1,0:T(8,128)(2,1)}), bf16[4,1,144,1024]{3,2,1,0:T(8,128)(2,1)}, u32[]{:S(2)}, u32[]{:S(2)}) async-start(bf16[4,1,144,1024]{3,2,1,0:T(8,128)(2,1)} %lambda.46), calls=%async_computation.5 | async-start | bytes 2359296 | tf_op jit(solution)/shard_map/all_to_all | solution.py:1082
  204.0 3.1 %collective-permute-start.18 = (f32[2,1024]{1,0:T(2,128)}, f32[2,1024]{1,0:T(2,128)}, u32[]{:S(2)}, u32[]{:S(2)}) collective-permute-start(f32[2,1024]{1,0:T(2,128)} %lambda.39), channel_id=1, source_target_pairs={{0,1},{1,0},{2,3},{3,2},{4,5},{5,4},{6,7},{7,6},{8,9},{9,8},{10,11... | collective-permute-start | bytes 24584 | tf_op jit(solution)/shard_map/ppermute | solution.py:1050
  207.1 0.6 copy-done.4
  207.7 3.0 %placed_kernel.2 = (bf16[4,256,1024]{2,1,0:T(8,128)(2,1)}, bf16[4,256,1024]{2,1,0:T(8,128)(2,1)}) custom-call(s32[2]{0:T(128)S(1)} %copy-done.4, bf16[2,128,1024]{2,1,0:T(8,128)(2,1)} %get-tuple-element.111.refs_1_.refs_4_, bf16[2,128,1024]{2,1,0:T(8,128)(2,1)} %lambda.41.refs_1_.refs_2_, bf16[2,128,1024]{2,1,0:T(8,128)(2,1)} %lambda.36.refs_6_.refs_3_, ...), custom_call_target="tpu_custom_call" | custom-call | flops 199999995904 | tf_op jit(solution)/shard_map/placed_kernel/pallas_call | solution.py:341
  210.7 0.1 collective-permute-start.25
  210.8 5.1 %dense_outs_kernel.1 = (f32[1024,1024]{1,0:T(8,128)}, f32[1024,1024]{1,0:T(8,128)}) custom-call(s32[2]{0:T(128)S(1)} %pad_add_fusion.1.refs_0_, bf16[4,2,128,1024]{3,2,1,0:T(8,128)(2,1)} %lambda.38.refs_1_, bf16[4,2,128,1024]{3,2,1,0:T(8,128)(2,1)} %lambda.44.refs_2_, bf16[2,128,1024]{2,1,0:T(8,128)(2,1)} %lambda.43.refs_1_.refs_3_), custom_call_target="tpu_custom_call" | custom-call | flops 399999991808 | tf_op jit(solution)/shard_map/dense_outs_kernel/pallas_call | solution.py:341
  216.0 4.1 %all-to-all-done.5.refs_0_ = bf16[4,1,144,1024]{3,2,1,0:T(8,128)(2,1)} async-done(((bf16[4,1,144,1024]{3,2,1,0:T(8,128)(2,1)}), bf16[4,1,144,1024]{3,2,1,0:T(8,128)(2,1)}, u32[]{:S(2)}, u32[]{:S(2)}) %all-to-all-start.5) | async-done | bytes 1179680 | tf_op jit(solution)/shard_map/all_to_all | solution.py:1082
  220.1 1.3 add.28
  221.4 2.4 %collective-permute-start.23 = (f32[2,1024]{1,0:T(2,128)}, f32[2,1024]{1,0:T(2,128)}, u32[]{:S(2)}, u32[]{:S(2)}) collective-permute-start(f32[2,1024]{1,0:T(2,128)} %add.28), channel_id=1, source_target_pairs={{0,2},{1,3},{2,0},{3,1},{4,6},{5,7},{6,4},{7,5},{8,10},{9,11},{10,... | collective-permute-start | bytes 24584 | tf_op jit(solution)/shard_map/ppermute | solution.py:1050
  223.8 3.9 %head_outs_kernel.1 = (f32[256,1024]{1,0:T(8,128)}, f32[1024,256]{1,0:T(8,128)}, f32[1024,256]{1,0:T(8,128)}, f32[1024,256]{1,0:T(8,128)}) custom-call(s32[2]{0:T(128)S(1)} %pad_add_fusion.1.refs_0_, bf16[4,1,144,1024]{3,2,1,0:T(8,128)(2,1)} %lambda.47.refs_1_, bf16[4,1,144,1024]{3,2,1,0:T(8,128)(2,1)S(1)} %lambda.48.refs_2_, ...), custom_call_target="tpu_custom_call" | custom-call | flops 299999985664 | tf_op jit(solution)/shard_map/head_outs_kernel/pallas_call | solution.py:341
  227.7 0.7 add.29.refs_1_
  228.5 0.6 fusion.1
  229.1 0.6 copy-done.5
  229.7 3.0 %placed_kernel.3 = (bf16[4,256,1024]{2,1,0:T(8,128)(2,1)}, bf16[4,256,1024]{2,1,0:T(8,128)(2,1)}) custom-call(s32[2]{0:T(128)S(1)} %copy-done.5, bf16[2,128,1024]{2,1,0:T(8,128)(2,1)} %get-tuple-element.123.refs_1_, bf16[2,128,1024]{2,1,0:T(8,128)(2,1)} %lambda.50.refs_1_.refs_2_, ...), custom_call_target="tpu_custom_call", output_to_operand_aliasing={{0}: (5, {}), {1}: (6, {})} | custom-call | flops 199999995904 | tf_op jit(solution)/shard_map/placed_kernel/pallas_call | solution.py:341
  (88 shorter events, 0.6 us)
Async XLA Ops:
  0.7 57.7 %copy-start = (s32[2]{0:T(128)}, s32[2]{0:T(128)S(1)}, u32[]{:S(2)}) copy-start(s32[2]{0:T(128)S(1)} %pad_add_fusion.refs_0_) | copy-start | bytes 28
  6.4 20.7 %all-to-all-start = ((bf16[8,256,256]{2,1,0:T(8,128)(2,1)}), bf16[8,256,256]{2,1,0:T(8,128)(2,1)}, u32[]{:S(2)}, u32[]{:S(2)}) async-start(bf16[8,256,256]{2,1,0:T(8,128)(2,1)} %get-tuple-element.80), calls=%async_computation | async-start | bytes 2097152 | tf_op jit(solution)/shard_map/all_to_all | solution.py:1047
  38.1 20.3 %all-to-all-start.1 = ((bf16[8,256,256]{2,1,0:T(8,128)(2,1)}), bf16[8,256,256]{2,1,0:T(8,128)(2,1)}, u32[]{:S(2)}, u32[]{:S(2)}) async-start(bf16[8,256,256]{2,1,0:T(8,128)(2,1)} %bitcast.9.refs_7_), calls=%async_computation.1 | async-start | bytes 2097152 | tf_op jit(solution)/shard_map/all_to_all | solution.py:1047
  51.9 13.6 %collective-permute-start.1 = (bf16[2,256,256]{2,1,0:T(8,128)(2,1)}, bf16[2,256,256]{2,1,0:T(8,128)(2,1)}, u32[]{:S(2)}, u32[]{:S(2)}) collective-permute-start(bf16[2,256,256]{2,1,0:T(8,128)(2,1)} %lambda.27), channel_id=1, source_target_pairs={{0,8},{4,12},{8,0},{12,4},{16,24},{20,28},{24,16},{28,20},{1,9},{5... | collective-permute-start | bytes 786440 | tf_op jit(solution)/shard_map/ppermute | solution.py:1012
  54.0 11.6 %collective-permute-start.3 = (bf16[2,256,256]{2,1,0:T(8,128)(2,1)}, bf16[2,256,256]{2,1,0:T(8,128)(2,1)}, u32[]{:S(2)}, u32[]{:S(2)}) collective-permute-start(bf16[2,256,256]{2,1,0:T(8,128)(2,1)} %lambda.29), channel_id=1, source_target_pairs={{0,16},{4,20},{8,24},{12,28},{16,0},{20,4},{24,8},{28,12},{1,17},{... | collective-permute-start | bytes 786440 | tf_op jit(solution)/shard_map/ppermute | solution.py:1012
  55.5 13.7 %collective-permute-start.5 = (bf16[2,256,256]{2,1,0:T(8,128)(2,1)}, bf16[2,256,256]{2,1,0:T(8,128)(2,1)}, u32[]{:S(2)}, u32[]{:S(2)}) collective-permute-start(bf16[2,256,256]{2,1,0:T(8,128)(2,1)} %lambda.31), channel_id=1, source_target_pairs={{0,24},{4,28},{8,16},{12,20},{16,8},{20,12},{24,0},{28,4},{1,25},{... | collective-permute-start | bytes 786440 | tf_op jit(solution)/shard_map/ppermute | solution.py:1012
  55.5 16.4 %collective-permute-start = (bf16[2,256,256]{2,1,0:T(8,128)(2,1)}, bf16[2,256,256]{2,1,0:T(8,128)(2,1)}, u32[]{:S(2)}, u32[]{:S(2)}) collective-permute-start(bf16[2,256,256]{2,1,0:T(8,128)(2,1)} %lambda.26.refs_1_), channel_id=1, source_target_pairs={{0,4},{4,0},{8,12},{12,8},{16,20},{20,16},{24,28},{28,24},{1,5},{5... | collective-permute-start | bytes 786440 | tf_op jit(solution)/shard_map/ppermute | solution.py:1012
  65.5 6.4 %collective-permute-start.2 = (bf16[2,256,256]{2,1,0:T(8,128)(2,1)}, bf16[2,256,256]{2,1,0:T(8,128)(2,1)}, u32[]{:S(2)}, u32[]{:S(2)}) collective-permute-start(bf16[2,256,256]{2,1,0:T(8,128)(2,1)} %lambda.28.refs_3_), channel_id=1, source_target_pairs={{0,4},{4,0},{8,12},{12,8},{16,20},{20,16},{24,28},{28,24},{1,5},{5... | collective-permute-start | bytes 786440 | tf_op jit(solution)/shard_map/ppermute | solution.py:1012
  65.6 3.7 %copy-start.10 = (f32[1,1024]{1,0:T(1,128)S(1)}, f32[1,1024]{1,0:T(1,128)}, u32[]{:S(2)}) copy-start(f32[1,1024]{1,0:T(1,128)} %get-tuple-element.81.refs_1_) | copy-start | bytes 12292
  65.6 3.6 %copy-start.11 = (f32[1,1024]{1,0:T(1,128)S(1)}, f32[1,1024]{1,0:T(1,128)}, u32[]{:S(2)}) copy-start(f32[1,1024]{1,0:T(1,128)} %get-tuple-element.104) | copy-start | bytes 12292
  65.6 3.6 %copy-start.12 = (f32[1,1024]{1,0:T(1,128)S(1)}, f32[1,1024]{1,0:T(1,128)}, u32[]{:S(2)}) copy-start(f32[1,1024]{1,0:T(1,128)} %get-tuple-element.82.refs_1_.refs_12_) | copy-start | bytes 12292
  65.6 3.6 %copy-start.13 = (f32[1,1024]{1,0:T(1,128)S(1)}, f32[1,1024]{1,0:T(1,128)}, u32[]{:S(2)}) copy-start(f32[1,1024]{1,0:T(1,128)} %get-tuple-element.105) | copy-start | bytes 12292
  65.6 6.3 %collective-permute-start.4 = (bf16[2,256,256]{2,1,0:T(8,128)(2,1)}, bf16[2,256,256]{2,1,0:T(8,128)(2,1)S(1)}, u32[]{:S(2)}, u32[]{:S(2)}) collective-permute-start(bf16[2,256,256]{2,1,0:T(8,128)(2,1)} %lambda.30.refs_5_), channel_id=1, source_target_pairs={{0,4},{4,0},{8,12},{12,8},{16,20},{20,16},{24,28},{28,24},{1,5},{5... | collective-permute-start | bytes 786440 | tf_op jit(solution)/shard_map/ppermute | solution.py:1012
  69.2 2.7 %collective-permute-start.6 = (bf16[2,256,256]{2,1,0:T(8,128)(2,1)}, bf16[2,256,256]{2,1,0:T(8,128)(2,1)S(1)}, u32[]{:S(2)}, u32[]{:S(2)}) collective-permute-start(bf16[2,256,256]{2,1,0:T(8,128)(2,1)} %lambda.32.refs_7_), channel_id=1, source_target_pairs={{0,4},{4,0},{8,12},{12,8},{16,20},{20,16},{24,28},{28,24},{1,5},{5... | collective-permute-start | bytes 786440 | tf_op jit(solution)/shard_map/ppermute | solution.py:1012
  69.9 27.5 %collective-permute-start.7 = (bf16[2,2,128,1024]{3,2,1,0:T(8,128)(2,1)}, bf16[2,2,128,1024]{3,2,1,0:T(8,128)(2,1)}, u32[]{:S(2)}, u32[]{:S(2)}) collective-permute-start(bf16[2,2,128,1024]{3,2,1,0:T(8,128)(2,1)} %get-tuple-element.93), channel_id=1, source_target_pairs={{0,1},{1,0},{2,3},{3,2},{4,5},{5,4},{6,7},{7,6},{8,9},{9,8},{10,11... | collective-permute-start | bytes 3145736 | tf_op jit(solution)/shard_map/ppermute | solution.py:1050
  83.0 19.7 %all-to-all-start.2 = ((bf16[8,256,256]{2,1,0:T(8,128)(2,1)}), bf16[8,256,256]{2,1,0:T(8,128)(2,1)}, u32[]{:S(2)}, u32[]{:S(2)}) async-start(bf16[8,256,256]{2,1,0:T(8,128)(2,1)} %bitcast.11.refs_5_), calls=%async_computation.2 | async-start | bytes 2097152 | tf_op jit(solution)/shard_map/all_to_all | solution.py:1047
  97.2 14.4 %collective-permute-start.9 = (bf16[2,512,1024]{2,1,0:T(8,128)(2,1)}, bf16[2,512,1024]{2,1,0:T(8,128)(2,1)}, u32[]{:S(2)}, u32[]{:S(2)}) collective-permute-start(bf16[2,512,1024]{2,1,0:T(8,128)(2,1)} %get-tuple-element.106), channel_id=1, source_target_pairs={{0,4},{4,0},{8,12},{12,8},{16,20},{20,16},{24,28},{28,24},{1,5},{5... | collective-permute-start | bytes 6291464 | tf_op jit(solution)/shard_map/ppermute | solution.py:1012
  97.4 5.3 %copy-start.1 = (s32[2]{0:T(128)S(1)}, s32[2]{0:T(128)}, u32[]{:S(2)}) copy-start(s32[2]{0:T(128)} %copy-done) | copy-start | bytes 28
  100.0 26.7 %collective-permute-start.11 = (bf16[2,128,1024]{2,1,0:T(8,128)(2,1)}, bf16[2,128,1024]{2,1,0:T(8,128)(2,1)}, u32[]{:S(2)}, u32[]{:S(2)}) collective-permute-start(bf16[2,128,1024]{2,1,0:T(8,128)(2,1)} %get-tuple-element.110), channel_id=1, source_target_pairs={{0,2},{1,3},{2,0},{3,1},{4,6},{5,7},{6,4},{7,5},{8,10},{9,11},{10,... | collective-permute-start | bytes 1572872 | tf_op jit(solution)/shard_map/ppermute | solution.py:1050
  102.7 8.0 %copy-start.8 = (f32[1,1024]{1,0:T(1,128)S(1)}, f32[1,1024]{1,0:T(1,128)}, u32[]{:S(2)}) copy-start(f32[1,1024]{1,0:T(1,128)} %get-tuple-element.86.refs_1_.refs_9_) | copy-start | bytes 12292
  102.7 8.0 %copy-start.9 = (f32[1,1024]{1,0:T(1,128)S(1)}, f32[1,1024]{1,0:T(1,128)}, u32[]{:S(2)}) copy-start(f32[1,1024]{1,0:T(1,128)} %get-tuple-element.102) | copy-start | bytes 12292
  102.7 8.8 %copy-start.6 = (bf16[1,1024]{1,0:T(2,128)(2,1)S(1)}, bf16[1,1024]{1,0:T(2,128)(2,1)}, u32[]{:S(2)}) copy-start(bf16[1,1024]{1,0:T(2,128)(2,1)} %get-tuple-element.142) | copy-start | bytes 6148
  102.7 8.8 %copy-start.7 = (bf16[1,1024]{1,0:T(2,128)(2,1)S(1)}, bf16[1,1024]{1,0:T(2,128)(2,1)}, u32[]{:S(2)}) copy-start(bf16[1,1024]{1,0:T(2,128)(2,1)} %get-tuple-element.143) | copy-start | bytes 6148
  109.6 52.0 %collective-permute-start.8 = (bf16[2,2,128,1024]{3,2,1,0:T(8,128)(2,1)}, bf16[2,2,128,1024]{3,2,1,0:T(8,128)(2,1)}, u32[]{:S(2)}, u32[]{:S(2)}) collective-permute-start(bf16[2,2,128,1024]{3,2,1,0:T(8,128)(2,1)} %get-tuple-element.99), channel_id=1, source_target_pairs={{0,1},{1,0},{2,3},{3,2},{4,5},{5,4},{6,7},{7,6},{8,9},{9,8},{10,11... | collective-permute-start | bytes 3145736 | tf_op jit(solution)/shard_map/ppermute | solution.py:1050
  116.4 10.3 %copy-start.2 = (s32[2]{0:T(128)S(1)}, s32[2]{0:T(128)}, u32[]{:S(2)}) copy-start(s32[2]{0:T(128)} %copy-done) | copy-start | bytes 28
  123.3 10.2 %collective-permute-start.10 = (bf16[1,768,1024]{2,1,0:T(8,128)(2,1)}, bf16[1,768,1024]{2,1,0:T(8,128)(2,1)}, u32[]{:S(2)}, u32[]{:S(2)}) collective-permute-start(bf16[1,768,1024]{2,1,0:T(8,128)(2,1)} %get-tuple-element.109), channel_id=1, source_target_pairs={{0,4},{4,0},{8,12},{12,8},{16,20},{20,16},{24,28},{28,24},{1,5},{5... | collective-permute-start | bytes 4718600 | tf_op jit(solution)/shard_map/ppermute | solution.py:1012
  130.3 45.7 %collective-permute-start.13 = (bf16[2,128,1024]{2,1,0:T(8,128)(2,1)}, bf16[2,128,1024]{2,1,0:T(8,128)(2,1)}, u32[]{:S(2)}, u32[]{:S(2)}) collective-permute-start(bf16[2,128,1024]{2,1,0:T(8,128)(2,1)} %get-tuple-element.115), channel_id=1, source_target_pairs={{0,2},{1,3},{2,0},{3,1},{4,6},{5,7},{6,4},{7,5},{8,10},{9,11},{10,... | collective-permute-start | bytes 1572872 | tf_op jit(solution)/shard_map/ppermute | solution.py:1050
  130.3 33.9 %collective-permute-start.14 = (bf16[2,128,1024]{2,1,0:T(8,128)(2,1)}, bf16[2,128,1024]{2,1,0:T(8,128)(2,1)}, u32[]{:S(2)}, u32[]{:S(2)}) collective-permute-start(bf16[2,128,1024]{2,1,0:T(8,128)(2,1)} %get-tuple-element.118), channel_id=1, source_target_pairs={{0,8},{4,12},{8,0},{12,4},{16,24},{20,28},{24,16},{28,20},{1,9},{5... | collective-permute-start | bytes 1572872 | tf_op jit(solution)/shard_map/ppermute | solution.py:1012
  132.0 32.7 %collective-permute-start.15 = (bf16[2,128,1024]{2,1,0:T(8,128)(2,1)}, bf16[2,128,1024]{2,1,0:T(8,128)(2,1)}, u32[]{:S(2)}, u32[]{:S(2)}) collective-permute-start(bf16[2,128,1024]{2,1,0:T(8,128)(2,1)} %get-tuple-element.119), channel_id=1, source_target_pairs={{0,16},{4,20},{8,24},{12,28},{16,0},{20,4},{24,8},{28,12},{1,17},{... | collective-permute-start | bytes 1572872 | tf_op jit(solution)/shard_map/ppermute | solution.py:1012
  133.5 31.2 %collective-permute-start.16 = (bf16[2,128,1024]{2,1,0:T(8,128)(2,1)}, bf16[2,128,1024]{2,1,0:T(8,128)(2,1)}, u32[]{:S(2)}, u32[]{:S(2)}) collective-permute-start(bf16[2,128,1024]{2,1,0:T(8,128)(2,1)} %get-tuple-element.120), channel_id=1, source_target_pairs={{0,24},{4,28},{8,16},{12,20},{16,8},{20,12},{24,0},{28,4},{1,25},{... | collective-permute-start | bytes 1572872 | tf_op jit(solution)/shard_map/ppermute | solution.py:1012
  137.5 31.8 %all-to-all-start.3 = ((bf16[4,1,144,1024]{3,2,1,0:T(8,128)(2,1)}), bf16[4,1,144,1024]{3,2,1,0:T(8,128)(2,1)}, u32[]{:S(2)}, u32[]{:S(2)}) async-start(bf16[4,1,144,1024]{3,2,1,0:T(8,128)(2,1)} %get-tuple-element.116), calls=%async_computation.3 | async-start | bytes 2359296 | tf_op jit(solution)/shard_map/all_to_all | solution.py:1082
  164.3 39.8 %collective-permute-start.21 = (bf16[2,128,1024]{2,1,0:T(8,128)(2,1)}, bf16[2,128,1024]{2,1,0:T(8,128)(2,1)}, u32[]{:S(2)}, u32[]{:S(2)}) collective-permute-start(bf16[2,128,1024]{2,1,0:T(8,128)(2,1)} %lambda.40), channel_id=1, source_target_pairs={{0,1},{1,0},{2,3},{3,2},{4,5},{5,4},{6,7},{7,6},{8,9},{9,8},{10,11... | collective-permute-start | bytes 1572872 | tf_op jit(solution)/shard_map/ppermute | solution.py:1050
  164.3 16.2 %collective-permute-start.12 = (bf16[2,128,1024]{2,1,0:T(8,128)(2,1)}, bf16[2,128,1024]{2,1,0:T(8,128)(2,1)}, u32[]{:S(2)}, u32[]{:S(2)}) collective-permute-start(bf16[2,128,1024]{2,1,0:T(8,128)(2,1)} %get-tuple-element.114), channel_id=1, source_target_pairs={{0,2},{1,3},{2,0},{3,1},{4,6},{5,7},{6,4},{7,5},{8,10},{9,11},{10,... | collective-permute-start | bytes 1572872 | tf_op jit(solution)/shard_map/ppermute | solution.py:1050
  171.5 28.2 %all-to-all-start.4 = ((bf16[4,2,128,1024]{3,2,1,0:T(8,128)(2,1)}), bf16[4,2,128,1024]{3,2,1,0:T(8,128)(2,1)}, u32[]{:S(2)}, u32[]{:S(2)}) async-start(bf16[4,2,128,1024]{3,2,1,0:T(8,128)(2,1)} %lambda.37), calls=%async_computation.4 | async-start | bytes 4194304 | tf_op jit(solution)/shard_map/all_to_all | solution.py:1082
  176.0 4.5 %copy-start.3 = (s32[2]{0:T(128)S(1)}, s32[2]{0:T(128)}, u32[]{:S(2)}) copy-start(s32[2]{0:T(128)} %copy-done) | copy-start | bytes 28
  176.0 31.1 %collective-permute-start.22 = (bf16[2,128,1024]{2,1,0:T(8,128)(2,1)}, bf16[2,128,1024]{2,1,0:T(8,128)(2,1)}, u32[]{:S(2)}, u32[]{:S(2)}) collective-permute-start(bf16[2,128,1024]{2,1,0:T(8,128)(2,1)} %lambda.36.refs_6_.refs_3_), channel_id=1, source_target_pairs={{0,1},{1,0},{2,3},{3,2},{4,5},{5,4},{6,7},{7,6},{8,9},{9,8},{10,11... | collective-permute-start | bytes 1572872 | tf_op jit(solution)/shard_map/ppermute | solution.py:1050
  183.9 26.8 %collective-permute-start.20 = (bf16[2,128,1024]{2,1,0:T(8,128)(2,1)}, bf16[2,128,1024]{2,1,0:T(8,128)(2,1)}, u32[]{:S(2)}, u32[]{:S(2)}) collective-permute-start(bf16[2,128,1024]{2,1,0:T(8,128)(2,1)} %get-tuple-element.123.refs_1_), channel_id=1, source_target_pairs={{0,2},{1,3},{2,0},{3,1},{4,6},{5,7},{6,4},{7,5},{8,10},{9,11},{10,... | collective-permute-start | bytes 1572872 | tf_op jit(solution)/shard_map/ppermute | solution.py:1050
  184.3 44.2 %collective-permute-start.17 = (bf16[2,128,1024]{2,1,0:T(8,128)(2,1)}, bf16[2,128,1024]{2,1,0:T(8,128)(2,1)}, u32[]{:S(2)}, u32[]{:S(2)}) collective-permute-start(bf16[2,128,1024]{2,1,0:T(8,128)(2,1)} %get-tuple-element.124.refs_1_), channel_id=1, source_target_pairs={{0,1},{1,0},{2,3},{3,2},{4,5},{5,4},{6,7},{7,6},{8,9},{9,8},{10,11... | collective-permute-start | bytes 1572872 | tf_op jit(solution)/shard_map/ppermute | solution.py:1050
  199.7 11.1 %collective-permute-start.19 = (bf16[4,2,128,1024]{3,2,1,0:T(8,128)(2,1)}, bf16[4,2,128,1024]{3,2,1,0:T(8,128)(2,1)}, u32[]{:S(2)}, u32[]{:S(2)}) collective-permute-start(bf16[4,2,128,1024]{3,2,1,0:T(8,128)(2,1)} %lambda.38.refs_1_), channel_id=1, source_target_pairs={{0,4},{4,0},{8,12},{12,8},{16,20},{20,16},{24,28},{28,24},{1,5},{5... | collective-permute-start | bytes 6291464 | tf_op jit(solution)/shard_map/ppermute | solution.py:1012
  199.7 20.3 %all-to-all-start.5 = ((bf16[4,1,144,1024]{3,2,1,0:T(8,128)(2,1)}), bf16[4,1,144,1024]{3,2,1,0:T(8,128)(2,1)}, u32[]{:S(2)}, u32[]{:S(2)}) async-start(bf16[4,1,144,1024]{3,2,1,0:T(8,128)(2,1)} %lambda.46), calls=%async_computation.5 | async-start | bytes 2359296 | tf_op jit(solution)/shard_map/all_to_all | solution.py:1082
  204.0 16.0 %collective-permute-start.18 = (f32[2,1024]{1,0:T(2,128)}, f32[2,1024]{1,0:T(2,128)}, u32[]{:S(2)}, u32[]{:S(2)}) collective-permute-start(f32[2,1024]{1,0:T(2,128)} %lambda.39), channel_id=1, source_target_pairs={{0,1},{1,0},{2,3},{3,2},{4,5},{5,4},{6,7},{7,6},{8,9},{9,8},{10,11... | collective-permute-start | bytes 24584 | tf_op jit(solution)/shard_map/ppermute | solution.py:1050
  207.1 0.6 copy-start.4
  210.7 18.3 %collective-permute-start.25 = (bf16[2,128,1024]{2,1,0:T(8,128)(2,1)}, bf16[2,128,1024]{2,1,0:T(8,128)(2,1)}, u32[]{:S(2)}, u32[]{:S(2)}) collective-permute-start(bf16[2,128,1024]{2,1,0:T(8,128)(2,1)} %lambda.43.refs_1_.refs_3_), channel_id=1, source_target_pairs={{0,1},{1,0},{2,3},{3,2},{4,5},{5,4},{6,7},{7,6},{8,9},{9,8},{10,11... | collective-permute-start | bytes 1572872 | tf_op jit(solution)/shard_map/ppermute | solution.py:1050
  220.1 3.7 %collective-permute-start.24 = (bf16[4,1,144,1024]{3,2,1,0:T(8,128)(2,1)}, bf16[4,1,144,1024]{3,2,1,0:T(8,128)(2,1)S(1)}, u32[]{:S(2)}, u32[]{:S(2)}) collective-permute-start(bf16[4,1,144,1024]{3,2,1,0:T(8,128)(2,1)} %lambda.47.refs_1_), channel_id=1, source_target_pairs={{0,4},{4,0},{8,12},{12,8},{16,20},{20,16},{24,28},{28,24},{1,5},{5... | collective-permute-start | bytes 3538952 | tf_op jit(solution)/shard_map/ppermute | solution.py:1012
  221.4 6.3 %collective-permute-start.23 = (f32[2,1024]{1,0:T(2,128)}, f32[2,1024]{1,0:T(2,128)}, u32[]{:S(2)}, u32[]{:S(2)}) collective-permute-start(f32[2,1024]{1,0:T(2,128)} %add.28), channel_id=1, source_target_pairs={{0,2},{1,3},{2,0},{3,1},{4,6},{5,7},{6,4},{7,5},{8,10},{9,11},{10,... | collective-permute-start | bytes 24584 | tf_op jit(solution)/shard_map/ppermute | solution.py:1050
  229.1 0.6 copy-start.5

commit v3 on v2

--- a/solution.py
+++ b/solution.py
@@ -1114,11 +1114,11 @@
     near_a = fence(near_a, dense)
     vectors_got = over_line(vectors, 1)
     beside_a = fence(beside_a, near_a)
-    d_tokens, mixed = placed(place, x.shape, 0, (more_a, near_a, far_a, beside_a), None, (beside_a,))
-    far_b = fence(far_b, d_tokens)
+    dense_other = fence(dense_other, beside_a)
+    far_b = fence(far_b, dense_other)
     beside_b = over_line(far_b, 1)
-    dense_other = fence(dense_other, far_b)
-    d_in, d_out = dense_outs(jnp.concatenate([core, jnp.zeros_like(core)]), dense, dense_other, width, (far_b,))
+    d_tokens, mixed = placed(place, x.shape, 0, (more_a, near_a, far_a, beside_a), None, (far_b,))
+    d_in, d_out = dense_outs(jnp.concatenate([core, jnp.zeros_like(core)]), dense, dense_other, width, (d_tokens,))
     vectors = vectors + fence(vectors_got, d_out)
     vectors_got = over_line(vectors, 2)
     head = fence(head, d_out)

time: 234 us -> 234 us (level)
  no operation moved by 1% of the time
where the time goes in v3:
time: 234 us; the launch traced here: 233 us
  Pallas kernels  125 us (53%)
  starting transfers between devices  51.7 us (22%)
  waiting for transfers between devices  47.5 us (20%)
  other arithmetic  4.27 us (2%)
  local copies, waits for them, and re-layouts  3.09 us (1%)
    pallas_call x48, Pallas kernels, call(): pl.pallas_call(body, name=getattr(kernel, 'func', kernel).__name__.strip(...  125 us
    ppermute x12, waiting for transfers between devices, over_line(): return lax.ppermute(v, 'mlp', [(i, i ^ bits) for i in range(4)])  24.4 us
    ppermute x12, starting transfers between devices, over_line(): return lax.ppermute(v, 'mlp', [(i, i ^ bits) for i in range(4)])  16.8 us
    all_to_all x3, waiting for transfers between devices, over_chips(): lax.all_to_all(v, 'seq', 0, 0, axis_index_groups=same_core, tiled=True)  16.7 us
    all_to_all x3, starting transfers between devices, traded(): return lax.all_to_all(v, 'seq', 0, 0, tiled=True)  14 us
    all_to_all x3, starting transfers between devices, over_chips(): lax.all_to_all(v, 'seq', 0, 0, axis_index_groups=same_core, tiled=True)  13 us
    ppermute x14, starting transfers between devices, exchanged(): lax.ppermute(x, 'seq', [(i, i ^ bits) for i in range(lax.axis_size('seq'))])  7.86 us
  transfers between devices with their start and end apart: 32, of which 10 were waited for; matrix products, arithmetic and copies ran while one was open for 3% of the time, Pallas kernels for 45%

profile of v3, /device:TPU:0, one launch (start us, length us, event | category | flops | bytes accessed | tf_op | source)
XLA Modules:
  0.0 232.9 jit_solution(11411164786609539195)
XLA Ops:
  0.7 5.6 %pre_kernel.2 = (bf16[1024,1024]{1,0:T(8,128)(2,1)}, bf16[8,256,256]{2,1,0:T(8,128)(2,1)}) custom-call(s32[2]{0:T(128)S(1)} %pad_add_fusion.refs_0_, bf16[4,256,1024]{2,1,0:T(8,128)(2,1)} %bitcast.26, bf16[4,256,1024]{2,1,0:T(8,128)(2,1)} %bitcast.32, f32[1,1024]{1,0:T(1,128)} %bitcast.46, f32[1,1024]{1,0:T(1,128)} %bitcast.40, bf16[1024,256]{1,0:T(8,128)(2,1)} %refs_6_.7, ...), custom_call_target="tpu_custom_call" | custom-call | flops 299999985664 | tf_op jit(solution)/shard_map/pre_kernel/pallas_call | solution.py:341
  6.4 5.2 %all-to-all-start = ((bf16[8,256,256]{2,1,0:T(8,128)(2,1)}), bf16[8,256,256]{2,1,0:T(8,128)(2,1)}, u32[]{:S(2)}, u32[]{:S(2)}) async-start(bf16[8,256,256]{2,1,0:T(8,128)(2,1)} %get-tuple-element.80), calls=%async_computation | async-start | bytes 2097152 | tf_op jit(solution)/shard_map/all_to_all | solution.py:1047
  11.5 6.3 %pre_kernel.3 = (bf16[1024,1024]{1,0:T(8,128)(2,1)}, bf16[2,256,256]{2,1,0:T(8,128)(2,1)}, bf16[2,256,256]{2,1,0:T(8,128)(2,1)}, bf16[2,256,256]{2,1,0:T(8,128)(2,1)}, bf16[2,256,256]{2,1,0:T(8,128)(2,1)}) custom-call(s32[2]{0:T(128)S(1)} %pad_add_fusion.refs_0_, bf16[4,256,1024]{2,1,0:T(8,128)(2,1)} %bitcast.27, ...), custom_call_target="tpu_custom_call", output_to_operand_aliasing={{0}: (11, {})} | custom-call | flops 299999985664 | tf_op jit(solution)/shard_map/pre_kernel/pallas_call | solution.py:341
  17.8 9.3 %mlp_kernel.2 = (bf16[1024,1024]{1,0:T(8,128)(2,1)}, bf16[1024,1024]{1,0:T(8,128)(2,1)}, bf16[512,1024]{1,0:T(8,128)(2,1)}, bf16[512,1024]{1,0:T(8,128)(2,1)}, f32[1,1024]{1,0:T(1,128)}, /*index=5*/f32[1,1024]{1,0:T(1,128)}) custom-call(bf16[1024,1024]{1,0:T(8,128)(2,1)} %get-tuple-element.77.refs_0_.refs_5_.refs_1_, bf16[1024,1024]{1,0:T(8,128)(2,1)} %bitcast.34, ...), custom_call_target="tpu_custom_call" | custom-call | flops 499999997952 | tf_op jit(solution)/shard_map/mlp_kernel/pallas_call | solution.py:341
  27.1 11.0 %attention_kernel.1 = bf16[1,2048,256]{2,1,0:T(8,128)(2,1)} custom-call(bf16[1,2048,256]{2,1,0:T(8,128)(2,1)} %bitcast.8.refs_0_, f32[1,1024]{1,0:T(1,128)} %get-tuple-element.81.refs_1_), custom_call_target="tpu_custom_call" | custom-call | flops 699999977472 | tf_op jit(solution)/shard_map/attention_kernel/pallas_call | solution.py:341
  38.1 4.4 %all-to-all-start.1 = ((bf16[8,256,256]{2,1,0:T(8,128)(2,1)}), bf16[8,256,256]{2,1,0:T(8,128)(2,1)}, u32[]{:S(2)}, u32[]{:S(2)}) async-start(bf16[8,256,256]{2,1,0:T(8,128)(2,1)} %bitcast.9.refs_7_), calls=%async_computation.1 | async-start | bytes 2097152 | tf_op jit(solution)/shard_map/all_to_all | solution.py:1047
  42.5 9.3 %mlp_kernel.3 = (bf16[1024,1024]{1,0:T(8,128)(2,1)}, bf16[1024,1024]{1,0:T(8,128)(2,1)}, bf16[512,1024]{1,0:T(8,128)(2,1)}, bf16[512,1024]{1,0:T(8,128)(2,1)}, f32[1,1024]{1,0:T(1,128)}, /*index=5*/f32[1,1024]{1,0:T(1,128)}) custom-call(bf16[1024,1024]{1,0:T(8,128)(2,1)} %get-tuple-element.77.refs_0_.refs_5_.refs_1_, ...), custom_call_target="tpu_custom_call", output_to_operand_aliasing={{0}: (5, {}), {1}: (6, {})} | custom-call | flops 499999997952 | tf_op jit(solution)/shard_map/mlp_kernel/pallas_call | solution.py:341
  51.9 2.1 collective-permute-start.1
  54.0 1.5 collective-permute-start.3
  55.5 2.9 %all-to-all-done.1.refs_1_ = bf16[8,256,256]{2,1,0:T(8,128)(2,1)} async-done(((bf16[8,256,256]{2,1,0:T(8,128)(2,1)}), bf16[8,256,256]{2,1,0:T(8,128)(2,1)}, u32[]{:S(2)}, u32[]{:S(2)}) %all-to-all-start.1) | async-done | bytes 1048608 | tf_op jit(solution)/shard_map/all_to_all | solution.py:1047
  58.4 7.0 %post_kernel.2 = (bf16[2,2,128,1024]{3,2,1,0:T(8,128)(2,1)}, bf16[2,2,128,1024]{3,2,1,0:T(8,128)(2,1)}, bf16[1024,1024]{1,0:T(8,128)(2,1)}, f32[1,1024]{1,0:T(1,128)}, f32[1,1024]{1,0:T(1,128)}) custom-call(s32[2]{0:T(128)S(1)} %pad_add_fusion.refs_0_, bf16[8,256,256]{2,1,0:T(8,128)(2,1)} %all-to-all-done.1.refs_1_, bf16[4,256,1024]{2,1,0:T(8,128)(2,1)} %bitcast.28, ...), custom_call_target="tpu_custom_call" | custom-call | flops 399999991808 | tf_op jit(solution)/shard_map/post_kernel/pallas_call | solution.py:341
  65.6 0.5 collective-permute-start.4
  66.2 3.0 %collective-permute-done.5.refs_0_ = bf16[2,256,256]{2,1,0:T(8,128)(2,1)} collective-permute-done((bf16[2,256,256]{2,1,0:T(8,128)(2,1)}, bf16[2,256,256]{2,1,0:T(8,128)(2,1)}, u32[]{:S(2)}, u32[]{:S(2)}) %collective-permute-start.5) | collective-permute-done | bytes 262176 | tf_op jit(solution)/shard_map/ppermute | solution.py:1012
  69.3 0.6 add_convert_fusion
  69.9 2.0 collective-permute-start.7
  71.9 11.1 %gathered_kernel.1 = bf16[1,2048,256]{2,1,0:T(8,128)(2,1)} custom-call(s32[1]{0:T(128)} %bitcast.refs_0_, bf16[2,256,256]{2,1,0:T(8,128)(2,1)} %lambda.26.refs_1_, bf16[2,256,256]{2,1,0:T(8,128)(2,1)} %collective-permute-done.refs_2_, bf16[2,256,256]{2,1,0:T(8,128)(2,1)} %lambda.28.refs_3_, bf16[2,256,256]{2,1,0:T(8,128)(2,1)} %collective-permute-done.2.refs_4_, ...), custom_call_target="tpu_custom_call" | custom-call | flops 699999977472 | tf_op jit(solution)/shard_map/gathered_kernel/pallas_call | solution.py:341
  83.0 4.5 %all-to-all-start.2 = ((bf16[8,256,256]{2,1,0:T(8,128)(2,1)}), bf16[8,256,256]{2,1,0:T(8,128)(2,1)}, u32[]{:S(2)}, u32[]{:S(2)}) async-start(bf16[8,256,256]{2,1,0:T(8,128)(2,1)} %bitcast.11.refs_5_), calls=%async_computation.2 | async-start | bytes 2097152 | tf_op jit(solution)/shard_map/all_to_all | solution.py:1047
  87.5 9.7 %dense_grads_kernel.1 = (bf16[2,512,1024]{2,1,0:T(8,128)(2,1)}, bf16[2,512,1024]{2,1,0:T(8,128)(2,1)}) custom-call(s32[1]{0:T(128)} %bitcast.12.refs_0_, bf16[1024,1024]{1,0:T(8,128)(2,1)} %get-tuple-element.77.refs_0_.refs_5_.refs_1_, bf16[1024,1024]{1,0:T(8,128)(2,1)} %get-tuple-element.94.refs_2_, bf16[1024,1024]{1,0:T(8,128)(2,1)} %get-tuple-element.95.refs_3_, ...), custom_call_target="tpu_custom_call" | custom-call | flops 599999971328 | tf_op jit(solution)/shard_map/dense_grads_kernel/pallas_call | solution.py:341
  97.2 0.2 collective-permute-start.9
  97.4 2.6 %pair_sum_kernel.2 = (bf16[2,128,1024]{2,1,0:T(8,128)(2,1)}, bf16[2,128,1024]{2,1,0:T(8,128)(2,1)}) custom-call(bf16[2,2,128,1024]{3,2,1,0:T(8,128)(2,1)} %get-tuple-element.92.refs_0_, bf16[2,2,128,1024]{3,2,1,0:T(8,128)(2,1)} %collective-permute-done.7.refs_1_, bf16[2,512,1024]{2,1,0:T(8,128)(2,1)} %get-tuple-element.96.refs_2_.refs_1_), custom_call_target="tpu_custom_call" | custom-call | flops 99999997952 | tf_op jit(solution)/shard_map/pair_sum_kernel/pallas_call | solution.py:341
  100.0 2.6 %collective-permute-start.11 = (bf16[2,128,1024]{2,1,0:T(8,128)(2,1)}, bf16[2,128,1024]{2,1,0:T(8,128)(2,1)}, u32[]{:S(2)}, u32[]{:S(2)}) collective-permute-start(bf16[2,128,1024]{2,1,0:T(8,128)(2,1)} %get-tuple-element.110), channel_id=1, source_target_pairs={{0,2},{1,3},{2,0},{3,1},{4,6},{5,7},{6,4},{7,5},{8,10},{9,11},{10,... | collective-permute-start | bytes 1572872 | tf_op jit(solution)/shard_map/ppermute | solution.py:1050
  102.7 6.9 %post_kernel.3 = (bf16[2,2,128,1024]{3,2,1,0:T(8,128)(2,1)}, bf16[2,2,128,1024]{3,2,1,0:T(8,128)(2,1)}, bf16[1024,1024]{1,0:T(8,128)(2,1)}, f32[1,1024]{1,0:T(1,128)}, f32[1,1024]{1,0:T(1,128)}) custom-call(s32[2]{0:T(128)S(1)} %copy-done.1, bf16[8,256,256]{2,1,0:T(8,128)(2,1)} %all-to-all-done.2.refs_1_, ...), custom_call_target="tpu_custom_call", output_to_operand_aliasing={{2}: (12, {})} | custom-call | flops 399999991808 | tf_op jit(solution)/shard_map/post_kernel/pallas_call | solution.py:341
  109.6 1.1 collective-permute-start.8
  110.7 0.7 add_convert_fusion.2
  111.4 0.2 concatenate.8.refs_4_.refs_2_
  111.6 4.7 %parted_kernel.1 = (bf16[2,128,1024]{2,1,0:T(8,128)(2,1)}, bf16[2,128,1024]{2,1,0:T(8,128)(2,1)}, bf16[2,128,1024]{2,1,0:T(8,128)(2,1)}, bf16[2,128,1024]{2,1,0:T(8,128)(2,1)}, f32[8,128]{1,0:T(8,128)}) custom-call(s32[1]{0:T(128)} %bitcast.13.refs_0_, bf16[2,512,1024]{2,1,0:T(8,128)(2,1)} %get-tuple-element.96.refs_2_.refs_1_, ...), custom_call_target="tpu_custom_call" | custom-call | flops 199999995904 | tf_op jit(solution)/shard_map/parted_kernel/pallas_call | solution.py:341
  116.4 6.9 %head_grads_kernel.1 = (bf16[1,768,1024]{2,1,0:T(8,128)(2,1)}, bf16[1,512,1024]{2,1,0:T(8,128)(2,1)}) custom-call(s32[1]{0:T(128)} %bitcast.12.refs_0_, bf16[1024,1024]{1,0:T(8,128)(2,1)} %get-tuple-element.77.refs_0_.refs_5_.refs_1_, bf16[1024,1024]{1,0:T(8,128)(2,1)} %bitcast.37, bf16[1024,1024]{1,0:T(8,128)(2,1)} %get-tuple-element.100.refs_3_, ...), custom_call_target="tpu_custom_call" | custom-call | flops 399999991808 | tf_op jit(solution)/shard_map/head_grads_kernel/pallas_call | solution.py:341
  123.3 3.4 %collective-permute-done.11.refs_4_ = bf16[2,128,1024]{2,1,0:T(8,128)(2,1)} collective-permute-done((bf16[2,128,1024]{2,1,0:T(8,128)(2,1)}, bf16[2,128,1024]{2,1,0:T(8,128)(2,1)}, u32[]{:S(2)}, u32[]{:S(2)}) %collective-permute-start.11) | collective-permute-done | bytes 524320 | tf_op jit(solution)/shard_map/ppermute | solution.py:1050
  126.7 3.6 %own_quarter_kernel.2 = (bf16[2,128,1024]{2,1,0:T(8,128)(2,1)}, bf16[2,128,1024]{2,1,0:T(8,128)(2,1)}, bf16[2,128,1024]{2,1,0:T(8,128)(2,1)}) custom-call(s32[2]{0:T(128)S(1)} %copy-done.2, bf16[4,256,1024]{2,1,0:T(8,128)(2,1)} %bitcast.30, bf16[4,256,1024]{2,1,0:T(8,128)(2,1)} %bitcast.38, bf16[2,128,1024]{2,1,0:T(8,128)(2,1)} %get-tuple-element.97.refs_13_.refs_3_, ...), custom_call_target="tpu_custom_call" | custom-call | flops 199999995904 | tf_op jit(solution)/shard_map/own_quarter_kernel/pallas_call | solution.py:341
  130.3 1.7 collective-permute-start.14
  132.0 1.5 collective-permute-start.15
  133.5 0.3 collective-permute-start.16
  133.8 3.7 %split_kernel.1 = (bf16[4,1,144,1024]{3,2,1,0:T(8,128)(2,1)}, f32[8,128]{1,0:T(8,128)}) custom-call(bf16[1,512,1024]{2,1,0:T(8,128)(2,1)} %get-tuple-element.108.refs_6_.refs_0_, bf16[1,768,1024]{2,1,0:T(8,128)(2,1)} %lambda.33.refs_1_.refs_3_, bf16[16,1024]{1,0:T(8,128)(2,1)S(1)} %concatenate.8.refs_4_.refs_2_, ...), custom_call_target="tpu_custom_call" | custom-call | flops 199999995904 | tf_op jit(solution)/shard_map/split_kernel/pallas_call | solution.py:341
  137.5 4.3 %all-to-all-start.3 = ((bf16[4,1,144,1024]{3,2,1,0:T(8,128)(2,1)}), bf16[4,1,144,1024]{3,2,1,0:T(8,128)(2,1)}, u32[]{:S(2)}, u32[]{:S(2)}) async-start(bf16[4,1,144,1024]{3,2,1,0:T(8,128)(2,1)} %get-tuple-element.116), calls=%async_computation.3 | async-start | bytes 2359296 | tf_op jit(solution)/shard_map/all_to_all | solution.py:1082
  141.8 19.8 %collective-permute-done.8.refs_1_ = bf16[2,2,128,1024]{3,2,1,0:T(8,128)(2,1)} collective-permute-done((bf16[2,2,128,1024]{3,2,1,0:T(8,128)(2,1)}, bf16[2,2,128,1024]{3,2,1,0:T(8,128)(2,1)}, u32[]{:S(2)}, u32[]{:S(2)}) %collective-permute-start.8) | collective-permute-done | bytes 1048608 | tf_op jit(solution)/shard_map/ppermute | solution.py:1050
  161.6 2.6 %pair_sum_kernel.3 = (bf16[2,128,1024]{2,1,0:T(8,128)(2,1)}, bf16[2,128,1024]{2,1,0:T(8,128)(2,1)}) custom-call(bf16[2,2,128,1024]{3,2,1,0:T(8,128)(2,1)} %get-tuple-element.98.refs_0_, bf16[2,2,128,1024]{3,2,1,0:T(8,128)(2,1)} %collective-permute-done.8.refs_1_, f32[8,128]{1,0:T(8,128)} %get-tuple-element.112.refs_2_), custom_call_target="tpu_custom_call" | custom-call | flops 99999997952 | tf_op jit(solution)/shard_map/pair_sum_kernel/pallas_call | solution.py:341
  164.4 0.4 collective-permute-done.15.refs_0_
  164.8 3.9 %joined_kernel.1 = (bf16[4,2,128,1024]{3,2,1,0:T(8,128)(2,1)}, f32[8,128]{1,0:T(8,128)}) custom-call(bf16[2,128,1024]{2,1,0:T(8,128)(2,1)} %get-tuple-element.117.refs_0_, bf16[2,128,1024]{2,1,0:T(8,128)(2,1)} %lambda.34.refs_1_, bf16[2,128,1024]{2,1,0:T(8,128)(2,1)} %lambda.35.refs_2_.refs_4_, bf16[2,128,1024]{2,1,0:T(8,128)(2,1)} %collective-permute-done.16.refs_3_, ...), custom_call_target="tpu_custom_call" | custom-call | flops 199999995904 | tf_op jit(solution)/shard_map/joined_kernel/pallas_call | solution.py:341
  168.7 0.7 all-to-all-done.3.refs_0_
  169.3 2.2 total_kernel.1
  171.5 4.5 %all-to-all-start.4 = ((bf16[4,2,128,1024]{3,2,1,0:T(8,128)(2,1)}), bf16[4,2,128,1024]{3,2,1,0:T(8,128)(2,1)}, u32[]{:S(2)}, u32[]{:S(2)}) async-start(bf16[4,2,128,1024]{3,2,1,0:T(8,128)(2,1)} %lambda.37), calls=%async_computation.4 | async-start | bytes 4194304 | tf_op jit(solution)/shard_map/all_to_all | solution.py:1082
  176.0 3.4 %collective-permute-start.20 = (bf16[2,128,1024]{2,1,0:T(8,128)(2,1)}, bf16[2,128,1024]{2,1,0:T(8,128)(2,1)}, u32[]{:S(2)}, u32[]{:S(2)}) collective-permute-start(bf16[2,128,1024]{2,1,0:T(8,128)(2,1)} %lambda.36.refs_6_.refs_3_), channel_id=1, source_target_pairs={{0,1},{1,0},{2,3},{3,2},{4,5},{5,4},{6,7},{7,6},{8,9},{9,8},{10,11... | collective-permute-start | bytes 1572872 | tf_op jit(solution)/shard_map/ppermute | solution.py:1050
  179.4 1.1 collective-permute-done.12.refs_4_
  180.5 3.5 %own_quarter_kernel.3 = (bf16[2,128,1024]{2,1,0:T(8,128)(2,1)}, bf16[2,128,1024]{2,1,0:T(8,128)(2,1)}) custom-call(s32[2]{0:T(128)S(1)} %copy-done.3, bf16[4,256,1024]{2,1,0:T(8,128)(2,1)} %bitcast.31, bf16[4,256,1024]{2,1,0:T(8,128)(2,1)} %bitcast.39, bf16[2,128,1024]{2,1,0:T(8,128)(2,1)} %get-tuple-element.113.refs_1_.refs_3_, ...), custom_call_target="tpu_custom_call" | custom-call | flops 199999995904 | tf_op jit(solution)/shard_map/own_quarter_kernel/pallas_call | solution.py:341
  183.9 0.3 collective-permute-start.22
  184.3 1.7 collective-permute-start.17
  186.0 0.8 slice_convert_fusion
  186.7 0.6 slice_bitcast_fusion.refs_0_
  187.3 0.6 fusion
  187.9 11.8 %all-to-all-done.4.refs_0_ = bf16[4,2,128,1024]{3,2,1,0:T(8,128)(2,1)} async-done(((bf16[4,2,128,1024]{3,2,1,0:T(8,128)(2,1)}), bf16[4,2,128,1024]{3,2,1,0:T(8,128)(2,1)}, u32[]{:S(2)}, u32[]{:S(2)}) %all-to-all-start.4) | async-done | bytes 2097184 | tf_op jit(solution)/shard_map/all_to_all | solution.py:1082
  199.7 4.3 %all-to-all-start.5 = ((bf16[4,1,144,1024]{3,2,1,0:T(8,128)(2,1)}), bf16[4,1,144,1024]{3,2,1,0:T(8,128)(2,1)}, u32[]{:S(2)}, u32[]{:S(2)}) async-start(bf16[4,1,144,1024]{3,2,1,0:T(8,128)(2,1)} %lambda.46), calls=%async_computation.5 | async-start | bytes 2359296 | tf_op jit(solution)/shard_map/all_to_all | solution.py:1082
  204.0 3.1 %collective-permute-start.18 = (f32[2,1024]{1,0:T(2,128)}, f32[2,1024]{1,0:T(2,128)}, u32[]{:S(2)}, u32[]{:S(2)}) collective-permute-start(f32[2,1024]{1,0:T(2,128)} %lambda.39), channel_id=1, source_target_pairs={{0,1},{1,0},{2,3},{3,2},{4,5},{5,4},{6,7},{7,6},{8,9},{9,8},{10,11... | collective-permute-start | bytes 24584 | tf_op jit(solution)/shard_map/ppermute | solution.py:1050
  207.2 0.2 collective-permute-start.25
  207.3 0.4 copy-done.4
  207.8 3.0 %placed_kernel.2 = (bf16[4,256,1024]{2,1,0:T(8,128)(2,1)}, bf16[4,256,1024]{2,1,0:T(8,128)(2,1)}) custom-call(s32[2]{0:T(128)S(1)} %copy-done.4, bf16[2,128,1024]{2,1,0:T(8,128)(2,1)} %get-tuple-element.111.refs_1_.refs_4_, bf16[2,128,1024]{2,1,0:T(8,128)(2,1)} %lambda.41.refs_1_.refs_2_, bf16[2,128,1024]{2,1,0:T(8,128)(2,1)} %lambda.36.refs_6_.refs_3_, ...), custom_call_target="tpu_custom_call" | custom-call | flops 199999995904 | tf_op jit(solution)/shard_map/placed_kernel/pallas_call | solution.py:341
  210.7 5.1 %dense_outs_kernel.1 = (f32[1024,1024]{1,0:T(8,128)}, f32[1024,1024]{1,0:T(8,128)}) custom-call(s32[2]{0:T(128)S(1)} %pad_add_fusion.1.refs_0_, bf16[4,2,128,1024]{3,2,1,0:T(8,128)(2,1)} %lambda.38.refs_1_, bf16[4,2,128,1024]{3,2,1,0:T(8,128)(2,1)} %lambda.43.refs_1_.refs_2_, bf16[4,256,1024]{2,1,0:T(8,128)(2,1)} %get-tuple-element.128.refs_3_.refs_5_), custom_call_target="tpu_custom_call" | custom-call | flops 399999991808 | tf_op jit(solution)/shard_map/dense_outs_kernel/pallas_call | solution.py:341
  215.9 4.2 %all-to-all-done.5.refs_0_ = bf16[4,1,144,1024]{3,2,1,0:T(8,128)(2,1)} async-done(((bf16[4,1,144,1024]{3,2,1,0:T(8,128)(2,1)}), bf16[4,1,144,1024]{3,2,1,0:T(8,128)(2,1)}, u32[]{:S(2)}, u32[]{:S(2)}) %all-to-all-start.5) | async-done | bytes 1179680 | tf_op jit(solution)/shard_map/all_to_all | solution.py:1082
  220.1 1.3 add.28
  221.4 2.4 %collective-permute-start.23 = (f32[2,1024]{1,0:T(2,128)}, f32[2,1024]{1,0:T(2,128)}, u32[]{:S(2)}, u32[]{:S(2)}) collective-permute-start(f32[2,1024]{1,0:T(2,128)} %add.28), channel_id=1, source_target_pairs={{0,2},{1,3},{2,0},{3,1},{4,6},{5,7},{6,4},{7,5},{8,10},{9,11},{10,... | collective-permute-start | bytes 24584 | tf_op jit(solution)/shard_map/ppermute | solution.py:1050
  223.8 3.9 %head_outs_kernel.1 = (f32[256,1024]{1,0:T(8,128)}, f32[1024,256]{1,0:T(8,128)}, f32[1024,256]{1,0:T(8,128)}, f32[1024,256]{1,0:T(8,128)}) custom-call(s32[2]{0:T(128)S(1)} %pad_add_fusion.1.refs_0_, bf16[4,1,144,1024]{3,2,1,0:T(8,128)(2,1)} %lambda.47.refs_1_, bf16[4,1,144,1024]{3,2,1,0:T(8,128)(2,1)S(1)} %lambda.48.refs_2_, ...), custom_call_target="tpu_custom_call" | custom-call | flops 299999985664 | tf_op jit(solution)/shard_map/head_outs_kernel/pallas_call | solution.py:341
  227.7 0.7 add.29.refs_1_
  228.5 0.6 fusion.1
  229.1 0.6 copy-done.5
  229.7 3.0 %placed_kernel.3 = (bf16[4,256,1024]{2,1,0:T(8,128)(2,1)}, bf16[4,256,1024]{2,1,0:T(8,128)(2,1)}) custom-call(s32[2]{0:T(128)S(1)} %copy-done.5, bf16[2,128,1024]{2,1,0:T(8,128)(2,1)} %get-tuple-element.123.refs_1_, bf16[2,128,1024]{2,1,0:T(8,128)(2,1)} %lambda.50.refs_1_.refs_2_, ...), custom_call_target="tpu_custom_call", output_to_operand_aliasing={{0}: (5, {}), {1}: (6, {})} | custom-call | flops 199999995904 | tf_op jit(solution)/shard_map/placed_kernel/pallas_call | solution.py:341
  (88 shorter events, 0.6 us)
Async XLA Ops:
  0.7 57.7 %copy-start = (s32[2]{0:T(128)}, s32[2]{0:T(128)S(1)}, u32[]{:S(2)}) copy-start(s32[2]{0:T(128)S(1)} %pad_add_fusion.refs_0_) | copy-start | bytes 28
  6.4 20.7 %all-to-all-start = ((bf16[8,256,256]{2,1,0:T(8,128)(2,1)}), bf16[8,256,256]{2,1,0:T(8,128)(2,1)}, u32[]{:S(2)}, u32[]{:S(2)}) async-start(bf16[8,256,256]{2,1,0:T(8,128)(2,1)} %get-tuple-element.80), calls=%async_computation | async-start | bytes 2097152 | tf_op jit(solution)/shard_map/all_to_all | solution.py:1047
  38.1 20.3 %all-to-all-start.1 = ((bf16[8,256,256]{2,1,0:T(8,128)(2,1)}), bf16[8,256,256]{2,1,0:T(8,128)(2,1)}, u32[]{:S(2)}, u32[]{:S(2)}) async-start(bf16[8,256,256]{2,1,0:T(8,128)(2,1)} %bitcast.9.refs_7_), calls=%async_computation.1 | async-start | bytes 2097152 | tf_op jit(solution)/shard_map/all_to_all | solution.py:1047
  51.9 13.6 %collective-permute-start.1 = (bf16[2,256,256]{2,1,0:T(8,128)(2,1)}, bf16[2,256,256]{2,1,0:T(8,128)(2,1)}, u32[]{:S(2)}, u32[]{:S(2)}) collective-permute-start(bf16[2,256,256]{2,1,0:T(8,128)(2,1)} %lambda.27), channel_id=1, source_target_pairs={{0,8},{4,12},{8,0},{12,4},{16,24},{20,28},{24,16},{28,20},{1,9},{5... | collective-permute-start | bytes 786440 | tf_op jit(solution)/shard_map/ppermute | solution.py:1012
  54.0 11.6 %collective-permute-start.3 = (bf16[2,256,256]{2,1,0:T(8,128)(2,1)}, bf16[2,256,256]{2,1,0:T(8,128)(2,1)}, u32[]{:S(2)}, u32[]{:S(2)}) collective-permute-start(bf16[2,256,256]{2,1,0:T(8,128)(2,1)} %lambda.29), channel_id=1, source_target_pairs={{0,16},{4,20},{8,24},{12,28},{16,0},{20,4},{24,8},{28,12},{1,17},{... | collective-permute-start | bytes 786440 | tf_op jit(solution)/shard_map/ppermute | solution.py:1012
  55.5 13.7 %collective-permute-start.5 = (bf16[2,256,256]{2,1,0:T(8,128)(2,1)}, bf16[2,256,256]{2,1,0:T(8,128)(2,1)}, u32[]{:S(2)}, u32[]{:S(2)}) collective-permute-start(bf16[2,256,256]{2,1,0:T(8,128)(2,1)} %lambda.31), channel_id=1, source_target_pairs={{0,24},{4,28},{8,16},{12,20},{16,8},{20,12},{24,0},{28,4},{1,25},{... | collective-permute-start | bytes 786440 | tf_op jit(solution)/shard_map/ppermute | solution.py:1012
  55.5 16.4 %collective-permute-start = (bf16[2,256,256]{2,1,0:T(8,128)(2,1)}, bf16[2,256,256]{2,1,0:T(8,128)(2,1)}, u32[]{:S(2)}, u32[]{:S(2)}) collective-permute-start(bf16[2,256,256]{2,1,0:T(8,128)(2,1)} %lambda.26.refs_1_), channel_id=1, source_target_pairs={{0,4},{4,0},{8,12},{12,8},{16,20},{20,16},{24,28},{28,24},{1,5},{5... | collective-permute-start | bytes 786440 | tf_op jit(solution)/shard_map/ppermute | solution.py:1012
  65.5 6.4 %collective-permute-start.2 = (bf16[2,256,256]{2,1,0:T(8,128)(2,1)}, bf16[2,256,256]{2,1,0:T(8,128)(2,1)}, u32[]{:S(2)}, u32[]{:S(2)}) collective-permute-start(bf16[2,256,256]{2,1,0:T(8,128)(2,1)} %lambda.28.refs_3_), channel_id=1, source_target_pairs={{0,4},{4,0},{8,12},{12,8},{16,20},{20,16},{24,28},{28,24},{1,5},{5... | collective-permute-start | bytes 786440 | tf_op jit(solution)/shard_map/ppermute | solution.py:1012
  65.6 3.7 %copy-start.10 = (f32[1,1024]{1,0:T(1,128)S(1)}, f32[1,1024]{1,0:T(1,128)}, u32[]{:S(2)}) copy-start(f32[1,1024]{1,0:T(1,128)} %get-tuple-element.81.refs_1_) | copy-start | bytes 12292
  65.6 3.6 %copy-start.11 = (f32[1,1024]{1,0:T(1,128)S(1)}, f32[1,1024]{1,0:T(1,128)}, u32[]{:S(2)}) copy-start(f32[1,1024]{1,0:T(1,128)} %get-tuple-element.104) | copy-start | bytes 12292
  65.6 3.6 %copy-start.12 = (f32[1,1024]{1,0:T(1,128)S(1)}, f32[1,1024]{1,0:T(1,128)}, u32[]{:S(2)}) copy-start(f32[1,1024]{1,0:T(1,128)} %get-tuple-element.82.refs_1_.refs_12_) | copy-start | bytes 12292
  65.6 3.6 %copy-start.13 = (f32[1,1024]{1,0:T(1,128)S(1)}, f32[1,1024]{1,0:T(1,128)}, u32[]{:S(2)}) copy-start(f32[1,1024]{1,0:T(1,128)} %get-tuple-element.105) | copy-start | bytes 12292
  65.6 6.3 %collective-permute-start.4 = (bf16[2,256,256]{2,1,0:T(8,128)(2,1)}, bf16[2,256,256]{2,1,0:T(8,128)(2,1)S(1)}, u32[]{:S(2)}, u32[]{:S(2)}) collective-permute-start(bf16[2,256,256]{2,1,0:T(8,128)(2,1)} %lambda.30.refs_5_), channel_id=1, source_target_pairs={{0,4},{4,0},{8,12},{12,8},{16,20},{20,16},{24,28},{28,24},{1,5},{5... | collective-permute-start | bytes 786440 | tf_op jit(solution)/shard_map/ppermute | solution.py:1012
  69.2 2.7 %collective-permute-start.6 = (bf16[2,256,256]{2,1,0:T(8,128)(2,1)}, bf16[2,256,256]{2,1,0:T(8,128)(2,1)S(1)}, u32[]{:S(2)}, u32[]{:S(2)}) collective-permute-start(bf16[2,256,256]{2,1,0:T(8,128)(2,1)} %lambda.32.refs_7_), channel_id=1, source_target_pairs={{0,4},{4,0},{8,12},{12,8},{16,20},{20,16},{24,28},{28,24},{1,5},{5... | collective-permute-start | bytes 786440 | tf_op jit(solution)/shard_map/ppermute | solution.py:1012
  69.9 27.5 %collective-permute-start.7 = (bf16[2,2,128,1024]{3,2,1,0:T(8,128)(2,1)}, bf16[2,2,128,1024]{3,2,1,0:T(8,128)(2,1)}, u32[]{:S(2)}, u32[]{:S(2)}) collective-permute-start(bf16[2,2,128,1024]{3,2,1,0:T(8,128)(2,1)} %get-tuple-element.93), channel_id=1, source_target_pairs={{0,1},{1,0},{2,3},{3,2},{4,5},{5,4},{6,7},{7,6},{8,9},{9,8},{10,11... | collective-permute-start | bytes 3145736 | tf_op jit(solution)/shard_map/ppermute | solution.py:1050
  83.0 19.7 %all-to-all-start.2 = ((bf16[8,256,256]{2,1,0:T(8,128)(2,1)}), bf16[8,256,256]{2,1,0:T(8,128)(2,1)}, u32[]{:S(2)}, u32[]{:S(2)}) async-start(bf16[8,256,256]{2,1,0:T(8,128)(2,1)} %bitcast.11.refs_5_), calls=%async_computation.2 | async-start | bytes 2097152 | tf_op jit(solution)/shard_map/all_to_all | solution.py:1047
  97.2 14.4 %collective-permute-start.9 = (bf16[2,512,1024]{2,1,0:T(8,128)(2,1)}, bf16[2,512,1024]{2,1,0:T(8,128)(2,1)}, u32[]{:S(2)}, u32[]{:S(2)}) collective-permute-start(bf16[2,512,1024]{2,1,0:T(8,128)(2,1)} %get-tuple-element.106), channel_id=1, source_target_pairs={{0,4},{4,0},{8,12},{12,8},{16,20},{20,16},{24,28},{28,24},{1,5},{5... | collective-permute-start | bytes 6291464 | tf_op jit(solution)/shard_map/ppermute | solution.py:1012
  97.4 5.3 %copy-start.1 = (s32[2]{0:T(128)S(1)}, s32[2]{0:T(128)}, u32[]{:S(2)}) copy-start(s32[2]{0:T(128)} %copy-done) | copy-start | bytes 28
  100.0 26.7 %collective-permute-start.11 = (bf16[2,128,1024]{2,1,0:T(8,128)(2,1)}, bf16[2,128,1024]{2,1,0:T(8,128)(2,1)}, u32[]{:S(2)}, u32[]{:S(2)}) collective-permute-start(bf16[2,128,1024]{2,1,0:T(8,128)(2,1)} %get-tuple-element.110), channel_id=1, source_target_pairs={{0,2},{1,3},{2,0},{3,1},{4,6},{5,7},{6,4},{7,5},{8,10},{9,11},{10,... | collective-permute-start | bytes 1572872 | tf_op jit(solution)/shard_map/ppermute | solution.py:1050
  102.7 8.0 %copy-start.8 = (f32[1,1024]{1,0:T(1,128)S(1)}, f32[1,1024]{1,0:T(1,128)}, u32[]{:S(2)}) copy-start(f32[1,1024]{1,0:T(1,128)} %get-tuple-element.86.refs_1_.refs_9_) | copy-start | bytes 12292
  102.7 8.0 %copy-start.9 = (f32[1,1024]{1,0:T(1,128)S(1)}, f32[1,1024]{1,0:T(1,128)}, u32[]{:S(2)}) copy-start(f32[1,1024]{1,0:T(1,128)} %get-tuple-element.102) | copy-start | bytes 12292
  102.7 8.8 %copy-start.6 = (bf16[1,1024]{1,0:T(2,128)(2,1)S(1)}, bf16[1,1024]{1,0:T(2,128)(2,1)}, u32[]{:S(2)}) copy-start(bf16[1,1024]{1,0:T(2,128)(2,1)} %get-tuple-element.142) | copy-start | bytes 6148
  102.7 8.8 %copy-start.7 = (bf16[1,1024]{1,0:T(2,128)(2,1)S(1)}, bf16[1,1024]{1,0:T(2,128)(2,1)}, u32[]{:S(2)}) copy-start(bf16[1,1024]{1,0:T(2,128)(2,1)} %get-tuple-element.143) | copy-start | bytes 6148
  109.6 52.0 %collective-permute-start.8 = (bf16[2,2,128,1024]{3,2,1,0:T(8,128)(2,1)}, bf16[2,2,128,1024]{3,2,1,0:T(8,128)(2,1)}, u32[]{:S(2)}, u32[]{:S(2)}) collective-permute-start(bf16[2,2,128,1024]{3,2,1,0:T(8,128)(2,1)} %get-tuple-element.99), channel_id=1, source_target_pairs={{0,1},{1,0},{2,3},{3,2},{4,5},{5,4},{6,7},{7,6},{8,9},{9,8},{10,11... | collective-permute-start | bytes 3145736 | tf_op jit(solution)/shard_map/ppermute | solution.py:1050
  116.4 10.3 %copy-start.2 = (s32[2]{0:T(128)S(1)}, s32[2]{0:T(128)}, u32[]{:S(2)}) copy-start(s32[2]{0:T(128)} %copy-done) | copy-start | bytes 28
  123.3 10.2 %collective-permute-start.10 = (bf16[1,768,1024]{2,1,0:T(8,128)(2,1)}, bf16[1,768,1024]{2,1,0:T(8,128)(2,1)}, u32[]{:S(2)}, u32[]{:S(2)}) collective-permute-start(bf16[1,768,1024]{2,1,0:T(8,128)(2,1)} %get-tuple-element.109), channel_id=1, source_target_pairs={{0,4},{4,0},{8,12},{12,8},{16,20},{20,16},{24,28},{28,24},{1,5},{5... | collective-permute-start | bytes 4718600 | tf_op jit(solution)/shard_map/ppermute | solution.py:1012
  130.3 45.7 %collective-permute-start.13 = (bf16[2,128,1024]{2,1,0:T(8,128)(2,1)}, bf16[2,128,1024]{2,1,0:T(8,128)(2,1)}, u32[]{:S(2)}, u32[]{:S(2)}) collective-permute-start(bf16[2,128,1024]{2,1,0:T(8,128)(2,1)} %get-tuple-element.115), channel_id=1, source_target_pairs={{0,2},{1,3},{2,0},{3,1},{4,6},{5,7},{6,4},{7,5},{8,10},{9,11},{10,... | collective-permute-start | bytes 1572872 | tf_op jit(solution)/shard_map/ppermute | solution.py:1050
  130.3 33.9 %collective-permute-start.14 = (bf16[2,128,1024]{2,1,0:T(8,128)(2,1)}, bf16[2,128,1024]{2,1,0:T(8,128)(2,1)}, u32[]{:S(2)}, u32[]{:S(2)}) collective-permute-start(bf16[2,128,1024]{2,1,0:T(8,128)(2,1)} %get-tuple-element.118), channel_id=1, source_target_pairs={{0,8},{4,12},{8,0},{12,4},{16,24},{20,28},{24,16},{28,20},{1,9},{5... | collective-permute-start | bytes 1572872 | tf_op jit(solution)/shard_map/ppermute | solution.py:1012
  132.0 32.7 %collective-permute-start.15 = (bf16[2,128,1024]{2,1,0:T(8,128)(2,1)}, bf16[2,128,1024]{2,1,0:T(8,128)(2,1)}, u32[]{:S(2)}, u32[]{:S(2)}) collective-permute-start(bf16[2,128,1024]{2,1,0:T(8,128)(2,1)} %get-tuple-element.119), channel_id=1, source_target_pairs={{0,16},{4,20},{8,24},{12,28},{16,0},{20,4},{24,8},{28,12},{1,17},{... | collective-permute-start | bytes 1572872 | tf_op jit(solution)/shard_map/ppermute | solution.py:1012
  133.5 31.2 %collective-permute-start.16 = (bf16[2,128,1024]{2,1,0:T(8,128)(2,1)}, bf16[2,128,1024]{2,1,0:T(8,128)(2,1)}, u32[]{:S(2)}, u32[]{:S(2)}) collective-permute-start(bf16[2,128,1024]{2,1,0:T(8,128)(2,1)} %get-tuple-element.120), channel_id=1, source_target_pairs={{0,24},{4,28},{8,16},{12,20},{16,8},{20,12},{24,0},{28,4},{1,25},{... | collective-permute-start | bytes 1572872 | tf_op jit(solution)/shard_map/ppermute | solution.py:1012
  137.5 31.8 %all-to-all-start.3 = ((bf16[4,1,144,1024]{3,2,1,0:T(8,128)(2,1)}), bf16[4,1,144,1024]{3,2,1,0:T(8,128)(2,1)}, u32[]{:S(2)}, u32[]{:S(2)}) async-start(bf16[4,1,144,1024]{3,2,1,0:T(8,128)(2,1)} %get-tuple-element.116), calls=%async_computation.3 | async-start | bytes 2359296 | tf_op jit(solution)/shard_map/all_to_all | solution.py:1082
  164.3 39.8 %collective-permute-start.21 = (bf16[2,128,1024]{2,1,0:T(8,128)(2,1)}, bf16[2,128,1024]{2,1,0:T(8,128)(2,1)}, u32[]{:S(2)}, u32[]{:S(2)}) collective-permute-start(bf16[2,128,1024]{2,1,0:T(8,128)(2,1)} %lambda.40), channel_id=1, source_target_pairs={{0,1},{1,0},{2,3},{3,2},{4,5},{5,4},{6,7},{7,6},{8,9},{9,8},{10,11... | collective-permute-start | bytes 1572872 | tf_op jit(solution)/shard_map/ppermute | solution.py:1050
  164.3 16.2 %collective-permute-start.12 = (bf16[2,128,1024]{2,1,0:T(8,128)(2,1)}, bf16[2,128,1024]{2,1,0:T(8,128)(2,1)}, u32[]{:S(2)}, u32[]{:S(2)}) collective-permute-start(bf16[2,128,1024]{2,1,0:T(8,128)(2,1)} %get-tuple-element.114), channel_id=1, source_target_pairs={{0,2},{1,3},{2,0},{3,1},{4,6},{5,7},{6,4},{7,5},{8,10},{9,11},{10,... | collective-permute-start | bytes 1572872 | tf_op jit(solution)/shard_map/ppermute | solution.py:1050
  171.5 28.2 %all-to-all-start.4 = ((bf16[4,2,128,1024]{3,2,1,0:T(8,128)(2,1)}), bf16[4,2,128,1024]{3,2,1,0:T(8,128)(2,1)}, u32[]{:S(2)}, u32[]{:S(2)}) async-start(bf16[4,2,128,1024]{3,2,1,0:T(8,128)(2,1)} %lambda.37), calls=%async_computation.4 | async-start | bytes 4194304 | tf_op jit(solution)/shard_map/all_to_all | solution.py:1082
  176.0 4.5 %copy-start.3 = (s32[2]{0:T(128)S(1)}, s32[2]{0:T(128)}, u32[]{:S(2)}) copy-start(s32[2]{0:T(128)} %copy-done) | copy-start | bytes 28
  176.0 31.1 %collective-permute-start.20 = (bf16[2,128,1024]{2,1,0:T(8,128)(2,1)}, bf16[2,128,1024]{2,1,0:T(8,128)(2,1)}, u32[]{:S(2)}, u32[]{:S(2)}) collective-permute-start(bf16[2,128,1024]{2,1,0:T(8,128)(2,1)} %lambda.36.refs_6_.refs_3_), channel_id=1, source_target_pairs={{0,1},{1,0},{2,3},{3,2},{4,5},{5,4},{6,7},{7,6},{8,9},{9,8},{10,11... | collective-permute-start | bytes 1572872 | tf_op jit(solution)/shard_map/ppermute | solution.py:1050
  183.9 23.2 %collective-permute-start.22 = (bf16[2,128,1024]{2,1,0:T(8,128)(2,1)}, bf16[2,128,1024]{2,1,0:T(8,128)(2,1)}, u32[]{:S(2)}, u32[]{:S(2)}) collective-permute-start(bf16[2,128,1024]{2,1,0:T(8,128)(2,1)} %get-tuple-element.123.refs_1_), channel_id=1, source_target_pairs={{0,2},{1,3},{2,0},{3,1},{4,6},{5,7},{6,4},{7,5},{8,10},{9,11},{10,... | collective-permute-start | bytes 1572872 | tf_op jit(solution)/shard_map/ppermute | solution.py:1050
  184.3 44.2 %collective-permute-start.17 = (bf16[2,128,1024]{2,1,0:T(8,128)(2,1)}, bf16[2,128,1024]{2,1,0:T(8,128)(2,1)}, u32[]{:S(2)}, u32[]{:S(2)}) collective-permute-start(bf16[2,128,1024]{2,1,0:T(8,128)(2,1)} %get-tuple-element.124.refs_1_), channel_id=1, source_target_pairs={{0,1},{1,0},{2,3},{3,2},{4,5},{5,4},{6,7},{7,6},{8,9},{9,8},{10,11... | collective-permute-start | bytes 1572872 | tf_op jit(solution)/shard_map/ppermute | solution.py:1050
  199.7 7.4 %collective-permute-start.19 = (bf16[4,2,128,1024]{3,2,1,0:T(8,128)(2,1)}, bf16[4,2,128,1024]{3,2,1,0:T(8,128)(2,1)}, u32[]{:S(2)}, u32[]{:S(2)}) collective-permute-start(bf16[4,2,128,1024]{3,2,1,0:T(8,128)(2,1)} %lambda.38.refs_1_), channel_id=1, source_target_pairs={{0,4},{4,0},{8,12},{12,8},{16,20},{20,16},{24,28},{28,24},{1,5},{5... | collective-permute-start | bytes 6291464 | tf_op jit(solution)/shard_map/ppermute | solution.py:1012
  199.7 20.3 %all-to-all-start.5 = ((bf16[4,1,144,1024]{3,2,1,0:T(8,128)(2,1)}), bf16[4,1,144,1024]{3,2,1,0:T(8,128)(2,1)}, u32[]{:S(2)}, u32[]{:S(2)}) async-start(bf16[4,1,144,1024]{3,2,1,0:T(8,128)(2,1)} %lambda.46), calls=%async_computation.5 | async-start | bytes 2359296 | tf_op jit(solution)/shard_map/all_to_all | solution.py:1082
  204.0 16.0 %collective-permute-start.18 = (f32[2,1024]{1,0:T(2,128)}, f32[2,1024]{1,0:T(2,128)}, u32[]{:S(2)}, u32[]{:S(2)}) collective-permute-start(f32[2,1024]{1,0:T(2,128)} %lambda.39), channel_id=1, source_target_pairs={{0,1},{1,0},{2,3},{3,2},{4,5},{5,4},{6,7},{7,6},{8,9},{9,8},{10,11... | collective-permute-start | bytes 24584 | tf_op jit(solution)/shard_map/ppermute | solution.py:1050
  207.1 0.6 copy-start.4
  207.2 21.9 %collective-permute-start.25 = (bf16[2,128,1024]{2,1,0:T(8,128)(2,1)}, bf16[2,128,1024]{2,1,0:T(8,128)(2,1)}, u32[]{:S(2)}, u32[]{:S(2)}) collective-permute-start(bf16[2,128,1024]{2,1,0:T(8,128)(2,1)} %lambda.44.refs_5_.refs_3_), channel_id=1, source_target_pairs={{0,1},{1,0},{2,3},{3,2},{4,5},{5,4},{6,7},{7,6},{8,9},{9,8},{10,11... | collective-permute-start | bytes 1572872 | tf_op jit(solution)/shard_map/ppermute | solution.py:1050
  220.1 3.7 %collective-permute-start.24 = (bf16[4,1,144,1024]{3,2,1,0:T(8,128)(2,1)}, bf16[4,1,144,1024]{3,2,1,0:T(8,128)(2,1)S(1)}, u32[]{:S(2)}, u32[]{:S(2)}) collective-permute-start(bf16[4,1,144,1024]{3,2,1,0:T(8,128)(2,1)} %lambda.47.refs_1_), channel_id=1, source_target_pairs={{0,4},{4,0},{8,12},{12,8},{16,20},{20,16},{24,28},{28,24},{1,5},{5... | collective-permute-start | bytes 3538952 | tf_op jit(solution)/shard_map/ppermute | solution.py:1012
  221.4 6.3 %collective-permute-start.23 = (f32[2,1024]{1,0:T(2,128)}, f32[2,1024]{1,0:T(2,128)}, u32[]{:S(2)}, u32[]{:S(2)}) collective-permute-start(f32[2,1024]{1,0:T(2,128)} %add.28), channel_id=1, source_target_pairs={{0,2},{1,3},{2,0},{3,1},{4,6},{5,7},{6,4},{7,5},{8,10},{9,11},{10,... | collective-permute-start | bytes 24584 | tf_op jit(solution)/shard_map/ppermute | solution.py:1050
  229.1 0.6 copy-start.5
